TPU v7x, 32 devices: a whole 2x2x4 slice. The times are simulated.
32 devices in a mesh: dp: 8 (over y, x, core), ctx: 4 (over z).
Axes of the slice: x: 2, y: 2, z: 4, core: 2. Of those that a mesh axis runs over, the one named last changes fastest.
Arguments:
- queries: bfloat16 [4096, 512], P(('dp', 'ctx')), may hold values from -25 to 25
- keys: bfloat16 [4096, 128], P(('dp', 'ctx')), may hold values from -6 to 6
- values: bfloat16 [4096, 128], P(('dp', 'ctx')), may hold values from -6 to 6
- out_grad: bfloat16 [4096, 512], P(('dp', 'ctx')), may hold values from -7 to 7
- doc_lengths: int32 [8, 17], P('dp'), may hold values from 0 to 512, as said below
- source_slot: int32 [4096], P(('dp', 'ctx')), may hold values from 0 to 127, as said below
Outputs:
- attended: bfloat16 [4096, 512], P(('dp', 'ctx'))
- query_grad: bfloat16 [4096, 512], P(('dp', 'ctx'))
- key_grad: bfloat16 [4096, 128], P(('dp', 'ctx'))
- value_grad: bfloat16 [4096, 128], P(('dp', 'ctx'))
Inputs may be any that keep to these rules, and one draw needn't show every extreme that they name: `doc_lengths`: row d lists group d's documents in order: the first covers devices 0 to m - 1 of the group whole (m * 128 tokens, 1 <= m <= 4, with m = 4 in row 0), then 4 documents of positive length for each later device that fill that device exactly, then zeros; every row sums to 512. `source_slot`: on each device the 128 entries are a permutation of 0 to 127.
All inputs are finite; a program needn't handle non-finite values.
Results may differ from a plain program's by a relative error of at most 0.033.
Values may be sent and summed in bfloat16 or wider, within the bound.
No kernel may reach another device: no remote copies, remote signals or barrier semaphores. Data moves between devices by JAX's collectives and lax.ppermute only.
A program may use at most 64 MiB of HBM per device.

v0:
```python
import math

import jax
import jax.numpy as jnp
from jax import lax
from jax.sharding import PartitionSpec as P


def contract(left, right):
    return lax.dot_general(
        left, right, (((1,), (1,)), ((), ())), preferred_element_type=jnp.float32
    )


def contract_rows(left, right):
    return lax.dot_general(
        left, right, (((0,), (0,)), ((), ())), preferred_element_type=jnp.float32
    )


def spread(vector, copies):
    return jnp.broadcast_to(vector[:, None], (vector.shape[0], copies)).reshape(-1)


def visible(query_doc, query_pos, key_doc, key_pos):
    return (query_doc[:, None] == key_doc[None, :]) & (key_pos[None, :] <= query_pos[:, None])


def local(queries, keys, values, out_grad, doc_lengths, source_slot):
    row_count = queries.shape[0]
    head_width = keys.shape[1]
    head_count = queries.shape[1] // head_width
    score_scale = head_width ** (-0.5)
    arrived = (
        lax.all_to_all(queries, "dp", split_axis=0, concat_axis=0, tiled=True),
        lax.all_to_all(keys, "dp", split_axis=0, concat_axis=0, tiled=True),
        lax.all_to_all(values, "dp", split_axis=0, concat_axis=0, tiled=True),
        lax.all_to_all(out_grad, "dp", split_axis=0, concat_axis=0, tiled=True),
    )
    query_local = jnp.take(arrived[0], source_slot, axis=0)
    key_local = jnp.take(arrived[1], source_slot, axis=0)
    value_local = jnp.take(arrived[2], source_slot, axis=0)
    grad_local = jnp.take(arrived[3], source_slot, axis=0)
    key_all, value_all = (
        lax.all_gather(key_local, "ctx", axis=0, tiled=True),
        lax.all_gather(value_local, "ctx", axis=0, tiled=True),
    )
    group_rows = key_all.shape[0]
    first_row = lax.axis_index("ctx") * row_count
    key_pos = jnp.arange(group_rows, dtype=jnp.int32)
    doc_ends = jnp.cumsum(doc_lengths[0], dtype=jnp.int32)
    key_doc = jnp.sum(
        (key_pos[:, None] >= doc_ends[None, :]).astype(jnp.int32), axis=1, dtype=jnp.int32
    )
    own_pos = first_row + jnp.arange(row_count, dtype=jnp.int32)
    own_doc = lax.dynamic_slice_in_dim(key_doc, first_row, row_count)
    query_pos = spread(own_pos, head_count)
    query_doc = spread(own_doc, head_count)
    query_flat = query_local.reshape(row_count * head_count, head_width)
    grad_flat = grad_local.reshape(row_count * head_count, head_width)
    query_count = row_count * head_count
    block_rows = math.gcd(group_rows, 512)
    block_count = group_rows // block_rows

    def key_block(start, size):
        key_part = lax.dynamic_slice_in_dim(key_all, start, size)
        value_part = lax.dynamic_slice_in_dim(value_all, start, size)
        seen_mask = visible(
            query_doc,
            query_pos,
            lax.dynamic_slice_in_dim(key_doc, start, size),
            lax.dynamic_slice_in_dim(key_pos, start, size),
        )
        return (key_part, value_part, seen_mask)

    def max_step(step_index, carry_in):
        key_part, value_part, seen_mask = key_block(step_index * block_rows, block_rows)
        running_max, running_sum = carry_in
        score = jnp.where(seen_mask, contract(query_flat, key_part) * score_scale, -1e30)
        new_max = jnp.maximum(running_max, jnp.max(score, axis=1))
        weights = jnp.where(seen_mask, jnp.exp(score - new_max[:, None]), 0.0)
        return (new_max, running_sum * jnp.exp(running_max - new_max) + jnp.sum(weights, axis=1))

    start_state = (
        jnp.full((query_count,), -1e30, jnp.float32),
        jnp.zeros((query_count,), jnp.float32),
    )
    running_max, running_sum = lax.fori_loop(0, block_count, max_step, start_state)
    log_total = running_max + jnp.log(running_sum)

    def probs_of(query_part, key_part, seen_mask, totals):
        score = contract(query_part, key_part) * score_scale
        return jnp.where(seen_mask, jnp.exp(score - totals[:, None]), 0.0)

    def out_step(step_index, carry_in):
        key_part, value_part, seen_mask = key_block(step_index * block_rows, block_rows)
        probs_low = probs_of(query_flat, key_part, seen_mask, log_total).astype(jnp.bfloat16)
        return carry_in + jnp.dot(probs_low, value_part, preferred_element_type=jnp.float32)

    attended_sum = lax.fori_loop(
        0, block_count, out_step, jnp.zeros((query_count, head_width), jnp.float32)
    )
    attended_low = attended_sum.astype(jnp.bfloat16)
    row_delta = jnp.sum(grad_flat.astype(jnp.float32) * attended_low.astype(jnp.float32), axis=1)

    def query_step(step_index, carry_in):
        key_part, value_part, seen_mask = key_block(step_index * block_rows, block_rows)
        probs = probs_of(query_flat, key_part, seen_mask, log_total)
        prob_grad = contract(grad_flat, value_part)
        score_grad = (probs * (prob_grad - row_delta[:, None])).astype(jnp.bfloat16)
        return carry_in + jnp.dot(score_grad, key_part, preferred_element_type=jnp.float32)

    query_sum = lax.fori_loop(
        0, block_count, query_step, jnp.zeros((query_count, head_width), jnp.float32)
    )
    query_grad_low = (query_sum * score_scale).astype(jnp.bfloat16)
    own_stats = jnp.concatenate(
        [log_total.reshape(row_count, head_count), row_delta.reshape(row_count, head_count)], axis=1
    )
    group_stats = lax.all_gather(own_stats, "ctx", axis=0, tiled=True)
    query_piece = lax.all_gather(query_local, "ctx", axis=0, tiled=True)
    grad_piece = lax.all_gather(grad_local, "ctx", axis=0, tiled=True)
    size = query_piece.shape[0]
    piece_rows = math.gcd(size, 128)

    def piece_step(piece_index, carry_part):
        offset = piece_index * piece_rows
        query_part = lax.dynamic_slice_in_dim(query_piece, offset, piece_rows).reshape(
            piece_rows * head_count, head_width
        )
        grad_part = lax.dynamic_slice_in_dim(grad_piece, offset, piece_rows).reshape(
            piece_rows * head_count, head_width
        )
        stat_rows = lax.dynamic_slice_in_dim(group_stats, offset, piece_rows)
        piece_total = stat_rows[:, :head_count].reshape(-1)
        piece_delta = stat_rows[:, head_count:].reshape(-1)
        positions = offset + jnp.arange(piece_rows, dtype=jnp.int32)
        piece_doc = lax.dynamic_slice_in_dim(key_doc, offset, piece_rows)
        seen_mask = visible(
            spread(piece_doc, head_count), spread(positions, head_count), own_doc, own_pos
        )
        probs = probs_of(query_part, key_local, seen_mask, piece_total)
        value_term = contract_rows(probs.astype(jnp.bfloat16), grad_part)
        prob_grad = contract(grad_part, value_local)
        score_grad = (probs * (prob_grad - piece_delta[:, None])).astype(jnp.bfloat16)
        key_term = contract_rows(score_grad, query_part) * score_scale
        return carry_part + jnp.concatenate([key_term, value_term], axis=1)

    key_value_sum = lax.fori_loop(
        0, size // piece_rows, piece_step, jnp.zeros((row_count, 2 * head_width), jnp.float32)
    )
    key_grad_low = key_value_sum[:, :head_width].astype(jnp.bfloat16)
    value_grad_low = key_value_sum[:, head_width:].astype(jnp.bfloat16)

    def placed(computed):
        return jnp.zeros_like(computed).at[source_slot].set(computed)

    returned = (
        lax.all_to_all(
            placed(attended_low.reshape(row_count, head_count * head_width)),
            "dp",
            split_axis=0,
            concat_axis=0,
            tiled=True,
        ),
        lax.all_to_all(
            placed(query_grad_low.reshape(row_count, head_count * head_width)),
            "dp",
            split_axis=0,
            concat_axis=0,
            tiled=True,
        ),
        lax.all_to_all(placed(key_grad_low), "dp", split_axis=0, concat_axis=0, tiled=True),
        lax.all_to_all(placed(value_grad_low), "dp", split_axis=0, concat_axis=0, tiled=True),
    )
    return (returned[0], returned[1], returned[2], returned[3])


def solution(mesh):
    placed = (
        P(("dp", "ctx"), None),
        P(("dp", "ctx"), None),
        P(("dp", "ctx"), None),
        P(("dp", "ctx"), None),
        P("dp", None),
        P(("dp", "ctx")),
    )
    return jax.shard_map(
        local,
        mesh=mesh,
        in_specs=placed,
        out_specs=(
            P(("dp", "ctx"), None),
            P(("dp", "ctx"), None),
            P(("dp", "ctx"), None),
            P(("dp", "ctx"), None),
        ),
        check_vma=False,
    )
```

profile of v0, /device:TPU:0, one launch (start us, length us, event | category | flops | bytes accessed | tf_op | source)
XLA Modules:
  0.0 154.1 jit_solution(2789744073260891532)
XLA Ops:
  0.6 5.2 %all-to-all-start.1 = ((bf16[8,16,128]{2,1,0:T(8,128)(2,1)}), bf16[8,16,128]{2,1,0:T(8,128)(2,1)S(1)}, u32[]{:S(2)}, u32[]{:S(2)}) async-start(bf16[8,16,128]{2,1,0:T(8,128)(2,1)} %bitcast.49), calls=%async_computation.1 | async-start | bytes 65536 | tf_op jit(solution)/shard_map/all_to_all | solution.py:36
  5.9 0.6 copy-done
  6.6 0.1 reduce
  6.8 3.9 %all-to-all-done.1 = bf16[8,16,128]{2,1,0:T(8,128)(2,1)S(1)} async-done(((bf16[8,16,128]{2,1,0:T(8,128)(2,1)}), bf16[8,16,128]{2,1,0:T(8,128)(2,1)S(1)}, u32[]{:S(2)}, u32[]{:S(2)}) %all-to-all-start.1) | async-done | bytes 32800 | tf_op jit(solution)/shard_map/all_to_all | solution.py:36
  10.7 3.3 %all-to-all-start.2 = ((bf16[8,16,128]{2,1,0:T(8,128)(2,1)}), bf16[8,16,128]{2,1,0:T(8,128)(2,1)S(1)}, u32[]{:S(2)}, u32[]{:S(2)}) async-start(bf16[8,16,128]{2,1,0:T(8,128)(2,1)} %bitcast.5), calls=%async_computation.2 | async-start | bytes 65536 | tf_op jit(solution)/shard_map/all_to_all | solution.py:37
  14.1 4.7 %all-to-all-done.2 = bf16[8,16,128]{2,1,0:T(8,128)(2,1)S(1)} async-done(((bf16[8,16,128]{2,1,0:T(8,128)(2,1)}), bf16[8,16,128]{2,1,0:T(8,128)(2,1)S(1)}, u32[]{:S(2)}, u32[]{:S(2)}) %all-to-all-start.2) | async-done | bytes 32800 | tf_op jit(solution)/shard_map/all_to_all | solution.py:37
  18.8 3.4 %all-to-all-start.4 = ((bf16[8,16,512]{2,1,0:T(8,128)(2,1)}), bf16[8,16,512]{2,1,0:T(8,128)(2,1)S(1)}, u32[]{:S(2)}, u32[]{:S(2)}) async-start(bf16[8,16,512]{2,1,0:T(8,128)(2,1)} %bitcast.9), calls=%async_computation.4 | async-start | bytes 262144 | tf_op jit(solution)/shard_map/all_to_all | solution.py:38
  22.3 0.1 le.102
  22.5 0.1 eq.87
  22.7 0.7 gather_fusion.1
  23.4 0.7 gather_fusion.2
  24.1 3.5 %all-to-all-done.4 = bf16[8,16,512]{2,1,0:T(8,128)(2,1)S(1)} async-done(((bf16[8,16,512]{2,1,0:T(8,128)(2,1)}), bf16[8,16,512]{2,1,0:T(8,128)(2,1)S(1)}, u32[]{:S(2)}, u32[]{:S(2)}) %all-to-all-start.4) | async-done | bytes 131104 | tf_op jit(solution)/shard_map/all_to_all | solution.py:38
  27.6 3.4 %all-to-all-start = ((bf16[8,16,512]{2,1,0:T(8,128)(2,1)}), bf16[8,16,512]{2,1,0:T(8,128)(2,1)S(1)}, u32[]{:S(2)}, u32[]{:S(2)}) async-start(bf16[8,16,512]{2,1,0:T(8,128)(2,1)} %bitcast.1), calls=%async_computation | async-start | bytes 262144 | tf_op jit(solution)/shard_map/all_to_all | solution.py:35
  31.1 13.6 %all_gather.16 = bf16[512,128]{1,0:T(8,128)(2,1)S(1)} all-gather(bf16[128,128]{1,0:T(8,128)(2,1)S(1)} %get-tuple-element.455), channel_id=1, replica_groups=mesh['dp'=8,'ctx'=4] {'ctx'}, dimensions={0}, use_global_device_ids=true | all-gather | bytes 163840 | tf_op jit(solution)/shard_map/all_gather | solution.py:46
  44.7 13.7 %all_gather.15 = bf16[512,128]{1,0:T(8,128)(2,1)S(1)} all-gather(bf16[128,128]{1,0:T(8,128)(2,1)S(1)} %get-tuple-element.452), channel_id=1, replica_groups=mesh['dp'=8,'ctx'=4] {'ctx'}, dimensions={0}, use_global_device_ids=true | all-gather | bytes 163840 | tf_op jit(solution)/shard_map/all_gather | solution.py:45
  58.4 0.8 gather_fusion.3
  59.2 0.8 gather_fusion
  60.3 16.1 %all_gather.17 = bf16[512,512]{1,0:T(8,128)(2,1)S(1)} all-gather(bf16[128,512]{1,0:T(8,128)(2,1)S(1)} %get-tuple-element.371), channel_id=1, replica_groups=mesh['dp'=8,'ctx'=4] {'ctx'}, dimensions={0}, use_global_device_ids=true | all-gather | bytes 655360 | tf_op jit(solution)/shard_map/all_gather | solution.py:121
  76.4 0.4 fusion.25
  76.9 0.4 select_reduce_fusion
  77.3 0.1 reduce_sum.33
  77.5 14.9 %all_gather.19 = bf16[512,512]{1,0:T(8,128)(2,1)S(1)} all-gather(bf16[128,512]{1,0:T(8,128)(2,1)S(1)} %get-tuple-element.370), channel_id=1, replica_groups=mesh['dp'=8,'ctx'=4] {'ctx'}, dimensions={0}, use_global_device_ids=true | all-gather | bytes 655360 | tf_op jit(solution)/shard_map/all_gather | solution.py:122
  92.4 0.1 copy.36
  92.6 0.4 multiply_reduce_fusion
  93.4 13.3 %all_gather.18 = f32[512,8]{0,1:T(8,128)S(1)} all-gather(f32[128,8]{0,1:T(8,128)S(1)} %pad_maximum_fusion), channel_id=1, replica_groups=mesh['dp'=8,'ctx'=4] {'ctx'}, dimensions={0}, use_global_device_ids=true | all-gather | bytes 20480 | tf_op jit(solution)/shard_map/all_gather | solution.py:120
  106.7 8.7 %while.9 = (s32[]{:T(128)}, f32[128,256]{0,1:T(8,128)S(1)}, s32[512]{0:T(512)S(1)}, s32[128]{0:T(128)S(1)}, bf16[512,512]{1,0:T(8,128)(2,1)S(1)}, /*index=5*/bf1...) while((s32[]{:T(128)}, f32[128,256]{0,1:T(8,128)S(1)}, ...), condition=%wide.region_8.11_spmd.clone, body=%wide.region_7.10_spmd.clone.sunk | while | flops 67879168 | bytes 3006681 | solution.py:149
  107.2 0.1 le.176
  107.5 0.1 eq.144
  107.6 0.3 fusion.71
  107.9 0.2 fusion.72
  108.4 0.4 fusion.73
  109.4 0.1 le.176
  109.7 0.1 eq.144
  109.8 0.3 fusion.71
  110.1 0.2 fusion.72
  110.6 0.4 fusion.73
  111.6 0.1 le.176
  111.9 0.1 eq.144
  112.0 0.3 fusion.71
  112.3 0.2 fusion.72
  112.7 0.4 fusion.73
  113.8 0.1 le.176
  114.0 0.1 eq.144
  114.2 0.3 fusion.71
  114.5 0.2 fusion.72
  114.9 0.4 fusion.73
  115.5 1.5 scatter_custom_fusion.2
  117.0 4.0 %all-to-all-start.6 = ((bf16[8,16,128]{2,1,0:T(8,128)(2,1)}), bf16[8,16,128]{2,1,0:T(8,128)(2,1)S(1)}, u32[]{:S(2)}, u32[]{:S(2)}) async-start(bf16[8,16,128]{2,1,0:T(8,128)(2,1)} %bitcast.13), calls=%async_computation.6 | async-start | bytes 65536 | tf_op jit(solution)/shard_map/all_to_all | solution.py:173
  121.1 1.5 scatter_custom_fusion.3
  122.5 3.3 %all-to-all-done.6 = bf16[8,16,128]{2,1,0:T(8,128)(2,1)S(1)} async-done(((bf16[8,16,128]{2,1,0:T(8,128)(2,1)}), bf16[8,16,128]{2,1,0:T(8,128)(2,1)S(1)}, u32[]{:S(2)}, u32[]{:S(2)}) %all-to-all-start.6) | async-done | bytes 32800 | tf_op jit(solution)/shard_map/all_to_all | solution.py:173
  125.8 3.3 %all-to-all-start.7 = ((bf16[8,16,128]{2,1,0:T(8,128)(2,1)}), bf16[8,16,128]{2,1,0:T(8,128)(2,1)S(1)}, u32[]{:S(2)}, u32[]{:S(2)}) async-start(bf16[8,16,128]{2,1,0:T(8,128)(2,1)} %bitcast.15), calls=%async_computation.7 | async-start | bytes 65536 | tf_op jit(solution)/shard_map/all_to_all | solution.py:174
  129.1 0.1 copy.35
  129.4 1.7 %scatter_custom_fusion = bf16[128,512]{1,0:T(8,128)(2,1)} fusion(s32[128]{0:T(128)S(1)} %compare_select_fusion, bf16[128,512]{1,0:T(8,128)(2,1)S(1)} %reshape.180, bf16[]{:T(256)} %constant.118.clone.1), kind=kCustom, calls=%fused_computation.52 | custom fusion | bytes 131074 | tf_op jit(solution)/shard_map/scatter | solution.py:156
  131.0 2.9 %all-to-all-done.7 = bf16[8,16,128]{2,1,0:T(8,128)(2,1)S(1)} async-done(((bf16[8,16,128]{2,1,0:T(8,128)(2,1)}), bf16[8,16,128]{2,1,0:T(8,128)(2,1)S(1)}, u32[]{:S(2)}, u32[]{:S(2)}) %all-to-all-start.7) | async-done | bytes 32800 | tf_op jit(solution)/shard_map/all_to_all | solution.py:174
  133.9 3.4 %all-to-all-start.3 = ((bf16[8,16,512]{2,1,0:T(8,128)(2,1)}), bf16[8,16,512]{2,1,0:T(8,128)(2,1)S(1)}, u32[]{:S(2)}, u32[]{:S(2)}) async-start(bf16[8,16,512]{2,1,0:T(8,128)(2,1)} %bitcast.7), calls=%async_computation.3 | async-start | bytes 262144 | tf_op jit(solution)/shard_map/all_to_all | solution.py:159
  137.3 0.8 fusion.16
  138.2 1.7 %scatter_custom_fusion.1 = bf16[128,512]{1,0:T(8,128)(2,1)} fusion(s32[128]{0:T(128)S(1)} %compare_select_fusion, bf16[128,512]{1,0:T(8,128)(2,1)S(1)} %reshape.188, bf16[]{:T(256)} %constant.118.clone.1), kind=kCustom, calls=%fused_computation.50 | custom fusion | bytes 131074 | tf_op jit(solution)/shard_map/scatter | solution.py:156
  139.8 2.9 %all-to-all-done.3 = bf16[8,16,512]{2,1,0:T(8,128)(2,1)S(1)} async-done(((bf16[8,16,512]{2,1,0:T(8,128)(2,1)}), bf16[8,16,512]{2,1,0:T(8,128)(2,1)S(1)}, u32[]{:S(2)}, u32[]{:S(2)}) %all-to-all-start.3) | async-done | bytes 131104 | tf_op jit(solution)/shard_map/all_to_all | solution.py:159
  142.8 3.4 %all-to-all-start.5 = ((bf16[8,16,512]{2,1,0:T(8,128)(2,1)}), bf16[8,16,512]{2,1,0:T(8,128)(2,1)S(1)}, u32[]{:S(2)}, u32[]{:S(2)}) async-start(bf16[8,16,512]{2,1,0:T(8,128)(2,1)} %bitcast.11), calls=%async_computation.5 | async-start | bytes 262144 | tf_op jit(solution)/shard_map/all_to_all | solution.py:166
  146.1 5.5 %all-to-all-done.5 = bf16[8,16,512]{2,1,0:T(8,128)(2,1)S(1)} async-done(((bf16[8,16,512]{2,1,0:T(8,128)(2,1)}), bf16[8,16,512]{2,1,0:T(8,128)(2,1)S(1)}, u32[]{:S(2)}, u32[]{:S(2)}) %all-to-all-start.5) | async-done | bytes 131104 | tf_op jit(solution)/shard_map/all_to_all | solution.py:166
  151.6 0.7 copy.63
  152.3 0.7 copy.64
  152.9 0.6 copy.65
  153.5 0.6 copy.66
  (94 shorter events, 5.4 us)
Async XLA Ops:
  0.6 5.2 %copy-start.1 = (s32[128]{0:T(128)S(1)}, s32[128]{0:T(128)}, u32[]{:S(2)}) copy-start(s32[128]{0:T(128)} %param.17) | copy-start | bytes 1540
  0.6 10.0 %all-to-all-start.1 = ((bf16[8,16,128]{2,1,0:T(8,128)(2,1)}), bf16[8,16,128]{2,1,0:T(8,128)(2,1)S(1)}, u32[]{:S(2)}, u32[]{:S(2)}) async-start(bf16[8,16,128]{2,1,0:T(8,128)(2,1)} %bitcast.49), calls=%async_computation.1 | async-start | bytes 65536 | tf_op jit(solution)/shard_map/all_to_all | solution.py:36
  5.9 0.7 copy-start
  10.7 8.1 %all-to-all-start.2 = ((bf16[8,16,128]{2,1,0:T(8,128)(2,1)}), bf16[8,16,128]{2,1,0:T(8,128)(2,1)S(1)}, u32[]{:S(2)}, u32[]{:S(2)}) async-start(bf16[8,16,128]{2,1,0:T(8,128)(2,1)} %bitcast.5), calls=%async_computation.2 | async-start | bytes 65536 | tf_op jit(solution)/shard_map/all_to_all | solution.py:37
  18.8 8.8 %all-to-all-start.4 = ((bf16[8,16,512]{2,1,0:T(8,128)(2,1)}), bf16[8,16,512]{2,1,0:T(8,128)(2,1)S(1)}, u32[]{:S(2)}, u32[]{:S(2)}) async-start(bf16[8,16,512]{2,1,0:T(8,128)(2,1)} %bitcast.9), calls=%async_computation.4 | async-start | bytes 262144 | tf_op jit(solution)/shard_map/all_to_all | solution.py:38
  27.6 31.6 %all-to-all-start = ((bf16[8,16,512]{2,1,0:T(8,128)(2,1)}), bf16[8,16,512]{2,1,0:T(8,128)(2,1)S(1)}, u32[]{:S(2)}, u32[]{:S(2)}) async-start(bf16[8,16,512]{2,1,0:T(8,128)(2,1)} %bitcast.1), calls=%async_computation | async-start | bytes 262144 | tf_op jit(solution)/shard_map/all_to_all | solution.py:35
  117.0 8.8 %all-to-all-start.6 = ((bf16[8,16,128]{2,1,0:T(8,128)(2,1)}), bf16[8,16,128]{2,1,0:T(8,128)(2,1)S(1)}, u32[]{:S(2)}, u32[]{:S(2)}) async-start(bf16[8,16,128]{2,1,0:T(8,128)(2,1)} %bitcast.13), calls=%async_computation.6 | async-start | bytes 65536 | tf_op jit(solution)/shard_map/all_to_all | solution.py:173
  125.8 8.1 %all-to-all-start.7 = ((bf16[8,16,128]{2,1,0:T(8,128)(2,1)}), bf16[8,16,128]{2,1,0:T(8,128)(2,1)S(1)}, u32[]{:S(2)}, u32[]{:S(2)}) async-start(bf16[8,16,128]{2,1,0:T(8,128)(2,1)} %bitcast.15), calls=%async_computation.7 | async-start | bytes 65536 | tf_op jit(solution)/shard_map/all_to_all | solution.py:174
  133.9 8.8 %all-to-all-start.3 = ((bf16[8,16,512]{2,1,0:T(8,128)(2,1)}), bf16[8,16,512]{2,1,0:T(8,128)(2,1)S(1)}, u32[]{:S(2)}, u32[]{:S(2)}) async-start(bf16[8,16,512]{2,1,0:T(8,128)(2,1)} %bitcast.7), calls=%async_computation.3 | async-start | bytes 262144 | tf_op jit(solution)/shard_map/all_to_all | solution.py:159
  142.8 8.8 %all-to-all-start.5 = ((bf16[8,16,512]{2,1,0:T(8,128)(2,1)}), bf16[8,16,512]{2,1,0:T(8,128)(2,1)S(1)}, u32[]{:S(2)}, u32[]{:S(2)}) async-start(bf16[8,16,512]{2,1,0:T(8,128)(2,1)} %bitcast.11), calls=%async_computation.5 | async-start | bytes 262144 | tf_op jit(solution)/shard_map/all_to_all | solution.py:166
where the time goes:
time: 155 us; the launch traced here: 154 us
  blocking collectives  71.6 us (46%)
  starting transfers between devices  29.3 us (19%)
  waiting for transfers between devices  26.7 us (17%)
  local copies, waits for them, and re-layouts  18.9 us (12%)
  matrix products  5.21 us (3%)
    all_gather x1, blocking collectives, local(): query_piece = lax.all_gather(query_local, 'ctx', axis=0, tiled=True)  16.1 us
    all_gather x1, blocking collectives, local(): grad_piece = lax.all_gather(grad_local, 'ctx', axis=0, tiled=True)  14.9 us
    all_gather x1, blocking collectives, local(): lax.all_gather(key_local, 'ctx', axis=0, tiled=True)  13.7 us
    all_gather x1, blocking collectives, local(): lax.all_gather(value_local, 'ctx', axis=0, tiled=True)  13.6 us
    all_gather x1, blocking collectives, local(): group_stats = lax.all_gather(own_stats, 'ctx', axis=0, tiled=True)  13.3 us
    scatter x4, local copies, waits for them, and re-layouts, placed(): return jnp.zeros_like(computed).at[source_slot].set(computed)  6.23 us
    all_to_all x1, waiting for transfers between devices, local(): lax.all_to_all(placed(query_grad_low.reshape(row_count, head_count * head...  5.46 us
    all_to_all x1, starting transfers between devices, local(): lax.all_to_all(keys, 'dp', split_axis=0, concat_axis=0, tiled=True)  5.18 us
  transfers between devices with their start and end apart: 8, of which 7 were waited for; matrix products, arithmetic and copies ran while one was open for 6% of the time, Pallas kernels for 0%

commit v1 on v0

v1 whole, which is shorter than its diff:
```python
import functools

import jax
import jax.numpy as jnp
from jax import lax
from jax.experimental import pallas as pl
from jax.experimental.pallas import tpu as pltpu
from jax.sharding import PartitionSpec as P

HIDDEN = -1e30
VMEM = pl.BlockSpec(memory_space=pltpu.VMEM)
SMEM = pl.BlockSpec(memory_space=pltpu.SMEM)


def contract(left, right):
    return lax.dot_general(
        left, right, (((1,), (1,)), ((), ())), preferred_element_type=jnp.float32
    )


def multiply(left, right):
    return jnp.dot(left, right, preferred_element_type=jnp.float32)


def params(mib):
    return pltpu.CompilerParams(vmem_limit_bytes=mib * 1024 * 1024)


def slots_of(rows, peer, own, swapped):
    row = lax.broadcasted_iota(jnp.int32, (rows, rows), 1)
    if not swapped:
        return row
    return lax.bitwise_xor(row // peer, own) * peer + row % peer


def mask_kernel(peer, swapped, place, lengths, slot_row, bias):
    rows = slot_row.shape[1]
    own, first = place[0], place[1] * rows
    slot = jnp.broadcast_to(slot_row[...], (rows, rows))
    along = lax.broadcasted_iota(jnp.int32, (rows, rows), 1)
    down = lax.broadcasted_iota(jnp.int32, (rows, rows), 0)
    key_pos = jnp.sum(jnp.where(slot == down, along, 0), axis=1, keepdims=True)
    slot_down = slot.astype(jnp.float32).T.astype(jnp.int32)
    wanted = slots_of(rows, peer, own, swapped)
    query_pos = jnp.sum(jnp.where(slot_down == wanted, down, 0), axis=0, keepdims=True)

    def later(k, carry):
        end, start = carry
        end = end + lengths[0, k]
        return end, jnp.where(query_pos + first >= end, end, start)

    _, doc_start = lax.fori_loop(
        0, lengths.shape[1], later, (jnp.int32(0), jnp.zeros((1, rows), jnp.int32))
    )
    seen = (key_pos <= query_pos) & (key_pos + first >= doc_start)
    bias[...] = jnp.where(seen, 0.0, HIDDEN)


def pack_kernel(peer, place, queries, out_grad, *pieces):
    own = place[0]
    width = queries.shape[1]
    for index, piece in enumerate(pieces):
        start = pl.multiple_of(lax.bitwise_xor(own, index) * peer, peer)
        piece[:, :width] = queries[pl.ds(start, peer), :]
        piece[:, width:] = out_grad[pl.ds(start, peer), :]


def core_kernel(heads, place, lengths, bias, kv, *refs):
    count = (len(refs) - 7) // 2
    pieces, returned = refs[:count], refs[count : 2 * count]
    kv_grad, key_all, value_all, query_flat, grad_flat, probs_all, score_all = refs[2 * count :]
    peers, planes, peer, both = kv.shape
    width = both // 2
    rows = peers * peer
    wide = heads * width
    scale = width**-0.5
    plane = place[1]
    for j in range(planes):
        block = kv[:, j].reshape(rows, both)
        key_all[j * rows : (j + 1) * rows, :] = block[:, :width]
        value_all[j * rows : (j + 1) * rows, :] = block[:, width:]
    size = pieces[0].shape[0]
    for index, piece in enumerate(pieces):
        for h in range(heads):
            at = h * rows + index * size
            query_flat[at : at + size, :] = piece[:, h * width : (h + 1) * width]
            grad_flat[at : at + size, :] = piece[:, wide + h * width : wide + (h + 1) * width]
    joined = plane * rows < lengths[0, 0]
    own_bias = bias[...]
    added = []
    for j in range(planes):
        other = jnp.where(joined & (plane > j), 0.0, HIDDEN).astype(jnp.float32)
        added.append(jnp.where(plane == j, own_bias, other))
    added = jnp.concatenate(added, axis=0)
    for h in range(heads):
        own = slice(h * rows, (h + 1) * rows)
        score = contract(key_all[...], query_flat[own, :]) * scale + added
        weight = jnp.exp(score - jnp.max(score, axis=0, keepdims=True))
        probs = weight * (1.0 / jnp.sum(weight, axis=0, keepdims=True))
        prob_grad = contract(value_all[...], grad_flat[own, :])
        delta = jnp.sum(probs * prob_grad, axis=0, keepdims=True)
        probs_all[:, own] = probs.astype(jnp.bfloat16)
        score_all[:, own] = (probs * (prob_grad - delta)).astype(jnp.bfloat16)
    key_grad = (multiply(score_all[...], query_flat[...]) * scale).astype(jnp.bfloat16)
    value_grad = multiply(probs_all[...], grad_flat[...]).astype(jnp.bfloat16)
    for j in range(planes):
        own = slice(j * rows, (j + 1) * rows)
        kv_grad[:, j, :, :width] = key_grad[own].reshape(peers, peer, width)
        kv_grad[:, j, :, width:] = value_grad[own].reshape(peers, peer, width)
    attended = multiply(value_all[...].T, probs_all[...])
    query_grad = multiply(key_all[...].T, score_all[...]) * scale
    for h in range(heads):
        own = slice(h * rows, (h + 1) * rows)
        out = attended[:, own].T.astype(jnp.bfloat16)
        grad = query_grad[:, own].T.astype(jnp.bfloat16)
        for index, piece in enumerate(returned):
            part = slice(index * size, (index + 1) * size)
            piece[:, h * width : (h + 1) * width] = out[part]
            piece[:, wide + h * width : wide + (h + 1) * width] = grad[part]


def unpack_kernel(place, kv, *refs):
    pieces = refs[:-4]
    attended, query_grad, key_grad, value_grad = refs[-4:]
    own = place[0]
    peers, planes, peer, both = kv.shape
    width, wide = both // 2, attended.shape[1]
    size = pieces[0].shape[0]
    for index, piece in enumerate(pieces):
        start = pl.multiple_of(lax.bitwise_xor(own, index) * size, size)
        attended[pl.ds(start, size), :] = piece[:, :wide]
        query_grad[pl.ds(start, size), :] = piece[:, wide:]
    total = kv[:, 0].astype(jnp.float32)
    for j in range(1, planes):
        total = total + kv[:, j].astype(jnp.float32)
    total = total.reshape(peers * peer, both).astype(jnp.bfloat16)
    key_grad[...] = total[:, :width]
    value_grad[...] = total[:, width:]


def local(queries, keys, values, out_grad, doc_lengths, source_slot):
    rows, wide = queries.shape
    width = keys.shape[1]
    heads = wide // width
    peers, planes = lax.axis_size("dp"), lax.axis_size("ctx")
    peer = rows // peers
    swapped = peers == 8 and peer % 16 == 0
    place = jnp.stack([lax.axis_index("dp"), lax.axis_index("ctx")]).astype(jnp.int32)
    low = functools.partial(jax.ShapeDtypeStruct, dtype=jnp.bfloat16)

    kv = jnp.concatenate([keys, values], axis=1).reshape(peers, 1, peer, 2 * width)
    kv = jnp.broadcast_to(kv, (peers, planes, peer, 2 * width))

    def everywhere(x):
        x = x.reshape(peers * planes, peer, 2 * width)
        x = lax.all_to_all(x, ("dp", "ctx"), split_axis=0, concat_axis=0, tiled=True)
        return x.reshape(peers, planes, peer, 2 * width)

    def in_plane(pieces):
        if not swapped:
            return [lax.all_to_all(pieces[0], "dp", split_axis=0, concat_axis=0, tiled=True)]
        return [pieces[0]] + [
            lax.ppermute(pieces[s], "dp", [(i, i ^ s) for i in range(peers)])
            for s in range(1, peers)
        ]

    kv = everywhere(kv)
    if swapped:
        pieces = pl.pallas_call(
            functools.partial(pack_kernel, peer),
            out_shape=[low((peer, 2 * wide))] * peers,
            in_specs=[SMEM, VMEM, VMEM],
            out_specs=[VMEM] * peers,
            compiler_params=params(4),
            name="pack",
        )(place, queries, out_grad)
    else:
        pieces = [jnp.concatenate([queries, out_grad], axis=1)]
    pieces = in_plane(pieces)
    bias = pl.pallas_call(
        functools.partial(mask_kernel, peer, swapped),
        out_shape=jax.ShapeDtypeStruct((rows, rows), jnp.float32),
        in_specs=[SMEM, SMEM, VMEM],
        out_specs=VMEM,
        compiler_params=params(4),
        name="mask",
    )(place, doc_lengths, source_slot.reshape(1, rows))
    fine = peer % 16 == 0
    if not fine:
        kv = kv.transpose(1, 0, 2, 3).reshape(1, planes, rows, 2 * width)
    count = rows * planes
    results = pl.pallas_call(
        functools.partial(core_kernel, heads),
        out_shape=[low(p.shape) for p in pieces] + [low(kv.shape)],
        in_specs=[SMEM, SMEM] + [VMEM] * (2 + len(pieces)),
        out_specs=[VMEM] * (len(pieces) + 1),
        scratch_shapes=[
            pltpu.VMEM((count, width), jnp.bfloat16),
            pltpu.VMEM((count, width), jnp.bfloat16),
            pltpu.VMEM((rows * heads, width), jnp.bfloat16),
            pltpu.VMEM((rows * heads, width), jnp.bfloat16),
            pltpu.VMEM((count, rows * heads), jnp.bfloat16),
            pltpu.VMEM((count, rows * heads), jnp.bfloat16),
        ],
        compiler_params=params(16 if planes <= 4 else 48),
        name="core",
    )(place, doc_lengths, bias, kv, *pieces)
    pieces, kv = list(results[:-1]), results[-1]
    if not fine:
        kv = kv.reshape(planes, peers, peer, 2 * width).transpose(1, 0, 2, 3)
    kv = everywhere(kv)
    if not fine:
        kv = kv.transpose(1, 0, 2, 3).reshape(1, planes, rows, 2 * width)
    pieces = in_plane(pieces)
    return tuple(
        pl.pallas_call(
            unpack_kernel,
            out_shape=[low((rows, wide))] * 2 + [low((rows, width))] * 2,
            in_specs=[SMEM, VMEM] + [VMEM] * len(pieces),
            out_specs=[VMEM] * 4,
            compiler_params=params(8),
            name="unpack",
        )(place if swapped else place * 0, kv, *pieces)
    )


def solution(mesh):
    rows = P(("dp", "ctx"), None)
    return jax.shard_map(
        local,
        mesh=mesh,
        in_specs=(rows, rows, rows, rows, P("dp", None), P(("dp", "ctx"))),
        out_specs=(rows, rows, rows, rows),
        check_vma=False,
    )
```

time: 155 us -> 40.1 us (0.26)
  blocking collectives: 71.6 us -> 0 us
  waiting for transfers between devices: 26.7 us -> 7.37 us
  local copies, waits for them, and re-layouts: 18.9 us -> 1.34 us
  matrix products: 5.21 us -> 0 us
  Pallas kernels: 0 us -> 5.1 us
  starting transfers between devices: 29.3 us -> 24.4 us
    all_gather x5 -> x0, blocking collectives: 71.6 us -> none  [the longest x1 16.1 us: local(): query_piece = lax.all_gather(query_local, 'ctx', axis=0, tiled=True)]
    all_to_all x8 -> x2, waiting for transfers between devices: 26.7 us -> 0.01 us  [everywhere(): lax.all_to_all(x, ('dp', 'ctx'), split_axis=0, concat_axis=0, tiled=True)]
    all_to_all x8 -> x2, starting transfers between devices: 29.3 us -> 11.4 us  [everywhere(): lax.all_to_all(x, ('dp', 'ctx'), split_axis=0, concat_axis=0, tiled=True)]
    ppermute x0 -> x14, starting transfers between devices: none -> 13 us  [in_plane(): lax.ppermute(pieces[s], 'dp', [(i, i ^ s) for i in range(peers)])]
    ppermute x0 -> x14, waiting for transfers between devices: none -> 7.37 us  [in_plane(): lax.ppermute(pieces[s], 'dp', [(i, i ^ s) for i in range(peers)])]
    scatter x4 -> x0, local copies, waits for them, and re-layouts: 6.23 us -> none  [placed(): return jnp.zeros_like(computed).at[source_slot].set(computed)]
    dot_general x15 -> x0, matrix products: 5.21 us -> none  [the longest x8 2.44 us: contract_rows(): lax.dot_general(left, right, (((0,), (0,)), ((), ())), preferred_element_...]
    pallas_call x0 -> x4, Pallas kernels: none -> 5.1 us  [the longest x1 2.45 us: local(): pl.pallas_call(functools.partial(core_kernel, heads), out_shape=[low(p.sh...]
  transfers between devices with their start and end apart: 8 -> 16, of which waited for: 7 -> 5; matrix products, arithmetic and copies ran while one was open for 6% -> 0% of each run, Pallas kernels for 0% -> 3%
where the time goes in v1:
time: 40.1 us; the launch traced here: 39.7 us
  starting transfers between devices  24.4 us (61%)
  waiting for transfers between devices  7.37 us (18%)
  Pallas kernels  5.1 us (13%)
  local copies, waits for them, and re-layouts  1.34 us (3%)
  other arithmetic  0.86 us (2%)
  between operations  0.71 us (2%)
    ppermute x14, starting transfers between devices, in_plane(): lax.ppermute(pieces[s], 'dp', [(i, i ^ s) for i in range(peers)])  13 us
    all_to_all x2, starting transfers between devices, everywhere(): lax.all_to_all(x, ('dp', 'ctx'), split_axis=0, concat_axis=0, tiled=True)  11.4 us
    ppermute x14, waiting for transfers between devices, in_plane(): lax.ppermute(pieces[s], 'dp', [(i, i ^ s) for i in range(peers)])  7.37 us
    pallas_call x1, Pallas kernels, local(): pl.pallas_call(functools.partial(core_kernel, heads), out_shape=[low(p.sh...  2.45 us
    pallas_call x1, Pallas kernels, local(): pl.pallas_call(unpack_kernel, out_shape=[low((rows, wide))] * 2 + [low((r...  1.28 us
    pallas_call x1, Pallas kernels, local(): pl.pallas_call(functools.partial(mask_kernel, peer, swapped), out_shape=j...  0.81 us
  transfers between devices with their start and end apart: 16, of which 5 were waited for; matrix products, arithmetic and copies ran while one was open for 0% of the time, Pallas kernels for 3%

profile of v1, /device:TPU:0, one launch (start us, length us, event | category | flops | bytes accessed | tf_op | source)
XLA Modules:
  0.0 39.7 jit_solution(8526486061457794406)
XLA Ops:
  0.6 0.8 %pad_maximum_fusion = bf16[128,256]{1,0:T(8,128)(2,1)S(1)} fusion(bf16[128,128]{1,0:T(8,128)(2,1)} %param.8, bf16[128,128]{1,0:T(8,128)(2,1)} %param.7), kind=kLoop, calls=%fused_computation | loop fusion | flops 131072 | bytes 131072 | tf_op jit(solution)/shard_map/concatenate | solution.py:151
  1.4 0.7 %broadcast_in_dim.8 = bf16[8,4,16,256]{3,2,1,0:T(8,128)(2,1)} broadcast(bf16[8,16,256]{2,1,0:T(8,128)(2,1)S(1)} %bitcast.11), dimensions={0,2,3} | broadcast | bytes 327680 | tf_op jit(solution)/shard_map/broadcast_in_dim | solution.py:152
  2.1 0.0 copy-start
  2.1 0.0 copy-start.1
  2.1 7.3 %all-to-all-start = ((bf16[32,16,256]{2,1,0:T(8,128)(2,1)}), bf16[32,16,256]{2,1,0:T(8,128)(2,1)S(1)}, u32[]{:S(2)}, u32[]{:S(2)}) async-start(bf16[32,16,256]{2,1,0:T(8,128)(2,1)} %bitcast.4), calls=%async_computation | async-start | bytes 524288 | tf_op jit(solution)/shard_map/all_to_all | solution.py:156
  9.4 0.1 pad_add_fusion.place
  9.5 0.0 copy-done
  9.5 0.0 copy-done.1
  9.5 0.6 %pack.1 = (bf16[16,1024]{1,0:T(8,128)(2,1)S(1)}, bf16[16,1024]{1,0:T(8,128)(2,1)S(1)}, bf16[16,1024]{1,0:T(8,128)(2,1)S(1)}, bf16[16,1024]{1,0:T(8,128)(2,1)S(1)...) custom-call(s32[2]{0:T(128)S(1)} %pad_add_fusion.place, ...), custom_call_target="tpu_custom_call" | custom-call | tf_op jit(solution)/shard_map/pack/pallas_call | solution.py:169
  10.1 0.3 collective-permute-start
  10.4 1.7 %collective-permute-start.1 = (bf16[16,1024]{1,0:T(8,128)(2,1)S(1)}, bf16[16,1024]{1,0:T(8,128)(2,1)S(1)}, u32[]{:S(2)}, u32[]{:S(2)}) collective-permute-start(bf16[16,1024]{1,0:T(8,128)(2,1)S(1)} %get-tuple-element.23), channel_id=1, source_target_pairs={{0,8},{4,12},{8,0},{12,4},{16,24},{20,28},{24,16},{28,20},{1,9},{5... | collective-permute-start | bytes 98312 | tf_op jit(solution)/shard_map/ppermute | solution.py:163
  12.1 0.0 collective-permute-start.2
  12.1 1.7 %collective-permute-start.3 = (bf16[16,1024]{1,0:T(8,128)(2,1)S(1)}, bf16[16,1024]{1,0:T(8,128)(2,1)S(1)}, u32[]{:S(2)}, u32[]{:S(2)}) collective-permute-start(bf16[16,1024]{1,0:T(8,128)(2,1)S(1)} %get-tuple-element.25), channel_id=1, source_target_pairs={{0,16},{4,20},{8,24},{12,28},{16,0},{20,4},{24,8},{28,12},{1,17},{... | collective-permute-start | bytes 98312 | tf_op jit(solution)/shard_map/ppermute | solution.py:163
  13.8 0.1 collective-permute-start.4
  13.9 0.0 collective-permute-done.refs_1_
  13.9 2.6 %collective-permute-start.5 = (bf16[16,1024]{1,0:T(8,128)(2,1)S(1)}, bf16[16,1024]{1,0:T(8,128)(2,1)S(1)}, u32[]{:S(2)}, u32[]{:S(2)}) collective-permute-start(bf16[16,1024]{1,0:T(8,128)(2,1)S(1)} %get-tuple-element.27), channel_id=1, source_target_pairs={{0,24},{4,28},{8,16},{12,20},{16,8},{20,12},{24,0},{28,4},{1,25},{... | collective-permute-start | bytes 98312 | tf_op jit(solution)/shard_map/ppermute | solution.py:163
  16.5 0.0 collective-permute-done.1.refs_2_
  16.5 0.0 copy-start.2
  16.5 0.0 copy-start.3
  16.5 0.1 collective-permute-start.6
  16.6 0.6 %copy-done.2 = s32[1,17]{1,0:T(1,128)S(1)} copy-done((s32[1,17]{1,0:T(1,128)S(1)}, s32[1,17]{1,0:T(1,128)}, u32[]{:S(2)}) %copy-start.2) | copy-done | bytes 92
  17.2 0.0 copy-done.3
  17.2 0.8 %mask.1.bias = f32[128,128]{1,0:T(8,128)S(1)} custom-call(s32[2]{0:T(128)S(1)} %pad_add_fusion.place, s32[1,17]{1,0:T(1,128)S(1)} %copy-done.2, s32[1,128]{1,0:T(1,128)S(1)} %bitcast.10), custom_call_target="tpu_custom_call" | custom-call | tf_op jit(solution)/shard_map/mask/pallas_call | solution.py:180
  18.0 0.0 collective-permute-done.2.refs_3_
  18.0 0.0 collective-permute-done.3.refs_4_
  18.0 0.0 collective-permute-done.4.refs_5_
  18.0 1.0 %collective-permute-done.5.refs_6_ = bf16[16,1024]{1,0:T(8,128)(2,1)S(1)} collective-permute-done((bf16[16,1024]{1,0:T(8,128)(2,1)S(1)}, bf16[16,1024]{1,0:T(8,128)(2,1)S(1)}, u32[]{:S(2)}, u32[]{:S(2)}) %collective-permute-start.5) | collective-permute-done | bytes 32800 | tf_op jit(solution)/shard_map/ppermute | solution.py:163
  19.0 2.0 %collective-permute-done.6.refs_7_ = bf16[16,1024]{1,0:T(8,128)(2,1)S(1)} collective-permute-done((bf16[16,1024]{1,0:T(8,128)(2,1)S(1)}, bf16[16,1024]{1,0:T(8,128)(2,1)S(1)}, u32[]{:S(2)}, u32[]{:S(2)}) %collective-permute-start.6) | collective-permute-done | bytes 32800 | tf_op jit(solution)/shard_map/ppermute | solution.py:163
  21.0 0.0 all-to-all-done
  21.0 2.4 %core.1 = (bf16[16,1024]{1,0:T(8,128)(2,1)S(1)}, bf16[16,1024]{1,0:T(8,128)(2,1)S(1)}, bf16[16,1024]{1,0:T(8,128)(2,1)S(1)}, bf16[16,1024]{1,0:T(8,128)(2,1)S(1)...) custom-call(s32[2]{0:T(128)S(1)} %pad_add_fusion.place, ...), custom_call_target="tpu_custom_call" | custom-call | tf_op jit(solution)/shard_map/core/pallas_call | solution.py:192
  23.4 4.1 %all-to-all-start.1 = ((bf16[32,16,256]{2,1,0:T(8,128)(2,1)}), bf16[32,16,256]{2,1,0:T(8,128)(2,1)S(1)}, u32[]{:S(2)}, u32[]{:S(2)}) async-start(bf16[32,16,256]{2,1,0:T(8,128)(2,1)} %bitcast.6), calls=%async_computation.1 | async-start | bytes 524288 | tf_op jit(solution)/shard_map/all_to_all | solution.py:156
  27.5 0.3 collective-permute-start.7
  27.8 1.7 %collective-permute-start.8 = (bf16[16,1024]{1,0:T(8,128)(2,1)S(1)}, bf16[16,1024]{1,0:T(8,128)(2,1)S(1)}, u32[]{:S(2)}, u32[]{:S(2)}) collective-permute-start(bf16[16,1024]{1,0:T(8,128)(2,1)S(1)} %get-tuple-element.32), channel_id=1, source_target_pairs={{0,8},{4,12},{8,0},{12,4},{16,24},{20,28},{24,16},{28,20},{1,9},{5... | collective-permute-start | bytes 98312 | tf_op jit(solution)/shard_map/ppermute | solution.py:163
  29.5 0.0 collective-permute-start.9
  29.5 1.7 %collective-permute-start.10 = (bf16[16,1024]{1,0:T(8,128)(2,1)S(1)}, bf16[16,1024]{1,0:T(8,128)(2,1)S(1)}, u32[]{:S(2)}, u32[]{:S(2)}) collective-permute-start(bf16[16,1024]{1,0:T(8,128)(2,1)S(1)} %get-tuple-element.34), channel_id=1, source_target_pairs={{0,16},{4,20},{8,24},{12,28},{16,0},{20,4},{24,8},{28,12},{1,17},{... | collective-permute-start | bytes 98312 | tf_op jit(solution)/shard_map/ppermute | solution.py:163
  31.2 0.1 collective-permute-start.11
  31.3 0.0 collective-permute-done.7.refs_1_
  31.3 2.6 %collective-permute-start.12 = (bf16[16,1024]{1,0:T(8,128)(2,1)S(1)}, bf16[16,1024]{1,0:T(8,128)(2,1)S(1)}, u32[]{:S(2)}, u32[]{:S(2)}) collective-permute-start(bf16[16,1024]{1,0:T(8,128)(2,1)S(1)} %get-tuple-element.36), channel_id=1, source_target_pairs={{0,24},{4,28},{8,16},{12,20},{16,8},{20,12},{24,0},{28,4},{1,25},{... | collective-permute-start | bytes 98312 | tf_op jit(solution)/shard_map/ppermute | solution.py:163
  33.9 0.0 collective-permute-done.8.refs_2_
  33.9 0.2 collective-permute-start.13
  34.1 0.0 collective-permute-done.9.refs_3_
  34.1 0.0 collective-permute-done.10.refs_4_
  34.1 0.8 %collective-permute-done.11.refs_5_ = bf16[16,1024]{1,0:T(8,128)(2,1)S(1)} collective-permute-done((bf16[16,1024]{1,0:T(8,128)(2,1)S(1)}, bf16[16,1024]{1,0:T(8,128)(2,1)S(1)}, u32[]{:S(2)}, u32[]{:S(2)}) %collective-permute-start.11) | collective-permute-done | bytes 32800 | tf_op jit(solution)/shard_map/ppermute | solution.py:163
  34.9 1.4 %collective-permute-done.12.refs_6_ = bf16[16,1024]{1,0:T(8,128)(2,1)S(1)} collective-permute-done((bf16[16,1024]{1,0:T(8,128)(2,1)S(1)}, bf16[16,1024]{1,0:T(8,128)(2,1)S(1)}, u32[]{:S(2)}, u32[]{:S(2)}) %collective-permute-start.12) | collective-permute-done | bytes 32800 | tf_op jit(solution)/shard_map/ppermute | solution.py:163
  36.3 2.2 %collective-permute-done.13.refs_7_ = bf16[16,1024]{1,0:T(8,128)(2,1)S(1)} collective-permute-done((bf16[16,1024]{1,0:T(8,128)(2,1)S(1)}, bf16[16,1024]{1,0:T(8,128)(2,1)S(1)}, u32[]{:S(2)}, u32[]{:S(2)}) %collective-permute-start.13) | collective-permute-done | bytes 32800 | tf_op jit(solution)/shard_map/ppermute | solution.py:163
  38.5 0.0 all-to-all-done.1
  38.5 1.3 %unpack.1 = (bf16[128,512]{1,0:T(8,128)(2,1)}, bf16[128,512]{1,0:T(8,128)(2,1)}, bf16[128,128]{1,0:T(8,128)(2,1)}, bf16[128,128]{1,0:T(8,128)(2,1)}) custom-call(s32[2]{0:T(128)S(1)} %pad_add_fusion.place, bf16[8,4,16,256]{3,2,1,0:T(8,128)(2,1)S(1)} %bitcast.8, bf16[16,1024]{1,0:T(8,128)(2,1)S(1)} %get-tuple-element.30.refs_0_, ...), custom_call_target="tpu_custom_call" | custom-call | tf_op jit(solution)/shard_map/unpack/pallas_call | solution.py:216
Async XLA Ops:
  2.1 7.4 %copy-start = (bf16[128,512]{1,0:T(8,128)(2,1)S(1)}, bf16[128,512]{1,0:T(8,128)(2,1)}, u32[]{:S(2)}) copy-start(bf16[128,512]{1,0:T(8,128)(2,1)} %queries.1) | copy-start | bytes 393220
  2.1 7.4 %copy-start.1 = (bf16[128,512]{1,0:T(8,128)(2,1)S(1)}, bf16[128,512]{1,0:T(8,128)(2,1)}, u32[]{:S(2)}) copy-start(bf16[128,512]{1,0:T(8,128)(2,1)} %out_grad.1) | copy-start | bytes 393220
  2.1 18.9 %all-to-all-start = ((bf16[32,16,256]{2,1,0:T(8,128)(2,1)}), bf16[32,16,256]{2,1,0:T(8,128)(2,1)S(1)}, u32[]{:S(2)}, u32[]{:S(2)}) async-start(bf16[32,16,256]{2,1,0:T(8,128)(2,1)} %bitcast.4), calls=%async_computation | async-start | bytes 524288 | tf_op jit(solution)/shard_map/all_to_all | solution.py:156
  10.1 3.8 %collective-permute-start = (bf16[16,1024]{1,0:T(8,128)(2,1)S(1)}, bf16[16,1024]{1,0:T(8,128)(2,1)S(1)}, u32[]{:S(2)}, u32[]{:S(2)}) collective-permute-start(bf16[16,1024]{1,0:T(8,128)(2,1)S(1)} %get-tuple-element.22), channel_id=1, source_target_pairs={{0,4},{4,0},{8,12},{12,8},{16,20},{20,16},{24,28},{28,24},{1,5},{5... | collective-permute-start | bytes 98312 | tf_op jit(solution)/shard_map/ppermute | solution.py:163
  10.4 6.1 %collective-permute-start.1 = (bf16[16,1024]{1,0:T(8,128)(2,1)S(1)}, bf16[16,1024]{1,0:T(8,128)(2,1)S(1)}, u32[]{:S(2)}, u32[]{:S(2)}) collective-permute-start(bf16[16,1024]{1,0:T(8,128)(2,1)S(1)} %get-tuple-element.23), channel_id=1, source_target_pairs={{0,8},{4,12},{8,0},{12,4},{16,24},{20,28},{24,16},{28,20},{1,9},{5... | collective-permute-start | bytes 98312 | tf_op jit(solution)/shard_map/ppermute | solution.py:163
  12.1 5.9 %collective-permute-start.2 = (bf16[16,1024]{1,0:T(8,128)(2,1)S(1)}, bf16[16,1024]{1,0:T(8,128)(2,1)S(1)}, u32[]{:S(2)}, u32[]{:S(2)}) collective-permute-start(bf16[16,1024]{1,0:T(8,128)(2,1)S(1)} %get-tuple-element.24), channel_id=1, source_target_pairs={{0,12},{4,8},{8,4},{12,0},{16,28},{20,24},{24,20},{28,16},{1,13},{... | collective-permute-start | bytes 98312 | tf_op jit(solution)/shard_map/ppermute | solution.py:163
  12.1 5.9 %collective-permute-start.3 = (bf16[16,1024]{1,0:T(8,128)(2,1)S(1)}, bf16[16,1024]{1,0:T(8,128)(2,1)S(1)}, u32[]{:S(2)}, u32[]{:S(2)}) collective-permute-start(bf16[16,1024]{1,0:T(8,128)(2,1)S(1)} %get-tuple-element.25), channel_id=1, source_target_pairs={{0,16},{4,20},{8,24},{12,28},{16,0},{20,4},{24,8},{28,12},{1,17},{... | collective-permute-start | bytes 98312 | tf_op jit(solution)/shard_map/ppermute | solution.py:163
  13.8 4.2 %collective-permute-start.4 = (bf16[16,1024]{1,0:T(8,128)(2,1)S(1)}, bf16[16,1024]{1,0:T(8,128)(2,1)S(1)}, u32[]{:S(2)}, u32[]{:S(2)}) collective-permute-start(bf16[16,1024]{1,0:T(8,128)(2,1)S(1)} %get-tuple-element.26), channel_id=1, source_target_pairs={{0,20},{4,16},{8,28},{12,24},{16,4},{20,0},{24,12},{28,8},{1,21},{... | collective-permute-start | bytes 98312 | tf_op jit(solution)/shard_map/ppermute | solution.py:163
  13.9 5.1 %collective-permute-start.5 = (bf16[16,1024]{1,0:T(8,128)(2,1)S(1)}, bf16[16,1024]{1,0:T(8,128)(2,1)S(1)}, u32[]{:S(2)}, u32[]{:S(2)}) collective-permute-start(bf16[16,1024]{1,0:T(8,128)(2,1)S(1)} %get-tuple-element.27), channel_id=1, source_target_pairs={{0,24},{4,28},{8,16},{12,20},{16,8},{20,12},{24,0},{28,4},{1,25},{... | collective-permute-start | bytes 98312 | tf_op jit(solution)/shard_map/ppermute | solution.py:163
  16.5 0.7 %copy-start.2 = (s32[1,17]{1,0:T(1,128)S(1)}, s32[1,17]{1,0:T(1,128)}, u32[]{:S(2)}) copy-start(s32[1,17]{1,0:T(1,128)} %lengths.3) | copy-start | bytes 208
  16.5 0.7 %copy-start.3 = (s32[128]{0:T(128)S(1)}, s32[128]{0:T(128)}, u32[]{:S(2)}) copy-start(s32[128]{0:T(128)} %param.11) | copy-start | bytes 1540
  16.5 4.5 %collective-permute-start.6 = (bf16[16,1024]{1,0:T(8,128)(2,1)S(1)}, bf16[16,1024]{1,0:T(8,128)(2,1)S(1)}, u32[]{:S(2)}, u32[]{:S(2)}) collective-permute-start(bf16[16,1024]{1,0:T(8,128)(2,1)S(1)} %get-tuple-element.28), channel_id=1, source_target_pairs={{0,28},{4,24},{8,20},{12,16},{16,12},{20,8},{24,4},{28,0},{1,29},{... | collective-permute-start | bytes 98312 | tf_op jit(solution)/shard_map/ppermute | solution.py:163
  23.4 15.0 %all-to-all-start.1 = ((bf16[32,16,256]{2,1,0:T(8,128)(2,1)}), bf16[32,16,256]{2,1,0:T(8,128)(2,1)S(1)}, u32[]{:S(2)}, u32[]{:S(2)}) async-start(bf16[32,16,256]{2,1,0:T(8,128)(2,1)} %bitcast.6), calls=%async_computation.1 | async-start | bytes 524288 | tf_op jit(solution)/shard_map/all_to_all | solution.py:156
  27.5 3.8 %collective-permute-start.7 = (bf16[16,1024]{1,0:T(8,128)(2,1)S(1)}, bf16[16,1024]{1,0:T(8,128)(2,1)S(1)}, u32[]{:S(2)}, u32[]{:S(2)}) collective-permute-start(bf16[16,1024]{1,0:T(8,128)(2,1)S(1)} %get-tuple-element.31), channel_id=1, source_target_pairs={{0,4},{4,0},{8,12},{12,8},{16,20},{20,16},{24,28},{28,24},{1,5},{5... | collective-permute-start | bytes 98312 | tf_op jit(solution)/shard_map/ppermute | solution.py:163
  27.8 6.1 %collective-permute-start.8 = (bf16[16,1024]{1,0:T(8,128)(2,1)S(1)}, bf16[16,1024]{1,0:T(8,128)(2,1)S(1)}, u32[]{:S(2)}, u32[]{:S(2)}) collective-permute-start(bf16[16,1024]{1,0:T(8,128)(2,1)S(1)} %get-tuple-element.32), channel_id=1, source_target_pairs={{0,8},{4,12},{8,0},{12,4},{16,24},{20,28},{24,16},{28,20},{1,9},{5... | collective-permute-start | bytes 98312 | tf_op jit(solution)/shard_map/ppermute | solution.py:163
  29.5 4.6 %collective-permute-start.9 = (bf16[16,1024]{1,0:T(8,128)(2,1)S(1)}, bf16[16,1024]{1,0:T(8,128)(2,1)S(1)}, u32[]{:S(2)}, u32[]{:S(2)}) collective-permute-start(bf16[16,1024]{1,0:T(8,128)(2,1)S(1)} %get-tuple-element.33), channel_id=1, source_target_pairs={{0,12},{4,8},{8,4},{12,0},{16,28},{20,24},{24,20},{28,16},{1,13},{... | collective-permute-start | bytes 98312 | tf_op jit(solution)/shard_map/ppermute | solution.py:163
  29.5 4.6 %collective-permute-start.10 = (bf16[16,1024]{1,0:T(8,128)(2,1)S(1)}, bf16[16,1024]{1,0:T(8,128)(2,1)S(1)}, u32[]{:S(2)}, u32[]{:S(2)}) collective-permute-start(bf16[16,1024]{1,0:T(8,128)(2,1)S(1)} %get-tuple-element.34), channel_id=1, source_target_pairs={{0,16},{4,20},{8,24},{12,28},{16,0},{20,4},{24,8},{28,12},{1,17},{... | collective-permute-start | bytes 98312 | tf_op jit(solution)/shard_map/ppermute | solution.py:163
  31.2 3.7 %collective-permute-start.11 = (bf16[16,1024]{1,0:T(8,128)(2,1)S(1)}, bf16[16,1024]{1,0:T(8,128)(2,1)S(1)}, u32[]{:S(2)}, u32[]{:S(2)}) collective-permute-start(bf16[16,1024]{1,0:T(8,128)(2,1)S(1)} %get-tuple-element.35), channel_id=1, source_target_pairs={{0,20},{4,16},{8,28},{12,24},{16,4},{20,0},{24,12},{28,8},{1,21},{... | collective-permute-start | bytes 98312 | tf_op jit(solution)/shard_map/ppermute | solution.py:163
  31.3 4.9 %collective-permute-start.12 = (bf16[16,1024]{1,0:T(8,128)(2,1)S(1)}, bf16[16,1024]{1,0:T(8,128)(2,1)S(1)}, u32[]{:S(2)}, u32[]{:S(2)}) collective-permute-start(bf16[16,1024]{1,0:T(8,128)(2,1)S(1)} %get-tuple-element.36), channel_id=1, source_target_pairs={{0,24},{4,28},{8,16},{12,20},{16,8},{20,12},{24,0},{28,4},{1,25},{... | collective-permute-start | bytes 98312 | tf_op jit(solution)/shard_map/ppermute | solution.py:163
  33.9 4.5 %collective-permute-start.13 = (bf16[16,1024]{1,0:T(8,128)(2,1)S(1)}, bf16[16,1024]{1,0:T(8,128)(2,1)S(1)}, u32[]{:S(2)}, u32[]{:S(2)}) collective-permute-start(bf16[16,1024]{1,0:T(8,128)(2,1)S(1)} %get-tuple-element.37), channel_id=1, source_target_pairs={{0,28},{4,24},{8,20},{12,16},{16,12},{20,8},{24,4},{28,0},{1,29},{... | collective-permute-start | bytes 98312 | tf_op jit(solution)/shard_map/ppermute | solution.py:163

commit v2 on v1

v2 whole, which is shorter than its diff:
```python
import functools

import jax
import jax.numpy as jnp
from jax import lax
from jax.experimental import pallas as pl
from jax.experimental.pallas import tpu as pltpu
from jax.sharding import PartitionSpec as P

HIDDEN = -1e30
VMEM = pl.BlockSpec(memory_space=pltpu.VMEM)
SMEM = pl.BlockSpec(memory_space=pltpu.SMEM)
HBM = pl.BlockSpec(memory_space=pltpu.HBM)


def contract(left, right):
    return lax.dot_general(
        left, right, (((1,), (1,)), ((), ())), preferred_element_type=jnp.float32
    )


def multiply(left, right):
    return jnp.dot(left, right, preferred_element_type=jnp.float32)


def params(mib):
    return pltpu.CompilerParams(vmem_limit_bytes=mib * 1024 * 1024)


def low(shape):
    return jax.ShapeDtypeStruct(shape, jnp.bfloat16)


def near(shape):
    return pltpu.VMEM(shape, jnp.bfloat16)


def far(x):
    return pltpu.with_memory_space_constraint(x, pltpu.HBM)


def ordered(blocks):
    if len(blocks) == 1:
        return [blocks[0]]
    first, second = blocks[:-1], blocks[-1]
    return [piece for k, block in enumerate(first) for piece in (block.at[0], second.at[k])]


def parted(blocks):
    if len(blocks) == 1:
        return [blocks[0]]
    return [block.at[core] for block in blocks for core in range(2)]


def fill_bias(peer, swapped, lengths, slot_row, bias):
    rows = slot_row.shape[1]
    own, first = lax.axis_index("dp"), lax.axis_index("ctx") * rows
    slot = jnp.broadcast_to(slot_row[...], (rows, rows))
    along = lax.broadcasted_iota(jnp.int32, (rows, rows), 1)
    down = lax.broadcasted_iota(jnp.int32, (rows, rows), 0)
    key_pos = jnp.sum(jnp.where(slot == down, along, 0), axis=1, keepdims=True)
    slot_down = slot.astype(jnp.float32).T.astype(jnp.int32)
    wanted = lax.bitwise_xor(along // peer, own) * peer + along % peer if swapped else along
    query_pos = jnp.sum(jnp.where(slot_down == wanted, down, 0), axis=0, keepdims=True)

    def later(k, carry):
        end, start = carry
        end = end + lengths[0, k]
        return end, jnp.where(query_pos + first >= end, end, start)

    _, doc_start = lax.fori_loop(
        0, lengths.shape[1], later, (jnp.int32(0), jnp.zeros((1, rows), jnp.int32))
    )
    seen = (key_pos <= query_pos) & (key_pos + first >= doc_start)
    bias[:rows, :] = jnp.where(seen, 0.0, HIDDEN)
    joined = jnp.where(first < lengths[0, 0], 0.0, HIDDEN).astype(jnp.float32)
    bias[rows:, :] = jnp.full((bias.shape[0] - rows, rows), joined)


def pack_kernel(keys, values, queries, out_grad, lengths, slot_row, *refs):
    *pieces, bias, kv, kv_buf, query_buf, grad_buf, length_buf, slot_buf, sems = refs
    own = lax.axis_index("dp")
    wide, width = queries.shape[1], keys.shape[2]
    peers, planes, peer, _ = kv.shape
    come = [
        pltpu.make_async_copy(keys, kv_buf.at[:, :, :width], sems.at[0]),
        pltpu.make_async_copy(values, kv_buf.at[:, :, width:], sems.at[1]),
        pltpu.make_async_copy(queries, query_buf, sems.at[2]),
        pltpu.make_async_copy(out_grad, grad_buf, sems.at[3]),
        pltpu.make_async_copy(lengths, length_buf, sems.at[4]),
        pltpu.make_async_copy(slot_row, slot_buf, sems.at[5]),
    ]
    for copy in come:
        copy.start()
    come[0].wait()
    come[1].wait()
    leave = [pltpu.make_async_copy(kv_buf, kv.at[:, j], sems.at[6 + j]) for j in range(planes)]
    for copy in leave:
        copy.start()
    come[4].wait()
    come[5].wait()
    fill_bias(peer, True, length_buf, slot_buf, bias)
    for k, buf in enumerate((query_buf, grad_buf)):
        come[2 + k].wait()
        for index, piece in enumerate(parted(pieces)):
            start = pl.multiple_of(lax.bitwise_xor(own, index) * peer, peer)
            piece[:, k * wide : (k + 1) * wide] = buf[pl.ds(start, peer), :]
    for copy in leave:
        copy.wait()


def join_kernel(*refs):
    *blocks, out = refs
    for k, block in enumerate(blocks):
        out[k] = block[1]


def core_kernel(heads, taken, bias, kv, *refs):
    pieces = ordered(refs[:taken])
    *returned, kv_grad, key_all, value_all, query_flat, grad_flat, probs_all, score_all = refs[
        taken:-2
    ]
    grad_buf, sem = refs[-2:]
    returned = parted(returned)
    peers, planes, peer, both = kv.shape
    width = both // 2
    rows = peers * peer
    wide = heads * width
    scale = width**-0.5
    plane = lax.axis_index("ctx")
    for j in range(planes):
        block = kv[:, j].reshape(rows, both)
        key_all[j * rows : (j + 1) * rows, :] = block[:, :width]
        value_all[j * rows : (j + 1) * rows, :] = block[:, width:]
    size = pieces[0].shape[0]
    for index, piece in enumerate(pieces):
        for h in range(heads):
            at = h * rows + index * size
            query_flat[at : at + size, :] = piece[:, h * width : (h + 1) * width]
            grad_flat[at : at + size, :] = piece[:, wide + h * width : wide + (h + 1) * width]
    seen, before = bias[:rows, :], bias[rows : rows + 1, :]
    added = []
    for j in range(planes):
        other = jnp.where(plane > j, before, HIDDEN)
        added.append(jnp.where(plane == j, seen, other))
    added = jnp.concatenate(added, axis=0)
    for h in range(heads):
        own = slice(h * rows, (h + 1) * rows)
        score = contract(key_all[...], query_flat[own, :]) * scale + added
        weight = jnp.exp(score - jnp.max(score, axis=0, keepdims=True))
        probs = weight * (1.0 / jnp.sum(weight, axis=0, keepdims=True))
        prob_grad = contract(value_all[...], grad_flat[own, :])
        delta = jnp.sum(probs * prob_grad, axis=0, keepdims=True)
        probs_all[:, own] = probs.astype(jnp.bfloat16)
        score_all[:, own] = (probs * (prob_grad - delta)).astype(jnp.bfloat16)
    key_grad = (multiply(score_all[...], query_flat[...]) * scale).astype(jnp.bfloat16)
    value_grad = multiply(probs_all[...], grad_flat[...]).astype(jnp.bfloat16)
    for j in range(planes):
        own = slice(j * rows, (j + 1) * rows)
        grad_buf[:, j, :, :width] = key_grad[own].reshape(peers, peer, width)
        grad_buf[:, j, :, width:] = value_grad[own].reshape(peers, peer, width)
    leave = pltpu.make_async_copy(grad_buf, kv_grad, sem)
    leave.start()
    attended = multiply(value_all[...].T, probs_all[...]).astype(jnp.bfloat16)
    query_grad = (multiply(key_all[...].T, score_all[...]) * scale).astype(jnp.bfloat16)
    for k, source in enumerate((attended, query_grad)):
        for h in range(heads):
            turned = source[:, h * rows : (h + 1) * rows].T
            at = (k * heads + h) * width
            for index, piece in enumerate(returned):
                piece[:, at : at + width] = turned[index * size : (index + 1) * size]
    leave.wait()


def last_kernel(kv, *refs):
    *blocks, attended, query_grad, key_grad, value_grad, key_buf, value_buf, sems = refs
    pieces = ordered(blocks)
    wide, size = attended.shape[1], pieces[0].shape[0]
    own = lax.axis_index("dp") if len(pieces) > 1 else 0
    copies = []
    for index, piece in enumerate(pieces):
        start = pl.multiple_of(lax.bitwise_xor(own, index) * size, size)
        for k, target in enumerate((attended, query_grad)):
            copies.append(
                pltpu.make_async_copy(
                    piece.at[:, k * wide : (k + 1) * wide],
                    target.at[pl.ds(start, size), :],
                    sems.at[len(copies)],
                )
            )
            copies[-1].start()
    peers, planes, peer, both = kv.shape
    width = both // 2
    for k, (buf, target) in enumerate(((key_buf, key_grad), (value_buf, value_grad))):
        part = slice(k * width, (k + 1) * width)
        total = kv[:, 0, :, part].astype(jnp.float32)
        for j in range(1, planes):
            total = total + kv[:, j, :, part].astype(jnp.float32)
        buf[...] = total.reshape(peers * peer, width).astype(jnp.bfloat16)
        copies.append(pltpu.make_async_copy(buf, target, sems.at[len(copies)]))
        copies[-1].start()
    for copy in copies:
        copy.wait()


def local(queries, keys, values, out_grad, doc_lengths, source_slot):
    rows, wide = queries.shape
    width = keys.shape[1]
    heads = wide // width
    peers, planes = lax.axis_size("dp"), lax.axis_size("ctx")
    peer = rows // peers
    fine = peer % 16 == 0
    swapped = peers == 8 and fine
    kv_shape = (peers, planes, peer, 2 * width)

    def everywhere(x):
        x = x.reshape(peers * planes, peer, 2 * width)
        x = lax.all_to_all(x, ("dp", "ctx"), split_axis=0, concat_axis=0, tiled=True)
        return x.reshape(kv_shape)

    def in_plane(pieces):
        if not swapped:
            return [lax.all_to_all(pieces[0], "dp", split_axis=0, concat_axis=0, tiled=True)]
        came = [pieces[0]] + [
            lax.ppermute(pieces[s], "dp", [(i, i ^ (2 * s)) for i in range(peers)])
            for s in range(1, peers // 2)
        ]
        other = pl.pallas_call(
            join_kernel,
            out_shape=near((peers // 2, peer, 2 * wide)),
            in_specs=[VMEM] * len(came),
            out_specs=VMEM,
            compiler_params=params(4),
            name="join",
        )(*came)
        return came + [lax.ppermute(other, "dp", [(i, i ^ 1) for i in range(peers)])]

    slot_row = source_slot.reshape(1, rows)
    if swapped:
        sent = [near((2, peer, 2 * wide))] * (peers // 2)
        *pieces, bias, kv = pl.pallas_call(
            pack_kernel,
            out_shape=sent + [pltpu.VMEM((rows + 8, rows), jnp.float32), low(kv_shape)],
            in_specs=[HBM] * 6,
            out_specs=[VMEM] * (len(sent) + 1) + [HBM],
            scratch_shapes=[
                pltpu.VMEM((peers, peer, 2 * width), jnp.bfloat16),
                pltpu.VMEM((rows, wide), jnp.bfloat16),
                pltpu.VMEM((rows, wide), jnp.bfloat16),
                pltpu.SMEM(doc_lengths.shape, jnp.int32),
                pltpu.VMEM(slot_row.shape, jnp.int32),
                pltpu.SemaphoreType.DMA((6 + planes,)),
            ],
            compiler_params=params(4),
            name="pack",
        )(
            far(keys.reshape(peers, peer, width)),
            far(values.reshape(peers, peer, width)),
            far(queries),
            far(out_grad),
            far(doc_lengths),
            far(slot_row),
        )
    else:
        sent = [low((rows, 2 * wide))]
        kv = jnp.concatenate([keys, values], axis=1).reshape(peers, 1, peer, 2 * width)
        kv = jnp.broadcast_to(kv, kv_shape)
        pieces = [jnp.concatenate([queries, out_grad], axis=1)]
        bias = pl.pallas_call(
            functools.partial(fill_bias, peer, False),
            out_shape=jax.ShapeDtypeStruct((rows + 8, rows), jnp.float32),
            in_specs=[SMEM, VMEM],
            out_specs=VMEM,
            compiler_params=params(4),
            name="mask",
        )(doc_lengths, slot_row)
    kv = everywhere(kv)
    pieces = in_plane(pieces)
    if not fine:
        kv = kv.transpose(1, 0, 2, 3).reshape(1, planes, rows, 2 * width)
    count = rows * planes
    *pieces, kv = pl.pallas_call(
        functools.partial(core_kernel, heads, len(pieces)),
        out_shape=sent + [low(kv.shape)],
        in_specs=[VMEM] * (2 + len(pieces)),
        out_specs=[VMEM] * len(sent) + [HBM],
        scratch_shapes=[
            pltpu.VMEM((count, width), jnp.bfloat16),
            pltpu.VMEM((count, width), jnp.bfloat16),
            pltpu.VMEM((rows * heads, width), jnp.bfloat16),
            pltpu.VMEM((rows * heads, width), jnp.bfloat16),
            pltpu.VMEM((count, rows * heads), jnp.bfloat16),
            pltpu.VMEM((count, rows * heads), jnp.bfloat16),
            pltpu.VMEM(kv.shape, jnp.bfloat16),
            pltpu.SemaphoreType.DMA,
        ],
        compiler_params=params(16 if planes <= 4 else 48),
        name="core",
    )(bias, kv, *pieces)
    if not fine:
        kv = kv.reshape(planes, peers, peer, 2 * width).transpose(1, 0, 2, 3)
    kv = everywhere(kv)
    if not fine:
        kv = kv.transpose(1, 0, 2, 3).reshape(1, planes, rows, 2 * width)
    pieces = in_plane(pieces)
    count = 8 * 2 if swapped else 2
    return tuple(
        pl.pallas_call(
            last_kernel,
            out_shape=[low((rows, wide))] * 2 + [low((rows, width))] * 2,
            in_specs=[VMEM] * (1 + len(pieces)),
            out_specs=[HBM] * 4,
            scratch_shapes=[
                pltpu.VMEM((rows, width), jnp.bfloat16),
                pltpu.VMEM((rows, width), jnp.bfloat16),
                pltpu.SemaphoreType.DMA((count + 2,)),
            ],
            compiler_params=params(8),
            name="last",
        )(kv, *pieces)
    )


def solution(mesh):
    rows = P(("dp", "ctx"), None)
    return jax.shard_map(
        local,
        mesh=mesh,
        in_specs=(rows, rows, rows, rows, P("dp", None), P(("dp", "ctx"))),
        out_specs=(rows, rows, rows, rows),
        check_vma=False,
    )
```

time: 40.1 us -> 37.4 us (0.933)
  waiting for transfers between devices: 7.37 us -> 13.1 us
  starting transfers between devices: 24.4 us -> 19 us
  local copies, waits for them, and re-layouts: 1.34 us -> 0 us
  other arithmetic: 0.86 us -> 0 us
  Pallas kernels: 5.1 us -> 4.38 us
    ppermute x14 -> x8, starting transfers between devices: 13 us -> 7.25 us  [the longest x6 7.11 us: in_plane(): lax.ppermute(pieces[s], 'dp', [(i, i ^ 2 * s) for i in range(peers)])]
    ppermute x14 -> x8, waiting for transfers between devices: 7.37 us -> 12.9 us  [the longest x6 10.3 us: in_plane(): lax.ppermute(pieces[s], 'dp', [(i, i ^ 2 * s) for i in range(peers)])]
    concatenate x1 -> x0, other arithmetic: 0.78 us -> none  [local(): jnp.concatenate([keys, values], axis=1).reshape(peers, 1, peer, 2 * width)]
    pallas_call x4 -> x5, Pallas kernels: 5.1 us -> 4.38 us  [the longest x1 1.91 us: local(): pl.pallas_call(functools.partial(core_kernel, heads, len(pieces)), out_sh...]
    broadcast_in_dim x1 -> x0, local copies, waits for them, and re-layouts: 0.72 us -> none  [local(): kv = jnp.broadcast_to(kv, (peers, planes, peer, 2 * width))]
    unnamed x8 -> x0, local copies, waits for them, and re-layouts: 0.62 us -> none
  transfers between devices with their start and end apart: 16 -> 10, of which waited for: 5 -> 10; matrix products, arithmetic and copies ran while one was open for 0% -> 0% of each run, Pallas kernels for 3% -> 0%
where the time goes in v2:
time: 37.4 us; the launch traced here: 37.1 us
  starting transfers between devices  19 us (51%)
  waiting for transfers between devices  13.1 us (35%)
  Pallas kernels  4.38 us (12%)
  between operations  0.7 us (2%)
    all_to_all x2, starting transfers between devices, everywhere(): lax.all_to_all(x, ('dp', 'ctx'), split_axis=0, concat_axis=0, tiled=True)  11.7 us
    ppermute x6, waiting for transfers between devices, in_plane(): lax.ppermute(pieces[s], 'dp', [(i, i ^ 2 * s) for i in range(peers)])  10.3 us
    ppermute x6, starting transfers between devices, in_plane(): lax.ppermute(pieces[s], 'dp', [(i, i ^ 2 * s) for i in range(peers)])  7.11 us
    ppermute x2, waiting for transfers between devices, in_plane(): lax.ppermute(other, 'dp', [(i, i ^ 1) for i in range(peers)])  2.67 us
    pallas_call x1, Pallas kernels, local(): pl.pallas_call(functools.partial(core_kernel, heads, len(pieces)), out_sh...  1.91 us
    pallas_call x1, Pallas kernels, local(): pl.pallas_call(pack_kernel, out_shape=sent + [pltpu.VMEM((rows + 8, rows)...  1.57 us
    pallas_call x1, Pallas kernels, local(): pl.pallas_call(last_kernel, out_shape=[low((rows, wide))] * 2 + [low((row...  0.88 us
  transfers between devices with their start and end apart: 10, of which 10 were waited for; matrix products, arithmetic and copies ran while one was open for 0% of the time, Pallas kernels for 0%

profile of v2, /device:TPU:0, one launch (start us, length us, event | category | flops | bytes accessed | tf_op | source)
XLA Modules:
  0.0 37.1 jit_solution(10604785293029938534)
XLA Ops:
  0.6 1.6 %pack.1 = (bf16[2,16,1024]{2,1,0:T(8,128)(2,1)S(1)}, bf16[2,16,1024]{2,1,0:T(8,128)(2,1)S(1)}, bf16[2,16,1024]{2,1,0:T(8,128)(2,1)S(1)}, bf16[2,16,1024]{2,1,0:T...) custom-call(bf16[8,16,128]{2,1,0:T(8,128)(2,1)} %bitcast.9, bf16[8,16,128]{2,1,0:T(8,128)(2,1)} %bitcast.10, ...), custom_call_target="tpu_custom_call" | custom-call | tf_op jit(solution)/shard_map/pack/pallas_call | solution.py:241
  2.2 7.3 %all-to-all-start = ((bf16[32,16,256]{2,1,0:T(8,128)(2,1)}), bf16[32,16,256]{2,1,0:T(8,128)(2,1)S(1)}, u32[]{:S(2)}, u32[]{:S(2)}) async-start(bf16[32,16,256]{2,1,0:T(8,128)(2,1)} %bitcast.3), calls=%async_computation | async-start | bytes 524288 | tf_op jit(solution)/shard_map/all_to_all | solution.py:218
  9.5 1.8 %collective-permute-start = (bf16[2,16,1024]{2,1,0:T(8,128)(2,1)S(1)}, bf16[2,16,1024]{2,1,0:T(8,128)(2,1)S(1)}, u32[]{:S(2)}, u32[]{:S(2)}) collective-permute-start(bf16[2,16,1024]{2,1,0:T(8,128)(2,1)S(1)} %get-tuple-element.18), channel_id=1, source_target_pairs={{0,8},{4,12},{8,0},{12,4},{16,24},{20,28},{24,16},{28,20},{1,9},{5... | collective-permute-start | bytes 196616 | tf_op jit(solution)/shard_map/ppermute | solution.py:225
  11.4 1.5 %collective-permute-start.1 = (bf16[2,16,1024]{2,1,0:T(8,128)(2,1)S(1)}, bf16[2,16,1024]{2,1,0:T(8,128)(2,1)S(1)}, u32[]{:S(2)}, u32[]{:S(2)}) collective-permute-start(bf16[2,16,1024]{2,1,0:T(8,128)(2,1)S(1)} %get-tuple-element.19), channel_id=1, source_target_pairs={{0,16},{4,20},{8,24},{12,28},{16,0},{20,4},{24,8},{28,12},{1,17},{... | collective-permute-start | bytes 196616 | tf_op jit(solution)/shard_map/ppermute | solution.py:225
  12.8 0.3 collective-permute-start.2
  13.1 2.9 %collective-permute-done.refs_1_ = bf16[2,16,1024]{2,1,0:T(8,128)(2,1)S(1)} collective-permute-done((bf16[2,16,1024]{2,1,0:T(8,128)(2,1)S(1)}, bf16[2,16,1024]{2,1,0:T(8,128)(2,1)S(1)}, u32[]{:S(2)}, u32[]{:S(2)}) %collective-permute-start) | collective-permute-done | bytes 65568 | tf_op jit(solution)/shard_map/ppermute | solution.py:225
  16.0 1.8 %collective-permute-done.1.refs_2_ = bf16[2,16,1024]{2,1,0:T(8,128)(2,1)S(1)} collective-permute-done((bf16[2,16,1024]{2,1,0:T(8,128)(2,1)S(1)}, bf16[2,16,1024]{2,1,0:T(8,128)(2,1)S(1)}, u32[]{:S(2)}, u32[]{:S(2)}) %collective-permute-start.1) | collective-permute-done | bytes 65568 | tf_op jit(solution)/shard_map/ppermute | solution.py:225
  17.8 0.4 %collective-permute-done.2.refs_3_ = bf16[2,16,1024]{2,1,0:T(8,128)(2,1)S(1)} collective-permute-done((bf16[2,16,1024]{2,1,0:T(8,128)(2,1)S(1)}, bf16[2,16,1024]{2,1,0:T(8,128)(2,1)S(1)}, u32[]{:S(2)}, u32[]{:S(2)}) %collective-permute-start.2) | collective-permute-done | bytes 65568 | tf_op jit(solution)/shard_map/ppermute | solution.py:225
  18.2 0.1 collective-permute-start.3
  18.3 1.3 %collective-permute-done.3.refs_4_ = bf16[4,16,1024]{2,1,0:T(8,128)(2,1)S(1)} collective-permute-done((bf16[4,16,1024]{2,1,0:T(8,128)(2,1)S(1)}, bf16[4,16,1024]{2,1,0:T(8,128)(2,1)S(1)}, u32[]{:S(2)}, u32[]{:S(2)}) %collective-permute-start.3) | collective-permute-done | bytes 131104 | tf_op jit(solution)/shard_map/ppermute | solution.py:236
  19.6 0.1 all-to-all-done
  19.7 1.9 %core.1 = (bf16[2,16,1024]{2,1,0:T(8,128)(2,1)S(1)}, bf16[2,16,1024]{2,1,0:T(8,128)(2,1)S(1)}, bf16[2,16,1024]{2,1,0:T(8,128)(2,1)S(1)}, bf16[2,16,1024]{2,1,0:T(8,128)(2,1)S(1)}, bf16[8,4,16,256]{3,2,1,0:T(8,128)(2,1)}) custom-call(f32[136,128]{1,0:T(8,128)S(1)} %get-tuple-element.15.bias, bf16[8,4,16,256]{3,2,1,0:T(8,128)(2,1)S(1)} %bitcast.8, ...), custom_call_target="tpu_custom_call" | custom-call | tf_op jit(solution)/shard_map/core/pallas_call | solution.py:282
  21.6 4.4 %all-to-all-start.1 = ((bf16[32,16,256]{2,1,0:T(8,128)(2,1)}), bf16[32,16,256]{2,1,0:T(8,128)(2,1)S(1)}, u32[]{:S(2)}, u32[]{:S(2)}) async-start(bf16[32,16,256]{2,1,0:T(8,128)(2,1)} %bitcast.5), calls=%async_computation.1 | async-start | bytes 524288 | tf_op jit(solution)/shard_map/all_to_all | solution.py:218
  26.1 1.8 %collective-permute-start.4 = (bf16[2,16,1024]{2,1,0:T(8,128)(2,1)S(1)}, bf16[2,16,1024]{2,1,0:T(8,128)(2,1)S(1)}, u32[]{:S(2)}, u32[]{:S(2)}) collective-permute-start(bf16[2,16,1024]{2,1,0:T(8,128)(2,1)S(1)} %get-tuple-element.23), channel_id=1, source_target_pairs={{0,8},{4,12},{8,0},{12,4},{16,24},{20,28},{24,16},{28,20},{1,9},{5... | collective-permute-start | bytes 196616 | tf_op jit(solution)/shard_map/ppermute | solution.py:225
  27.9 1.5 %collective-permute-start.5 = (bf16[2,16,1024]{2,1,0:T(8,128)(2,1)S(1)}, bf16[2,16,1024]{2,1,0:T(8,128)(2,1)S(1)}, u32[]{:S(2)}, u32[]{:S(2)}) collective-permute-start(bf16[2,16,1024]{2,1,0:T(8,128)(2,1)S(1)} %get-tuple-element.24), channel_id=1, source_target_pairs={{0,16},{4,20},{8,24},{12,28},{16,0},{20,4},{24,8},{28,12},{1,17},{... | collective-permute-start | bytes 196616 | tf_op jit(solution)/shard_map/ppermute | solution.py:225
  29.4 0.3 collective-permute-start.6
  29.6 2.9 %collective-permute-done.4.refs_1_ = bf16[2,16,1024]{2,1,0:T(8,128)(2,1)S(1)} collective-permute-done((bf16[2,16,1024]{2,1,0:T(8,128)(2,1)S(1)}, bf16[2,16,1024]{2,1,0:T(8,128)(2,1)S(1)}, u32[]{:S(2)}, u32[]{:S(2)}) %collective-permute-start.4) | collective-permute-done | bytes 65568 | tf_op jit(solution)/shard_map/ppermute | solution.py:225
  32.6 1.8 %collective-permute-done.5.refs_2_ = bf16[2,16,1024]{2,1,0:T(8,128)(2,1)S(1)} collective-permute-done((bf16[2,16,1024]{2,1,0:T(8,128)(2,1)S(1)}, bf16[2,16,1024]{2,1,0:T(8,128)(2,1)S(1)}, u32[]{:S(2)}, u32[]{:S(2)}) %collective-permute-start.5) | collective-permute-done | bytes 65568 | tf_op jit(solution)/shard_map/ppermute | solution.py:225
  34.4 0.4 %collective-permute-done.6.refs_3_ = bf16[2,16,1024]{2,1,0:T(8,128)(2,1)S(1)} collective-permute-done((bf16[2,16,1024]{2,1,0:T(8,128)(2,1)S(1)}, bf16[2,16,1024]{2,1,0:T(8,128)(2,1)S(1)}, u32[]{:S(2)}, u32[]{:S(2)}) %collective-permute-start.6) | collective-permute-done | bytes 65568 | tf_op jit(solution)/shard_map/ppermute | solution.py:225
  34.8 0.1 collective-permute-start.7
  34.8 1.3 %collective-permute-done.7.refs_4_ = bf16[4,16,1024]{2,1,0:T(8,128)(2,1)S(1)} collective-permute-done((bf16[4,16,1024]{2,1,0:T(8,128)(2,1)S(1)}, bf16[4,16,1024]{2,1,0:T(8,128)(2,1)S(1)}, u32[]{:S(2)}, u32[]{:S(2)}) %collective-permute-start.7) | collective-permute-done | bytes 131104 | tf_op jit(solution)/shard_map/ppermute | solution.py:236
  36.2 0.1 all-to-all-done.1
  36.3 0.9 %last.1 = (bf16[128,512]{1,0:T(8,128)(2,1)}, bf16[128,512]{1,0:T(8,128)(2,1)}, bf16[128,128]{1,0:T(8,128)(2,1)}, bf16[128,128]{1,0:T(8,128)(2,1)}) custom-call(bf16[8,4,16,256]{3,2,1,0:T(8,128)(2,1)S(1)} %bitcast.7, bf16[2,16,1024]{2,1,0:T(8,128)(2,1)S(1)} %get-tuple-element.22.refs_0_, bf16[2,16,1024]{2,1,0:T(8,128)(2,1)S(1)} %collective-permute-done.4.refs_1_, ...), custom_call_target="tpu_custom_call" | custom-call | tf_op jit(solution)/shard_map/last/pallas_call | solution.py:308
  (2 shorter events, 0.0 us)
Async XLA Ops:
  2.2 17.5 %all-to-all-start = ((bf16[32,16,256]{2,1,0:T(8,128)(2,1)}), bf16[32,16,256]{2,1,0:T(8,128)(2,1)S(1)}, u32[]{:S(2)}, u32[]{:S(2)}) async-start(bf16[32,16,256]{2,1,0:T(8,128)(2,1)} %bitcast.3), calls=%async_computation | async-start | bytes 524288 | tf_op jit(solution)/shard_map/all_to_all | solution.py:218
  9.5 6.5 %collective-permute-start = (bf16[2,16,1024]{2,1,0:T(8,128)(2,1)S(1)}, bf16[2,16,1024]{2,1,0:T(8,128)(2,1)S(1)}, u32[]{:S(2)}, u32[]{:S(2)}) collective-permute-start(bf16[2,16,1024]{2,1,0:T(8,128)(2,1)S(1)} %get-tuple-element.18), channel_id=1, source_target_pairs={{0,8},{4,12},{8,0},{12,4},{16,24},{20,28},{24,16},{28,20},{1,9},{5... | collective-permute-start | bytes 196616 | tf_op jit(solution)/shard_map/ppermute | solution.py:225
  11.4 6.5 %collective-permute-start.1 = (bf16[2,16,1024]{2,1,0:T(8,128)(2,1)S(1)}, bf16[2,16,1024]{2,1,0:T(8,128)(2,1)S(1)}, u32[]{:S(2)}, u32[]{:S(2)}) collective-permute-start(bf16[2,16,1024]{2,1,0:T(8,128)(2,1)S(1)} %get-tuple-element.19), channel_id=1, source_target_pairs={{0,16},{4,20},{8,24},{12,28},{16,0},{20,4},{24,8},{28,12},{1,17},{... | collective-permute-start | bytes 196616 | tf_op jit(solution)/shard_map/ppermute | solution.py:225
  12.8 5.4 %collective-permute-start.2 = (bf16[2,16,1024]{2,1,0:T(8,128)(2,1)S(1)}, bf16[2,16,1024]{2,1,0:T(8,128)(2,1)S(1)}, u32[]{:S(2)}, u32[]{:S(2)}) collective-permute-start(bf16[2,16,1024]{2,1,0:T(8,128)(2,1)S(1)} %get-tuple-element.20), channel_id=1, source_target_pairs={{0,24},{4,28},{8,16},{12,20},{16,8},{20,12},{24,0},{28,4},{1,25},{... | collective-permute-start | bytes 196616 | tf_op jit(solution)/shard_map/ppermute | solution.py:225
  18.2 1.4 %collective-permute-start.3 = (bf16[4,16,1024]{2,1,0:T(8,128)(2,1)S(1)}, bf16[4,16,1024]{2,1,0:T(8,128)(2,1)S(1)}, u32[]{:S(2)}, u32[]{:S(2)}) collective-permute-start(bf16[4,16,1024]{2,1,0:T(8,128)(2,1)S(1)} %join.2), channel_id=1, source_target_pairs={{0,4},{4,0},{8,12},{12,8},{16,20},{20,16},{24,28},{28,24},{1,5},{5... | collective-permute-start | bytes 393224 | tf_op jit(solution)/shard_map/ppermute | solution.py:236
  21.6 14.6 %all-to-all-start.1 = ((bf16[32,16,256]{2,1,0:T(8,128)(2,1)}), bf16[32,16,256]{2,1,0:T(8,128)(2,1)S(1)}, u32[]{:S(2)}, u32[]{:S(2)}) async-start(bf16[32,16,256]{2,1,0:T(8,128)(2,1)} %bitcast.5), calls=%async_computation.1 | async-start | bytes 524288 | tf_op jit(solution)/shard_map/all_to_all | solution.py:218
  26.1 6.5 %collective-permute-start.4 = (bf16[2,16,1024]{2,1,0:T(8,128)(2,1)S(1)}, bf16[2,16,1024]{2,1,0:T(8,128)(2,1)S(1)}, u32[]{:S(2)}, u32[]{:S(2)}) collective-permute-start(bf16[2,16,1024]{2,1,0:T(8,128)(2,1)S(1)} %get-tuple-element.23), channel_id=1, source_target_pairs={{0,8},{4,12},{8,0},{12,4},{16,24},{20,28},{24,16},{28,20},{1,9},{5... | collective-permute-start | bytes 196616 | tf_op jit(solution)/shard_map/ppermute | solution.py:225
  27.9 6.5 %collective-permute-start.5 = (bf16[2,16,1024]{2,1,0:T(8,128)(2,1)S(1)}, bf16[2,16,1024]{2,1,0:T(8,128)(2,1)S(1)}, u32[]{:S(2)}, u32[]{:S(2)}) collective-permute-start(bf16[2,16,1024]{2,1,0:T(8,128)(2,1)S(1)} %get-tuple-element.24), channel_id=1, source_target_pairs={{0,16},{4,20},{8,24},{12,28},{16,0},{20,4},{24,8},{28,12},{1,17},{... | collective-permute-start | bytes 196616 | tf_op jit(solution)/shard_map/ppermute | solution.py:225
  29.4 5.4 %collective-permute-start.6 = (bf16[2,16,1024]{2,1,0:T(8,128)(2,1)S(1)}, bf16[2,16,1024]{2,1,0:T(8,128)(2,1)S(1)}, u32[]{:S(2)}, u32[]{:S(2)}) collective-permute-start(bf16[2,16,1024]{2,1,0:T(8,128)(2,1)S(1)} %get-tuple-element.25), channel_id=1, source_target_pairs={{0,24},{4,28},{8,16},{12,20},{16,8},{20,12},{24,0},{28,4},{1,25},{... | collective-permute-start | bytes 196616 | tf_op jit(solution)/shard_map/ppermute | solution.py:225
  34.8 1.4 %collective-permute-start.7 = (bf16[4,16,1024]{2,1,0:T(8,128)(2,1)S(1)}, bf16[4,16,1024]{2,1,0:T(8,128)(2,1)S(1)}, u32[]{:S(2)}, u32[]{:S(2)}) collective-permute-start(bf16[4,16,1024]{2,1,0:T(8,128)(2,1)S(1)} %join.3), channel_id=1, source_target_pairs={{0,4},{4,0},{8,12},{12,8},{16,20},{20,16},{24,28},{28,24},{1,5},{5... | collective-permute-start | bytes 393224 | tf_op jit(solution)/shard_map/ppermute | solution.py:236

commit v3 on v2

--- a/solution.py
+++ b/solution.py
@@ -39,17 +39,18 @@
     return pltpu.with_memory_space_constraint(x, pltpu.HBM)
 
 
-def ordered(blocks):
-    if len(blocks) == 1:
-        return [blocks[0]]
-    first, second = blocks[:-1], blocks[-1]
-    return [piece for k, block in enumerate(first) for piece in (block.at[0], second.at[k])]
-
-
 def parted(blocks):
     if len(blocks) == 1:
         return [blocks[0]]
-    return [block.at[core] for block in blocks for core in range(2)]
+    kept, crossed = blocks
+    return [half.at[k] for k in range(kept.shape[0]) for half in (kept, crossed)]
+
+
+def paired(blocks):
+    if len(blocks) == 1:
+        return [blocks[0]]
+    kept, swapped, *chips = blocks
+    return [kept.at[0], swapped.at[0]] + [chip.at[core] for chip in chips for core in range(2)]
 
 
 def fill_bias(peer, swapped, lengths, slot_row, bias):
@@ -78,7 +79,7 @@
 
 
 def pack_kernel(keys, values, queries, out_grad, lengths, slot_row, *refs):
-    *pieces, bias, kv, kv_buf, query_buf, grad_buf, length_buf, slot_buf, sems = refs
+    kept, crossed, bias, kv, kv_buf, query_buf, grad_buf, length_buf, slot_buf, sems = refs
     own = lax.axis_index("dp")
     wide, width = queries.shape[1], keys.shape[2]
     peers, planes, peer, _ = kv.shape
@@ -102,21 +103,21 @@
     fill_bias(peer, True, length_buf, slot_buf, bias)
     for k, buf in enumerate((query_buf, grad_buf)):
         come[2 + k].wait()
-        for index, piece in enumerate(parted(pieces)):
+        for index, piece in enumerate(parted((kept, crossed))):
             start = pl.multiple_of(lax.bitwise_xor(own, index) * peer, peer)
             piece[:, k * wide : (k + 1) * wide] = buf[pl.ds(start, peer), :]
     for copy in leave:
         copy.wait()
 
 
-def join_kernel(*refs):
-    *blocks, out = refs
-    for k, block in enumerate(blocks):
-        out[k] = block[1]
+def pair_kernel(kept, swapped, *out):
+    for k, block in enumerate(out):
+        block[0] = kept[k + 1]
+        block[1] = swapped[k + 1]
 
 
 def core_kernel(heads, taken, bias, kv, *refs):
-    pieces = ordered(refs[:taken])
+    pieces = paired(refs[:taken])
     *returned, kv_grad, key_all, value_all, query_flat, grad_flat, probs_all, score_all = refs[
         taken:-2
     ]
@@ -174,7 +175,7 @@
 
 def last_kernel(kv, *refs):
     *blocks, attended, query_grad, key_grad, value_grad, key_buf, value_buf, sems = refs
-    pieces = ordered(blocks)
+    pieces = paired(blocks)
     wide, size = attended.shape[1], pieces[0].shape[0]
     own = lax.axis_index("dp") if len(pieces) > 1 else 0
     copies = []
@@ -218,31 +219,32 @@
         x = lax.all_to_all(x, ("dp", "ctx"), split_axis=0, concat_axis=0, tiled=True)
         return x.reshape(kv_shape)
 
+    def swap(x, mask):
+        return lax.ppermute(x, "dp", [(i, i ^ mask) for i in range(peers)])
+
     def in_plane(pieces):
         if not swapped:
             return [lax.all_to_all(pieces[0], "dp", split_axis=0, concat_axis=0, tiled=True)]
-        came = [pieces[0]] + [
-            lax.ppermute(pieces[s], "dp", [(i, i ^ (2 * s)) for i in range(peers)])
-            for s in range(1, peers // 2)
-        ]
-        other = pl.pallas_call(
-            join_kernel,
-            out_shape=near((peers // 2, peer, 2 * wide)),
-            in_specs=[VMEM] * len(came),
-            out_specs=VMEM,
+        kept, crossed = pieces
+        crossed = swap(crossed, 1)
+        chips = pl.pallas_call(
+            pair_kernel,
+            out_shape=[near((2, peer, 2 * wide))] * (peers // 2 - 1),
+            in_specs=[VMEM] * 2,
+            out_specs=[VMEM] * (peers // 2 - 1),
             compiler_params=params(4),
-            name="join",
-        )(*came)
-        return came + [lax.ppermute(other, "dp", [(i, i ^ 1) for i in range(peers)])]
+            name="pair",
+        )(kept, crossed)
+        return [kept, crossed] + [swap(chip, 2 * s + 2) for s, chip in enumerate(chips)]
 
     slot_row = source_slot.reshape(1, rows)
     if swapped:
-        sent = [near((2, peer, 2 * wide))] * (peers // 2)
+        sent = [near((peers // 2, peer, 2 * wide))] * 2
         *pieces, bias, kv = pl.pallas_call(
             pack_kernel,
             out_shape=sent + [pltpu.VMEM((rows + 8, rows), jnp.float32), low(kv_shape)],
             in_specs=[HBM] * 6,
-            out_specs=[VMEM] * (len(sent) + 1) + [HBM],
+            out_specs=[VMEM] * 3 + [HBM],
             scratch_shapes=[
                 pltpu.VMEM((peers, peer, 2 * width), jnp.bfloat16),
                 pltpu.VMEM((rows, wide), jnp.bfloat16),

time: 37.4 us -> 36.8 us (0.984)
  waiting for transfers between devices: 13.1 us -> 12.6 us
    ppermute x8, waiting for transfers between devices: 12.9 us -> 12.3 us  [swap(): return lax.ppermute(x, 'dp', [(i, i ^ mask) for i in range(peers)])]
    all_to_all x2, starting transfers between devices: 11.7 us -> 11.1 us  [everywhere(): lax.all_to_all(x, ('dp', 'ctx'), split_axis=0, concat_axis=0, tiled=True)]
    ppermute x8, starting transfers between devices: 7.25 us -> 7.74 us  [swap(): return lax.ppermute(x, 'dp', [(i, i ^ mask) for i in range(peers)])]
where the time goes in v3:
time: 36.8 us; the launch traced here: 36.5 us
  starting transfers between devices  18.8 us (51%)
  waiting for transfers between devices  12.6 us (34%)
  Pallas kernels  4.4 us (12%)
  between operations  0.68 us (2%)
    ppermute x8, waiting for transfers between devices, swap(): return lax.ppermute(x, 'dp', [(i, i ^ mask) for i in range(peers)])  12.3 us
    all_to_all x2, starting transfers between devices, everywhere(): lax.all_to_all(x, ('dp', 'ctx'), split_axis=0, concat_axis=0, tiled=True)  11.1 us
    ppermute x8, starting transfers between devices, swap(): return lax.ppermute(x, 'dp', [(i, i ^ mask) for i in range(peers)])  7.74 us
    pallas_call x1, Pallas kernels, local(): pl.pallas_call(functools.partial(core_kernel, heads, len(pieces)), out_sh...  1.92 us
    pallas_call x1, Pallas kernels, local(): pl.pallas_call(pack_kernel, out_shape=sent + [pltpu.VMEM((rows + 8, rows)...  1.57 us
    pallas_call x1, Pallas kernels, local(): pl.pallas_call(last_kernel, out_shape=[low((rows, wide))] * 2 + [low((row...  0.88 us
  transfers between devices with their start and end apart: 10, of which 10 were waited for; matrix products, arithmetic and copies ran while one was open for 0% of the time, Pallas kernels for 0%

profile of v3, /device:TPU:0, one launch (start us, length us, event | category | flops | bytes accessed | tf_op | source)
XLA Modules:
  0.0 36.5 jit_solution(5326132753441416379)
XLA Ops:
  0.6 1.6 %pack.1 = (bf16[4,16,1024]{2,1,0:T(8,128)(2,1)S(1)}, bf16[4,16,1024]{2,1,0:T(8,128)(2,1)S(1)}, f32[136,128]{1,0:T(8,128)S(1)}, bf16[8,4,16,256]{3,2,1,0:T(8,128)(2,1)}) custom-call(bf16[8,16,128]{2,1,0:T(8,128)(2,1)} %bitcast.9, bf16[8,16,128]{2,1,0:T(8,128)(2,1)} %bitcast.10, bf16[128,512]{1,0:T(8,128)(2,1)} %queries.1, bf16[128,512]{1,0:T(8,128)(2,1)} %out_grad.1, ...), custom_call_target="tpu_custom_call" | custom-call | tf_op jit(solution)/shard_map/pack/pallas_call | solution.py:243
  2.2 7.3 %all-to-all-start = ((bf16[32,16,256]{2,1,0:T(8,128)(2,1)}), bf16[32,16,256]{2,1,0:T(8,128)(2,1)S(1)}, u32[]{:S(2)}, u32[]{:S(2)}) async-start(bf16[32,16,256]{2,1,0:T(8,128)(2,1)} %bitcast.3), calls=%async_computation | async-start | bytes 524288 | tf_op jit(solution)/shard_map/all_to_all | solution.py:219
  9.5 0.3 collective-permute-start
  9.8 1.1 %collective-permute-done.swapped.refs_1_ = bf16[4,16,1024]{2,1,0:T(8,128)(2,1)S(1)} collective-permute-done((bf16[4,16,1024]{2,1,0:T(8,128)(2,1)S(1)}, bf16[4,16,1024]{2,1,0:T(8,128)(2,1)S(1)}, u32[]{:S(2)}, u32[]{:S(2)}) %collective-permute-start) | collective-permute-done | bytes 131104 | tf_op jit(solution)/shard_map/ppermute | solution.py:223
  10.9 1.8 %collective-permute-start.1 = (bf16[2,16,1024]{2,1,0:T(8,128)(2,1)S(1)}, bf16[2,16,1024]{2,1,0:T(8,128)(2,1)S(1)}, u32[]{:S(2)}, u32[]{:S(2)}) collective-permute-start(bf16[2,16,1024]{2,1,0:T(8,128)(2,1)S(1)} %get-tuple-element.21), channel_id=1, source_target_pairs={{0,8},{4,12},{8,0},{12,4},{16,24},{20,28},{24,16},{28,20},{1,9},{5... | collective-permute-start | bytes 196616 | tf_op jit(solution)/shard_map/ppermute | solution.py:223
  12.8 1.5 %collective-permute-start.2 = (bf16[2,16,1024]{2,1,0:T(8,128)(2,1)S(1)}, bf16[2,16,1024]{2,1,0:T(8,128)(2,1)S(1)}, u32[]{:S(2)}, u32[]{:S(2)}) collective-permute-start(bf16[2,16,1024]{2,1,0:T(8,128)(2,1)S(1)} %get-tuple-element.22), channel_id=1, source_target_pairs={{0,16},{4,20},{8,24},{12,28},{16,0},{20,4},{24,8},{28,12},{1,17},{... | collective-permute-start | bytes 196616 | tf_op jit(solution)/shard_map/ppermute | solution.py:223
  14.2 0.3 collective-permute-start.3
  14.5 1.6 %collective-permute-done.1.refs_2_ = bf16[2,16,1024]{2,1,0:T(8,128)(2,1)S(1)} collective-permute-done((bf16[2,16,1024]{2,1,0:T(8,128)(2,1)S(1)}, bf16[2,16,1024]{2,1,0:T(8,128)(2,1)S(1)}, u32[]{:S(2)}, u32[]{:S(2)}) %collective-permute-start.1) | collective-permute-done | bytes 65568 | tf_op jit(solution)/shard_map/ppermute | solution.py:223
  16.1 1.9 %collective-permute-done.2.refs_3_ = bf16[2,16,1024]{2,1,0:T(8,128)(2,1)S(1)} collective-permute-done((bf16[2,16,1024]{2,1,0:T(8,128)(2,1)S(1)}, bf16[2,16,1024]{2,1,0:T(8,128)(2,1)S(1)}, u32[]{:S(2)}, u32[]{:S(2)}) %collective-permute-start.2) | collective-permute-done | bytes 65568 | tf_op jit(solution)/shard_map/ppermute | solution.py:223
  18.1 1.5 %collective-permute-done.3.refs_4_ = bf16[2,16,1024]{2,1,0:T(8,128)(2,1)S(1)} collective-permute-done((bf16[2,16,1024]{2,1,0:T(8,128)(2,1)S(1)}, bf16[2,16,1024]{2,1,0:T(8,128)(2,1)S(1)}, u32[]{:S(2)}, u32[]{:S(2)}) %collective-permute-start.3) | collective-permute-done | bytes 65568 | tf_op jit(solution)/shard_map/ppermute | solution.py:223
  19.5 0.2 all-to-all-done
  19.7 1.9 %core.1 = (bf16[4,16,1024]{2,1,0:T(8,128)(2,1)S(1)}, bf16[4,16,1024]{2,1,0:T(8,128)(2,1)S(1)}, bf16[8,4,16,256]{3,2,1,0:T(8,128)(2,1)}) custom-call(f32[136,128]{1,0:T(8,128)S(1)} %get-tuple-element.17.bias, bf16[8,4,16,256]{3,2,1,0:T(8,128)(2,1)S(1)} %bitcast.7, bf16[4,16,1024]{2,1,0:T(8,128)(2,1)S(1)} %get-tuple-element.19.kept.refs_0_, ...), custom_call_target="tpu_custom_call" | custom-call | tf_op jit(solution)/shard_map/core/pallas_call | solution.py:284
  21.6 3.8 %all-to-all-start.1 = ((bf16[32,16,256]{2,1,0:T(8,128)(2,1)}), bf16[32,16,256]{2,1,0:T(8,128)(2,1)S(1)}, u32[]{:S(2)}, u32[]{:S(2)}) async-start(bf16[32,16,256]{2,1,0:T(8,128)(2,1)} %bitcast.5), calls=%async_computation.1 | async-start | bytes 524288 | tf_op jit(solution)/shard_map/all_to_all | solution.py:219
  25.5 0.3 collective-permute-start.4
  25.8 1.1 %collective-permute-done.4.swapped.refs_1_ = bf16[4,16,1024]{2,1,0:T(8,128)(2,1)S(1)} collective-permute-done((bf16[4,16,1024]{2,1,0:T(8,128)(2,1)S(1)}, bf16[4,16,1024]{2,1,0:T(8,128)(2,1)S(1)}, u32[]{:S(2)}, u32[]{:S(2)}) %collective-permute-start.4) | collective-permute-done | bytes 131104 | tf_op jit(solution)/shard_map/ppermute | solution.py:223
  26.9 1.8 %collective-permute-start.5 = (bf16[2,16,1024]{2,1,0:T(8,128)(2,1)S(1)}, bf16[2,16,1024]{2,1,0:T(8,128)(2,1)S(1)}, u32[]{:S(2)}, u32[]{:S(2)}) collective-permute-start(bf16[2,16,1024]{2,1,0:T(8,128)(2,1)S(1)} %get-tuple-element.27), channel_id=1, source_target_pairs={{0,8},{4,12},{8,0},{12,4},{16,24},{20,28},{24,16},{28,20},{1,9},{5... | collective-permute-start | bytes 196616 | tf_op jit(solution)/shard_map/ppermute | solution.py:223
  28.7 1.5 %collective-permute-start.6 = (bf16[2,16,1024]{2,1,0:T(8,128)(2,1)S(1)}, bf16[2,16,1024]{2,1,0:T(8,128)(2,1)S(1)}, u32[]{:S(2)}, u32[]{:S(2)}) collective-permute-start(bf16[2,16,1024]{2,1,0:T(8,128)(2,1)S(1)} %get-tuple-element.28), channel_id=1, source_target_pairs={{0,16},{4,20},{8,24},{12,28},{16,0},{20,4},{24,8},{28,12},{1,17},{... | collective-permute-start | bytes 196616 | tf_op jit(solution)/shard_map/ppermute | solution.py:223
  30.2 0.3 collective-permute-start.7
  30.4 1.6 %collective-permute-done.5.refs_2_ = bf16[2,16,1024]{2,1,0:T(8,128)(2,1)S(1)} collective-permute-done((bf16[2,16,1024]{2,1,0:T(8,128)(2,1)S(1)}, bf16[2,16,1024]{2,1,0:T(8,128)(2,1)S(1)}, u32[]{:S(2)}, u32[]{:S(2)}) %collective-permute-start.5) | collective-permute-done | bytes 65568 | tf_op jit(solution)/shard_map/ppermute | solution.py:223
  32.0 1.9 %collective-permute-done.6.refs_3_ = bf16[2,16,1024]{2,1,0:T(8,128)(2,1)S(1)} collective-permute-done((bf16[2,16,1024]{2,1,0:T(8,128)(2,1)S(1)}, bf16[2,16,1024]{2,1,0:T(8,128)(2,1)S(1)}, u32[]{:S(2)}, u32[]{:S(2)}) %collective-permute-start.6) | collective-permute-done | bytes 65568 | tf_op jit(solution)/shard_map/ppermute | solution.py:223
  34.0 1.5 %collective-permute-done.7.refs_4_ = bf16[2,16,1024]{2,1,0:T(8,128)(2,1)S(1)} collective-permute-done((bf16[2,16,1024]{2,1,0:T(8,128)(2,1)S(1)}, bf16[2,16,1024]{2,1,0:T(8,128)(2,1)S(1)}, u32[]{:S(2)}, u32[]{:S(2)}) %collective-permute-start.7) | collective-permute-done | bytes 65568 | tf_op jit(solution)/shard_map/ppermute | solution.py:223
  35.5 0.2 all-to-all-done.1
  35.6 0.9 %last.1 = (bf16[128,512]{1,0:T(8,128)(2,1)}, bf16[128,512]{1,0:T(8,128)(2,1)}, bf16[128,128]{1,0:T(8,128)(2,1)}, bf16[128,128]{1,0:T(8,128)(2,1)}) custom-call(bf16[8,4,16,256]{3,2,1,0:T(8,128)(2,1)S(1)} %bitcast.8, bf16[4,16,1024]{2,1,0:T(8,128)(2,1)S(1)} %get-tuple-element.25.kept.refs_0_, bf16[4,16,1024]{2,1,0:T(8,128)(2,1)S(1)} %collective-permute-done.4.swapped.refs_1_, ...), custom_call_target="tpu_custom_call" | custom-call | tf_op jit(solution)/shard_map/last/pallas_call | solution.py:310
  (2 shorter events, 0.0 us)
Async XLA Ops:
  2.2 17.5 %all-to-all-start = ((bf16[32,16,256]{2,1,0:T(8,128)(2,1)}), bf16[32,16,256]{2,1,0:T(8,128)(2,1)S(1)}, u32[]{:S(2)}, u32[]{:S(2)}) async-start(bf16[32,16,256]{2,1,0:T(8,128)(2,1)} %bitcast.3), calls=%async_computation | async-start | bytes 524288 | tf_op jit(solution)/shard_map/all_to_all | solution.py:219
  9.5 1.4 %collective-permute-start = (bf16[4,16,1024]{2,1,0:T(8,128)(2,1)S(1)}, bf16[4,16,1024]{2,1,0:T(8,128)(2,1)S(1)}, u32[]{:S(2)}, u32[]{:S(2)}) collective-permute-start(bf16[4,16,1024]{2,1,0:T(8,128)(2,1)S(1)} %get-tuple-element.20), channel_id=1, source_target_pairs={{0,4},{4,0},{8,12},{12,8},{16,20},{20,16},{24,28},{28,24},{1,5},{5... | collective-permute-start | bytes 393224 | tf_op jit(solution)/shard_map/ppermute | solution.py:223
  10.9 5.2 %collective-permute-start.1 = (bf16[2,16,1024]{2,1,0:T(8,128)(2,1)S(1)}, bf16[2,16,1024]{2,1,0:T(8,128)(2,1)S(1)}, u32[]{:S(2)}, u32[]{:S(2)}) collective-permute-start(bf16[2,16,1024]{2,1,0:T(8,128)(2,1)S(1)} %get-tuple-element.21), channel_id=1, source_target_pairs={{0,8},{4,12},{8,0},{12,4},{16,24},{20,28},{24,16},{28,20},{1,9},{5... | collective-permute-start | bytes 196616 | tf_op jit(solution)/shard_map/ppermute | solution.py:223
  12.8 5.3 %collective-permute-start.2 = (bf16[2,16,1024]{2,1,0:T(8,128)(2,1)S(1)}, bf16[2,16,1024]{2,1,0:T(8,128)(2,1)S(1)}, u32[]{:S(2)}, u32[]{:S(2)}) collective-permute-start(bf16[2,16,1024]{2,1,0:T(8,128)(2,1)S(1)} %get-tuple-element.22), channel_id=1, source_target_pairs={{0,16},{4,20},{8,24},{12,28},{16,0},{20,4},{24,8},{28,12},{1,17},{... | collective-permute-start | bytes 196616 | tf_op jit(solution)/shard_map/ppermute | solution.py:223
  14.2 5.3 %collective-permute-start.3 = (bf16[2,16,1024]{2,1,0:T(8,128)(2,1)S(1)}, bf16[2,16,1024]{2,1,0:T(8,128)(2,1)S(1)}, u32[]{:S(2)}, u32[]{:S(2)}) collective-permute-start(bf16[2,16,1024]{2,1,0:T(8,128)(2,1)S(1)} %get-tuple-element.23), channel_id=1, source_target_pairs={{0,24},{4,28},{8,16},{12,20},{16,8},{20,12},{24,0},{28,4},{1,25},{... | collective-permute-start | bytes 196616 | tf_op jit(solution)/shard_map/ppermute | solution.py:223
  21.6 14.0 %all-to-all-start.1 = ((bf16[32,16,256]{2,1,0:T(8,128)(2,1)}), bf16[32,16,256]{2,1,0:T(8,128)(2,1)S(1)}, u32[]{:S(2)}, u32[]{:S(2)}) async-start(bf16[32,16,256]{2,1,0:T(8,128)(2,1)} %bitcast.5), calls=%async_computation.1 | async-start | bytes 524288 | tf_op jit(solution)/shard_map/all_to_all | solution.py:219
  25.5 1.4 %collective-permute-start.4 = (bf16[4,16,1024]{2,1,0:T(8,128)(2,1)S(1)}, bf16[4,16,1024]{2,1,0:T(8,128)(2,1)S(1)}, u32[]{:S(2)}, u32[]{:S(2)}) collective-permute-start(bf16[4,16,1024]{2,1,0:T(8,128)(2,1)S(1)} %get-tuple-element.26), channel_id=1, source_target_pairs={{0,4},{4,0},{8,12},{12,8},{16,20},{20,16},{24,28},{28,24},{1,5},{5... | collective-permute-start | bytes 393224 | tf_op jit(solution)/shard_map/ppermute | solution.py:223
  26.9 5.2 %collective-permute-start.5 = (bf16[2,16,1024]{2,1,0:T(8,128)(2,1)S(1)}, bf16[2,16,1024]{2,1,0:T(8,128)(2,1)S(1)}, u32[]{:S(2)}, u32[]{:S(2)}) collective-permute-start(bf16[2,16,1024]{2,1,0:T(8,128)(2,1)S(1)} %get-tuple-element.27), channel_id=1, source_target_pairs={{0,8},{4,12},{8,0},{12,4},{16,24},{20,28},{24,16},{28,20},{1,9},{5... | collective-permute-start | bytes 196616 | tf_op jit(solution)/shard_map/ppermute | solution.py:223
  28.7 5.3 %collective-permute-start.6 = (bf16[2,16,1024]{2,1,0:T(8,128)(2,1)S(1)}, bf16[2,16,1024]{2,1,0:T(8,128)(2,1)S(1)}, u32[]{:S(2)}, u32[]{:S(2)}) collective-permute-start(bf16[2,16,1024]{2,1,0:T(8,128)(2,1)S(1)} %get-tuple-element.28), channel_id=1, source_target_pairs={{0,16},{4,20},{8,24},{12,28},{16,0},{20,4},{24,8},{28,12},{1,17},{... | collective-permute-start | bytes 196616 | tf_op jit(solution)/shard_map/ppermute | solution.py:223
  30.2 5.3 %collective-permute-start.7 = (bf16[2,16,1024]{2,1,0:T(8,128)(2,1)S(1)}, bf16[2,16,1024]{2,1,0:T(8,128)(2,1)S(1)}, u32[]{:S(2)}, u32[]{:S(2)}) collective-permute-start(bf16[2,16,1024]{2,1,0:T(8,128)(2,1)S(1)} %get-tuple-element.29), channel_id=1, source_target_pairs={{0,24},{4,28},{8,16},{12,20},{16,8},{20,12},{24,0},{28,4},{1,25},{... | collective-permute-start | bytes 196616 | tf_op jit(solution)/shard_map/ppermute | solution.py:223

commit v4 on v3

--- a/solution.py
+++ b/solution.py
@@ -1,4 +1,5 @@
 import functools
+import math
 
 import jax
 import jax.numpy as jnp
@@ -117,6 +118,15 @@
 
 
 def core_kernel(heads, taken, bias, kv, *refs):
+    planes, plane = kv.shape[1], lax.axis_index("ctx")
+    if planes > 4:
+        core(heads, taken, None, bias, kv, *refs)
+        return
+    for k in range(planes):
+        pl.when(plane == k)(functools.partial(core, heads, taken, k, bias, kv, *refs))
+
+
+def core(heads, taken, plane, bias, kv, *refs):
     pieces = paired(refs[:taken])
     *returned, kv_grad, key_all, value_all, query_flat, grad_flat, probs_all, score_all = refs[
         taken:-2
@@ -128,42 +138,49 @@
     rows = peers * peer
     wide = heads * width
     scale = width**-0.5
-    plane = lax.axis_index("ctx")
-    for j in range(planes):
+    seen, before = bias[:rows, :], bias[rows : rows + 1, :]
+    added = []
+    for j in range(planes if plane is None else plane + 1):
+        if plane is None:
+            other = jnp.where(lax.axis_index("ctx") > j, before, HIDDEN)
+            added.append(jnp.where(lax.axis_index("ctx") == j, seen, other))
+        else:
+            added.append(seen if j == plane else jnp.broadcast_to(before, (rows, rows)))
         block = kv[:, j].reshape(rows, both)
         key_all[j * rows : (j + 1) * rows, :] = block[:, :width]
         value_all[j * rows : (j + 1) * rows, :] = block[:, width:]
+    count = len(added) * rows
+    added = jnp.concatenate(added, axis=0)
     size = pieces[0].shape[0]
     for index, piece in enumerate(pieces):
         for h in range(heads):
             at = h * rows + index * size
             query_flat[at : at + size, :] = piece[:, h * width : (h + 1) * width]
             grad_flat[at : at + size, :] = piece[:, wide + h * width : wide + (h + 1) * width]
-    seen, before = bias[:rows, :], bias[rows : rows + 1, :]
-    added = []
-    for j in range(planes):
-        other = jnp.where(plane > j, before, HIDDEN)
-        added.append(jnp.where(plane == j, seen, other))
-    added = jnp.concatenate(added, axis=0)
-    for h in range(heads):
-        own = slice(h * rows, (h + 1) * rows)
-        score = contract(key_all[...], query_flat[own, :]) * scale + added
-        weight = jnp.exp(score - jnp.max(score, axis=0, keepdims=True))
+    at_once = 2 if heads % 2 == 0 else 1
+    added = jnp.concatenate([added] * at_once, axis=1)
+    for h in range(0, heads, at_once):
+        own = slice(h * rows, (h + at_once) * rows)
+        score = contract(key_all[:count], query_flat[own, :]) * (scale * math.log2(math.e)) + added
+        weight = jnp.exp2(score - jnp.max(score, axis=0, keepdims=True))
         probs = weight * (1.0 / jnp.sum(weight, axis=0, keepdims=True))
-        prob_grad = contract(value_all[...], grad_flat[own, :])
+        prob_grad = contract(value_all[:count], grad_flat[own, :])
         delta = jnp.sum(probs * prob_grad, axis=0, keepdims=True)
-        probs_all[:, own] = probs.astype(jnp.bfloat16)
-        score_all[:, own] = (probs * (prob_grad - delta)).astype(jnp.bfloat16)
-    key_grad = (multiply(score_all[...], query_flat[...]) * scale).astype(jnp.bfloat16)
-    value_grad = multiply(probs_all[...], grad_flat[...]).astype(jnp.bfloat16)
+        probs_all[:count, own] = probs.astype(jnp.bfloat16)
+        score_all[:count, own] = (probs * (prob_grad - delta)).astype(jnp.bfloat16)
+    key_grad = (multiply(score_all[:count], query_flat[...]) * scale).astype(jnp.bfloat16)
+    value_grad = multiply(probs_all[:count], grad_flat[...]).astype(jnp.bfloat16)
     for j in range(planes):
         own = slice(j * rows, (j + 1) * rows)
-        grad_buf[:, j, :, :width] = key_grad[own].reshape(peers, peer, width)
-        grad_buf[:, j, :, width:] = value_grad[own].reshape(peers, peer, width)
+        if j * rows < count:
+            grad_buf[:, j, :, :width] = key_grad[own].reshape(peers, peer, width)
+            grad_buf[:, j, :, width:] = value_grad[own].reshape(peers, peer, width)
+        else:
+            grad_buf[:, j] = jnp.zeros((peers, peer, both), jnp.bfloat16)
     leave = pltpu.make_async_copy(grad_buf, kv_grad, sem)
     leave.start()
-    attended = multiply(value_all[...].T, probs_all[...]).astype(jnp.bfloat16)
-    query_grad = (multiply(key_all[...].T, score_all[...]) * scale).astype(jnp.bfloat16)
+    attended = multiply(value_all[:count].T, probs_all[:count]).astype(jnp.bfloat16)
+    query_grad = (multiply(key_all[:count].T, score_all[:count]) * scale).astype(jnp.bfloat16)
     for k, source in enumerate((attended, query_grad)):
         for h in range(heads):
             turned = source[:, h * rows : (h + 1) * rows].T
@@ -222,7 +239,7 @@
     def swap(x, mask):
         return lax.ppermute(x, "dp", [(i, i ^ mask) for i in range(peers)])
 
-    def in_plane(pieces):
+    def in_plane(pieces, cost=None):
         if not swapped:
             return [lax.all_to_all(pieces[0], "dp", split_axis=0, concat_axis=0, tiled=True)]
         kept, crossed = pieces
@@ -233,6 +250,7 @@
             in_specs=[VMEM] * 2,
             out_specs=[VMEM] * (peers // 2 - 1),
             compiler_params=params(4),
+            cost_estimate=cost,
             name="pair",
         )(kept, crossed)
         return [kept, crossed] + [swap(chip, 2 * s + 2) for s, chip in enumerate(chips)]
@@ -277,7 +295,7 @@
             name="mask",
         )(doc_lengths, slot_row)
     kv = everywhere(kv)
-    pieces = in_plane(pieces)
+    pieces = in_plane(pieces, pl.CostEstimate(flops=10**10, bytes_accessed=0, transcendentals=0))
     if not fine:
         kv = kv.transpose(1, 0, 2, 3).reshape(1, planes, rows, 2 * width)
     count = rows * planes

time: 36.8 us -> 36.2 us (0.984)
  Pallas kernels: 4.4 us -> 3.71 us
    all_to_all x2, waiting for transfers between devices: 0.35 us -> 1.65 us  [everywhere(): lax.all_to_all(x, ('dp', 'ctx'), split_axis=0, concat_axis=0, tiled=True)]
    ppermute x8, waiting for transfers between devices: 12.3 us -> 11.3 us  [swap(): return lax.ppermute(x, 'dp', [(i, i ^ mask) for i in range(peers)])]
    pallas_call x1, Pallas kernels: 1.92 us -> 1.23 us  [local(): pl.pallas_call(functools.partial(core_kernel, heads, len(pieces)), out_sh...]
    all_to_all x2, starting transfers between devices: 11.1 us -> 10.6 us  [everywhere(): lax.all_to_all(x, ('dp', 'ctx'), split_axis=0, concat_axis=0, tiled=True)]
  transfers between devices with their start and end apart: 10 -> 10, of which waited for: 10 -> 9; matrix products, arithmetic and copies ran while one was open for 0% -> 0% of each run, Pallas kernels for 0% -> 0%
where the time goes in v4:
time: 36.2 us; the launch traced here: 35.9 us
  starting transfers between devices  18.6 us (51%)
  waiting for transfers between devices  12.9 us (36%)
  Pallas kernels  3.71 us (10%)
  between operations  0.69 us (2%)
    ppermute x8, waiting for transfers between devices, swap(): return lax.ppermute(x, 'dp', [(i, i ^ mask) for i in range(peers)])  11.3 us
    all_to_all x2, starting transfers between devices, everywhere(): lax.all_to_all(x, ('dp', 'ctx'), split_axis=0, concat_axis=0, tiled=True)  10.6 us
    ppermute x8, starting transfers between devices, swap(): return lax.ppermute(x, 'dp', [(i, i ^ mask) for i in range(peers)])  7.94 us
    all_to_all x2, waiting for transfers between devices, everywhere(): lax.all_to_all(x, ('dp', 'ctx'), split_axis=0, concat_axis=0, tiled=True)  1.65 us
    pallas_call x1, Pallas kernels, local(): pl.pallas_call(pack_kernel, out_shape=sent + [pltpu.VMEM((rows + 8, rows)...  1.57 us
    pallas_call x1, Pallas kernels, local(): pl.pallas_call(functools.partial(core_kernel, heads, len(pieces)), out_sh...  1.23 us
    pallas_call x1, Pallas kernels, local(): pl.pallas_call(last_kernel, out_shape=[low((rows, wide))] * 2 + [low((row...  0.88 us
  transfers between devices with their start and end apart: 10, of which 9 were waited for; matrix products, arithmetic and copies ran while one was open for 0% of the time, Pallas kernels for 0%

profile of v4, /device:TPU:0, one launch (start us, length us, event | category | flops | bytes accessed | tf_op | source)
XLA Modules:
  0.0 35.9 jit_solution(16259396852853667975)
XLA Ops:
  0.6 1.6 %pack.1 = (bf16[4,16,1024]{2,1,0:T(8,128)(2,1)S(1)}, bf16[4,16,1024]{2,1,0:T(8,128)(2,1)S(1)}, f32[136,128]{1,0:T(8,128)S(1)}, bf16[8,4,16,256]{3,2,1,0:T(8,128)(2,1)}) custom-call(bf16[8,16,128]{2,1,0:T(8,128)(2,1)} %bitcast.9, bf16[8,16,128]{2,1,0:T(8,128)(2,1)} %bitcast.10, bf16[128,512]{1,0:T(8,128)(2,1)} %queries.1, bf16[128,512]{1,0:T(8,128)(2,1)} %out_grad.1, ...), custom_call_target="tpu_custom_call" | custom-call | tf_op jit(solution)/shard_map/pack/pallas_call | solution.py:261
  2.2 0.5 %collective-permute-start = (bf16[4,16,1024]{2,1,0:T(8,128)(2,1)S(1)}, bf16[4,16,1024]{2,1,0:T(8,128)(2,1)S(1)}, u32[]{:S(2)}, u32[]{:S(2)}) collective-permute-start(bf16[4,16,1024]{2,1,0:T(8,128)(2,1)S(1)} %get-tuple-element.20), channel_id=1, source_target_pairs={{0,4},{4,0},{8,12},{12,8},{16,20},{20,16},{24,28},{28,24},{1,5},{5... | collective-permute-start | bytes 393224 | tf_op jit(solution)/shard_map/ppermute | solution.py:240
  2.7 7.0 %all-to-all-start = ((bf16[32,16,256]{2,1,0:T(8,128)(2,1)}), bf16[32,16,256]{2,1,0:T(8,128)(2,1)S(1)}, u32[]{:S(2)}, u32[]{:S(2)}) async-start(bf16[32,16,256]{2,1,0:T(8,128)(2,1)} %bitcast.3), calls=%async_computation | async-start | bytes 524288 | tf_op jit(solution)/shard_map/all_to_all | solution.py:236
  9.7 0.0 collective-permute-done.swapped.refs_1_
  9.7 1.8 %collective-permute-start.1 = (bf16[2,16,1024]{2,1,0:T(8,128)(2,1)S(1)}, bf16[2,16,1024]{2,1,0:T(8,128)(2,1)S(1)}, u32[]{:S(2)}, u32[]{:S(2)}) collective-permute-start(bf16[2,16,1024]{2,1,0:T(8,128)(2,1)S(1)} %get-tuple-element.21), channel_id=1, source_target_pairs={{0,8},{4,12},{8,0},{12,4},{16,24},{20,28},{24,16},{28,20},{1,9},{5... | collective-permute-start | bytes 196616 | tf_op jit(solution)/shard_map/ppermute | solution.py:240
  11.6 1.5 %collective-permute-start.2 = (bf16[2,16,1024]{2,1,0:T(8,128)(2,1)S(1)}, bf16[2,16,1024]{2,1,0:T(8,128)(2,1)S(1)}, u32[]{:S(2)}, u32[]{:S(2)}) collective-permute-start(bf16[2,16,1024]{2,1,0:T(8,128)(2,1)S(1)} %get-tuple-element.22), channel_id=1, source_target_pairs={{0,16},{4,20},{8,24},{12,28},{16,0},{20,4},{24,8},{28,12},{1,17},{... | collective-permute-start | bytes 196616 | tf_op jit(solution)/shard_map/ppermute | solution.py:240
  13.0 0.3 collective-permute-start.3
  13.3 2.9 %collective-permute-done.1.refs_2_ = bf16[2,16,1024]{2,1,0:T(8,128)(2,1)S(1)} collective-permute-done((bf16[2,16,1024]{2,1,0:T(8,128)(2,1)S(1)}, bf16[2,16,1024]{2,1,0:T(8,128)(2,1)S(1)}, u32[]{:S(2)}, u32[]{:S(2)}) %collective-permute-start.1) | collective-permute-done | bytes 65568 | tf_op jit(solution)/shard_map/ppermute | solution.py:240
  16.2 2.2 %collective-permute-done.2.refs_3_ = bf16[2,16,1024]{2,1,0:T(8,128)(2,1)S(1)} collective-permute-done((bf16[2,16,1024]{2,1,0:T(8,128)(2,1)S(1)}, bf16[2,16,1024]{2,1,0:T(8,128)(2,1)S(1)}, u32[]{:S(2)}, u32[]{:S(2)}) %collective-permute-start.2) | collective-permute-done | bytes 65568 | tf_op jit(solution)/shard_map/ppermute | solution.py:240
  18.3 0.1 collective-permute-done.3.refs_4_
  18.4 1.5 %all-to-all-done = bf16[32,16,256]{2,1,0:T(8,128)(2,1)S(1)} async-done(((bf16[32,16,256]{2,1,0:T(8,128)(2,1)}), bf16[32,16,256]{2,1,0:T(8,128)(2,1)S(1)}, u32[]{:S(2)}, u32[]{:S(2)}) %all-to-all-start) | async-done | bytes 262176 | tf_op jit(solution)/shard_map/all_to_all | solution.py:236
  19.9 1.2 %core.1 = (bf16[4,16,1024]{2,1,0:T(8,128)(2,1)S(1)}, bf16[4,16,1024]{2,1,0:T(8,128)(2,1)S(1)}, bf16[8,4,16,256]{3,2,1,0:T(8,128)(2,1)}) custom-call(f32[136,128]{1,0:T(8,128)S(1)} %get-tuple-element.17.bias, bf16[8,4,16,256]{3,2,1,0:T(8,128)(2,1)S(1)} %bitcast.7, bf16[4,16,1024]{2,1,0:T(8,128)(2,1)S(1)} %get-tuple-element.19.kept.refs_0_, ...), custom_call_target="tpu_custom_call" | custom-call | tf_op jit(solution)/shard_map/core/pallas_call | solution.py:302
  21.1 3.7 %all-to-all-start.1 = ((bf16[32,16,256]{2,1,0:T(8,128)(2,1)}), bf16[32,16,256]{2,1,0:T(8,128)(2,1)S(1)}, u32[]{:S(2)}, u32[]{:S(2)}) async-start(bf16[32,16,256]{2,1,0:T(8,128)(2,1)} %bitcast.5), calls=%async_computation.1 | async-start | bytes 524288 | tf_op jit(solution)/shard_map/all_to_all | solution.py:236
  24.8 0.3 collective-permute-start.4
  25.1 1.1 %collective-permute-done.4.swapped.refs_1_ = bf16[4,16,1024]{2,1,0:T(8,128)(2,1)S(1)} collective-permute-done((bf16[4,16,1024]{2,1,0:T(8,128)(2,1)S(1)}, bf16[4,16,1024]{2,1,0:T(8,128)(2,1)S(1)}, u32[]{:S(2)}, u32[]{:S(2)}) %collective-permute-start.4) | collective-permute-done | bytes 131104 | tf_op jit(solution)/shard_map/ppermute | solution.py:240
  26.2 1.8 %collective-permute-start.5 = (bf16[2,16,1024]{2,1,0:T(8,128)(2,1)S(1)}, bf16[2,16,1024]{2,1,0:T(8,128)(2,1)S(1)}, u32[]{:S(2)}, u32[]{:S(2)}) collective-permute-start(bf16[2,16,1024]{2,1,0:T(8,128)(2,1)S(1)} %get-tuple-element.27), channel_id=1, source_target_pairs={{0,8},{4,12},{8,0},{12,4},{16,24},{20,28},{24,16},{28,20},{1,9},{5... | collective-permute-start | bytes 196616 | tf_op jit(solution)/shard_map/ppermute | solution.py:240
  28.1 1.5 %collective-permute-start.6 = (bf16[2,16,1024]{2,1,0:T(8,128)(2,1)S(1)}, bf16[2,16,1024]{2,1,0:T(8,128)(2,1)S(1)}, u32[]{:S(2)}, u32[]{:S(2)}) collective-permute-start(bf16[2,16,1024]{2,1,0:T(8,128)(2,1)S(1)} %get-tuple-element.28), channel_id=1, source_target_pairs={{0,16},{4,20},{8,24},{12,28},{16,0},{20,4},{24,8},{28,12},{1,17},{... | collective-permute-start | bytes 196616 | tf_op jit(solution)/shard_map/ppermute | solution.py:240
  29.5 0.3 collective-permute-start.7
  29.8 1.6 %collective-permute-done.5.refs_2_ = bf16[2,16,1024]{2,1,0:T(8,128)(2,1)S(1)} collective-permute-done((bf16[2,16,1024]{2,1,0:T(8,128)(2,1)S(1)}, bf16[2,16,1024]{2,1,0:T(8,128)(2,1)S(1)}, u32[]{:S(2)}, u32[]{:S(2)}) %collective-permute-start.5) | collective-permute-done | bytes 65568 | tf_op jit(solution)/shard_map/ppermute | solution.py:240
  31.4 1.9 %collective-permute-done.6.refs_3_ = bf16[2,16,1024]{2,1,0:T(8,128)(2,1)S(1)} collective-permute-done((bf16[2,16,1024]{2,1,0:T(8,128)(2,1)S(1)}, bf16[2,16,1024]{2,1,0:T(8,128)(2,1)S(1)}, u32[]{:S(2)}, u32[]{:S(2)}) %collective-permute-start.6) | collective-permute-done | bytes 65568 | tf_op jit(solution)/shard_map/ppermute | solution.py:240
  33.3 1.5 %collective-permute-done.7.refs_4_ = bf16[2,16,1024]{2,1,0:T(8,128)(2,1)S(1)} collective-permute-done((bf16[2,16,1024]{2,1,0:T(8,128)(2,1)S(1)}, bf16[2,16,1024]{2,1,0:T(8,128)(2,1)S(1)}, u32[]{:S(2)}, u32[]{:S(2)}) %collective-permute-start.7) | collective-permute-done | bytes 65568 | tf_op jit(solution)/shard_map/ppermute | solution.py:240
  34.8 0.2 all-to-all-done.1
  35.0 0.9 %last.1 = (bf16[128,512]{1,0:T(8,128)(2,1)}, bf16[128,512]{1,0:T(8,128)(2,1)}, bf16[128,128]{1,0:T(8,128)(2,1)}, bf16[128,128]{1,0:T(8,128)(2,1)}) custom-call(bf16[8,4,16,256]{3,2,1,0:T(8,128)(2,1)S(1)} %bitcast.8, bf16[4,16,1024]{2,1,0:T(8,128)(2,1)S(1)} %get-tuple-element.25.kept.refs_0_, bf16[4,16,1024]{2,1,0:T(8,128)(2,1)S(1)} %collective-permute-done.4.swapped.refs_1_, ...), custom_call_target="tpu_custom_call" | custom-call | tf_op jit(solution)/shard_map/last/pallas_call | solution.py:328
  (2 shorter events, 0.0 us)
Async XLA Ops:
  2.2 7.5 %collective-permute-start = (bf16[4,16,1024]{2,1,0:T(8,128)(2,1)S(1)}, bf16[4,16,1024]{2,1,0:T(8,128)(2,1)S(1)}, u32[]{:S(2)}, u32[]{:S(2)}) collective-permute-start(bf16[4,16,1024]{2,1,0:T(8,128)(2,1)S(1)} %get-tuple-element.20), channel_id=1, source_target_pairs={{0,4},{4,0},{8,12},{12,8},{16,20},{20,16},{24,28},{28,24},{1,5},{5... | collective-permute-start | bytes 393224 | tf_op jit(solution)/shard_map/ppermute | solution.py:240
  2.7 17.2 %all-to-all-start = ((bf16[32,16,256]{2,1,0:T(8,128)(2,1)}), bf16[32,16,256]{2,1,0:T(8,128)(2,1)S(1)}, u32[]{:S(2)}, u32[]{:S(2)}) async-start(bf16[32,16,256]{2,1,0:T(8,128)(2,1)} %bitcast.3), calls=%async_computation | async-start | bytes 524288 | tf_op jit(solution)/shard_map/all_to_all | solution.py:236
  9.7 6.4 %collective-permute-start.1 = (bf16[2,16,1024]{2,1,0:T(8,128)(2,1)S(1)}, bf16[2,16,1024]{2,1,0:T(8,128)(2,1)S(1)}, u32[]{:S(2)}, u32[]{:S(2)}) collective-permute-start(bf16[2,16,1024]{2,1,0:T(8,128)(2,1)S(1)} %get-tuple-element.21), channel_id=1, source_target_pairs={{0,8},{4,12},{8,0},{12,4},{16,24},{20,28},{24,16},{28,20},{1,9},{5... | collective-permute-start | bytes 196616 | tf_op jit(solution)/shard_map/ppermute | solution.py:240
  11.6 6.8 %collective-permute-start.2 = (bf16[2,16,1024]{2,1,0:T(8,128)(2,1)S(1)}, bf16[2,16,1024]{2,1,0:T(8,128)(2,1)S(1)}, u32[]{:S(2)}, u32[]{:S(2)}) collective-permute-start(bf16[2,16,1024]{2,1,0:T(8,128)(2,1)S(1)} %get-tuple-element.22), channel_id=1, source_target_pairs={{0,16},{4,20},{8,24},{12,28},{16,0},{20,4},{24,8},{28,12},{1,17},{... | collective-permute-start | bytes 196616 | tf_op jit(solution)/shard_map/ppermute | solution.py:240
  13.0 5.4 %collective-permute-start.3 = (bf16[2,16,1024]{2,1,0:T(8,128)(2,1)S(1)}, bf16[2,16,1024]{2,1,0:T(8,128)(2,1)S(1)}, u32[]{:S(2)}, u32[]{:S(2)}) collective-permute-start(bf16[2,16,1024]{2,1,0:T(8,128)(2,1)S(1)} %get-tuple-element.23), channel_id=1, source_target_pairs={{0,24},{4,28},{8,16},{12,20},{16,8},{20,12},{24,0},{28,4},{1,25},{... | collective-permute-start | bytes 196616 | tf_op jit(solution)/shard_map/ppermute | solution.py:240
  21.1 13.9 %all-to-all-start.1 = ((bf16[32,16,256]{2,1,0:T(8,128)(2,1)}), bf16[32,16,256]{2,1,0:T(8,128)(2,1)S(1)}, u32[]{:S(2)}, u32[]{:S(2)}) async-start(bf16[32,16,256]{2,1,0:T(8,128)(2,1)} %bitcast.5), calls=%async_computation.1 | async-start | bytes 524288 | tf_op jit(solution)/shard_map/all_to_all | solution.py:236
  24.8 1.4 %collective-permute-start.4 = (bf16[4,16,1024]{2,1,0:T(8,128)(2,1)S(1)}, bf16[4,16,1024]{2,1,0:T(8,128)(2,1)S(1)}, u32[]{:S(2)}, u32[]{:S(2)}) collective-permute-start(bf16[4,16,1024]{2,1,0:T(8,128)(2,1)S(1)} %get-tuple-element.26), channel_id=1, source_target_pairs={{0,4},{4,0},{8,12},{12,8},{16,20},{20,16},{24,28},{28,24},{1,5},{5... | collective-permute-start | bytes 393224 | tf_op jit(solution)/shard_map/ppermute | solution.py:240
  26.2 5.2 %collective-permute-start.5 = (bf16[2,16,1024]{2,1,0:T(8,128)(2,1)S(1)}, bf16[2,16,1024]{2,1,0:T(8,128)(2,1)S(1)}, u32[]{:S(2)}, u32[]{:S(2)}) collective-permute-start(bf16[2,16,1024]{2,1,0:T(8,128)(2,1)S(1)} %get-tuple-element.27), channel_id=1, source_target_pairs={{0,8},{4,12},{8,0},{12,4},{16,24},{20,28},{24,16},{28,20},{1,9},{5... | collective-permute-start | bytes 196616 | tf_op jit(solution)/shard_map/ppermute | solution.py:240
  28.1 5.3 %collective-permute-start.6 = (bf16[2,16,1024]{2,1,0:T(8,128)(2,1)S(1)}, bf16[2,16,1024]{2,1,0:T(8,128)(2,1)S(1)}, u32[]{:S(2)}, u32[]{:S(2)}) collective-permute-start(bf16[2,16,1024]{2,1,0:T(8,128)(2,1)S(1)} %get-tuple-element.28), channel_id=1, source_target_pairs={{0,16},{4,20},{8,24},{12,28},{16,0},{20,4},{24,8},{28,12},{1,17},{... | collective-permute-start | bytes 196616 | tf_op jit(solution)/shard_map/ppermute | solution.py:240
  29.5 5.3 %collective-permute-start.7 = (bf16[2,16,1024]{2,1,0:T(8,128)(2,1)S(1)}, bf16[2,16,1024]{2,1,0:T(8,128)(2,1)S(1)}, u32[]{:S(2)}, u32[]{:S(2)}) collective-permute-start(bf16[2,16,1024]{2,1,0:T(8,128)(2,1)S(1)} %get-tuple-element.29), channel_id=1, source_target_pairs={{0,24},{4,28},{8,16},{12,20},{16,8},{20,12},{24,0},{28,4},{1,25},{... | collective-permute-start | bytes 196616 | tf_op jit(solution)/shard_map/ppermute | solution.py:240

commit v5 on v4

--- a/solution.py
+++ b/solution.py
@@ -9,6 +9,8 @@
 from jax.sharding import PartitionSpec as P
 
 HIDDEN = -1e30
+ORDER_IN = (0, 3, 14, 11, 6, 18, 25, 9, 8, 2, 16, 1, 12, 27, 28, 20, 10, 15, 19, 21, 23, 7, 22, 17, 4, 24, 26, 13, 31, 29, 30, 5)
+ORDER_OUT = (0, 3, 14, 11, 6, 18, 25, 9, 8, 2, 10, 1, 12, 27, 28, 20, 16, 19, 15, 21, 23, 7, 22, 17, 4, 24, 26, 13, 31, 29, 30, 5)
 VMEM = pl.BlockSpec(memory_space=pltpu.VMEM)
 SMEM = pl.BlockSpec(memory_space=pltpu.SMEM)
 HBM = pl.BlockSpec(memory_space=pltpu.HBM)
@@ -79,11 +81,11 @@
     bias[rows:, :] = jnp.full((bias.shape[0] - rows, rows), joined)
 
 
-def pack_kernel(keys, values, queries, out_grad, lengths, slot_row, *refs):
-    kept, crossed, bias, kv, kv_buf, query_buf, grad_buf, length_buf, slot_buf, sems = refs
+def pack_kernel(spots, keys, values, queries, out_grad, lengths, slot_row, *refs):
+    kept, crossed, bias, kv, kv_buf, block_buf, query_buf, grad_buf, length_buf, slot_buf, sems = refs
     own = lax.axis_index("dp")
     wide, width = queries.shape[1], keys.shape[2]
-    peers, planes, peer, _ = kv.shape
+    peers, planes, peer = len(spots), len(spots[0]), kv.shape[1]
     come = [
         pltpu.make_async_copy(keys, kv_buf.at[:, :, :width], sems.at[0]),
         pltpu.make_async_copy(values, kv_buf.at[:, :, width:], sems.at[1]),
@@ -96,9 +98,12 @@
         copy.start()
     come[0].wait()
     come[1].wait()
-    leave = [pltpu.make_async_copy(kv_buf, kv.at[:, j], sems.at[6 + j]) for j in range(planes)]
-    for copy in leave:
-        copy.start()
+    for d in range(peers):
+        block = kv_buf[d]
+        for j in range(planes):
+            block_buf[spots[d][j]] = block
+    leave = pltpu.make_async_copy(block_buf, kv, sems.at[6])
+    leave.start()
     come[4].wait()
     come[5].wait()
     fill_bias(peer, True, length_buf, slot_buf, bias)
@@ -107,8 +112,7 @@
         for index, piece in enumerate(parted((kept, crossed))):
             start = pl.multiple_of(lax.bitwise_xor(own, index) * peer, peer)
             piece[:, k * wide : (k + 1) * wide] = buf[pl.ds(start, peer), :]
-    for copy in leave:
-        copy.wait()
+    leave.wait()
 
 
 def pair_kernel(kept, swapped, *out):
@@ -117,23 +121,25 @@
         block[1] = swapped[k + 1]
 
 
-def core_kernel(heads, taken, bias, kv, *refs):
-    planes, plane = kv.shape[1], lax.axis_index("ctx")
+def core_kernel(heads, taken, spots, bias, kv, *refs):
+    planes, plane = len(spots[0][0]), lax.axis_index("ctx")
     if planes > 4:
-        core(heads, taken, None, bias, kv, *refs)
+        core(heads, taken, spots, None, bias, kv, *refs)
         return
     for k in range(planes):
-        pl.when(plane == k)(functools.partial(core, heads, taken, k, bias, kv, *refs))
-
-
-def core(heads, taken, plane, bias, kv, *refs):
+        pl.when(plane == k)(functools.partial(core, heads, taken, spots, k, bias, kv, *refs))
+
+
+def core(heads, taken, spots, plane, bias, kv, *refs):
     pieces = paired(refs[:taken])
     *returned, kv_grad, key_all, value_all, query_flat, grad_flat, probs_all, score_all = refs[
         taken:-2
     ]
     grad_buf, sem = refs[-2:]
     returned = parted(returned)
-    peers, planes, peer, both = kv.shape
+    spots_in, spots_out = spots
+    peers, planes = len(spots_in), len(spots_in[0])
+    _, peer, both = kv.shape
     width = both // 2
     rows = peers * peer
     wide = heads * width
@@ -146,9 +152,10 @@
             added.append(jnp.where(lax.axis_index("ctx") == j, seen, other))
         else:
             added.append(seen if j == plane else jnp.broadcast_to(before, (rows, rows)))
-        block = kv[:, j].reshape(rows, both)
-        key_all[j * rows : (j + 1) * rows, :] = block[:, :width]
-        value_all[j * rows : (j + 1) * rows, :] = block[:, width:]
+        for d in range(peers):
+            at = j * rows + d * peer
+            key_all[at : at + peer, :] = kv[spots_in[d][j], :, :width]
+            value_all[at : at + peer, :] = kv[spots_in[d][j], :, width:]
     count = len(added) * rows
     added = jnp.concatenate(added, axis=0)
     size = pieces[0].shape[0]
@@ -171,12 +178,13 @@
     key_grad = (multiply(score_all[:count], query_flat[...]) * scale).astype(jnp.bfloat16)
     value_grad = multiply(probs_all[:count], grad_flat[...]).astype(jnp.bfloat16)
     for j in range(planes):
-        own = slice(j * rows, (j + 1) * rows)
-        if j * rows < count:
-            grad_buf[:, j, :, :width] = key_grad[own].reshape(peers, peer, width)
-            grad_buf[:, j, :, width:] = value_grad[own].reshape(peers, peer, width)
-        else:
-            grad_buf[:, j] = jnp.zeros((peers, peer, both), jnp.bfloat16)
+        for d in range(peers):
+            if j * rows < count:
+                part = slice(j * rows + d * peer, j * rows + (d + 1) * peer)
+                grad_buf[spots_out[d][j], :, :width] = key_grad[part]
+                grad_buf[spots_out[d][j], :, width:] = value_grad[part]
+            else:
+                grad_buf[spots_out[d][j]] = jnp.zeros((peer, both), jnp.bfloat16)
     leave = pltpu.make_async_copy(grad_buf, kv_grad, sem)
     leave.start()
     attended = multiply(value_all[:count].T, probs_all[:count]).astype(jnp.bfloat16)
@@ -190,7 +198,7 @@
     leave.wait()
 
 
-def last_kernel(kv, *refs):
+def last_kernel(spots, kv, *refs):
     *blocks, attended, query_grad, key_grad, value_grad, key_buf, value_buf, sems = refs
     pieces = paired(blocks)
     wide, size = attended.shape[1], pieces[0].shape[0]
@@ -207,18 +215,26 @@
                 )
             )
             copies[-1].start()
-    peers, planes, peer, both = kv.shape
+    _, peer, both = kv.shape
     width = both // 2
     for k, (buf, target) in enumerate(((key_buf, key_grad), (value_buf, value_grad))):
         part = slice(k * width, (k + 1) * width)
-        total = kv[:, 0, :, part].astype(jnp.float32)
-        for j in range(1, planes):
-            total = total + kv[:, j, :, part].astype(jnp.float32)
-        buf[...] = total.reshape(peers * peer, width).astype(jnp.bfloat16)
+        for d, spot in enumerate(spots):
+            total = kv[spot[0], :, part].astype(jnp.float32)
+            for block in spot[1:]:
+                total = total + kv[block, :, part].astype(jnp.float32)
+            buf[d * peer : (d + 1) * peer, :] = total.astype(jnp.bfloat16)
         copies.append(pltpu.make_async_copy(buf, target, sems.at[len(copies)]))
         copies[-1].start()
     for copy in copies:
         copy.wait()
+
+
+def spots_of(order, peers, planes):
+    if len(order) != peers * planes:
+        order = range(peers * planes)
+    at = {index: spot for spot, index in enumerate(order)}
+    return tuple(tuple(at[d * planes + j] for j in range(planes)) for d in range(peers))
 
 
 def local(queries, keys, values, out_grad, doc_lengths, source_slot):
@@ -229,12 +245,21 @@
     peer = rows // peers
     fine = peer % 16 == 0
     swapped = peers == 8 and fine
-    kv_shape = (peers, planes, peer, 2 * width)
-
-    def everywhere(x):
-        x = x.reshape(peers * planes, peer, 2 * width)
-        x = lax.all_to_all(x, ("dp", "ctx"), split_axis=0, concat_axis=0, tiled=True)
-        return x.reshape(kv_shape)
+    kv_shape = (peers * planes, peer, 2 * width)
+    if fine:
+        spots_in, spots_out = (spots_of(order, peers, planes) for order in (ORDER_IN, ORDER_OUT))
+    else:
+        spots_in = spots_out = (tuple(range(planes)),)
+
+    def everywhere(x, order):
+        groups = [list(order)] if len(order) == peers * planes else None
+        return lax.all_to_all(
+            x, ("dp", "ctx"), split_axis=0, concat_axis=0, tiled=True, axis_index_groups=groups
+        )
+
+    def by_plane(x):
+        x = x.reshape(peers, planes, peer, 2 * width)
+        return x.transpose(1, 0, 2, 3).reshape(planes, rows, 2 * width)
 
     def swap(x, mask):
         return lax.ppermute(x, "dp", [(i, i ^ mask) for i in range(peers)])
@@ -259,17 +284,18 @@
     if swapped:
         sent = [near((peers // 2, peer, 2 * wide))] * 2
         *pieces, bias, kv = pl.pallas_call(
-            pack_kernel,
+            functools.partial(pack_kernel, spots_in),
             out_shape=sent + [pltpu.VMEM((rows + 8, rows), jnp.float32), low(kv_shape)],
             in_specs=[HBM] * 6,
             out_specs=[VMEM] * 3 + [HBM],
             scratch_shapes=[
                 pltpu.VMEM((peers, peer, 2 * width), jnp.bfloat16),
+                pltpu.VMEM(kv_shape, jnp.bfloat16),
                 pltpu.VMEM((rows, wide), jnp.bfloat16),
                 pltpu.VMEM((rows, wide), jnp.bfloat16),
                 pltpu.SMEM(doc_lengths.shape, jnp.int32),
                 pltpu.VMEM(slot_row.shape, jnp.int32),
-                pltpu.SemaphoreType.DMA((6 + planes,)),
+                pltpu.SemaphoreType.DMA((7,)),
             ],
             compiler_params=params(4),
             name="pack",
@@ -284,7 +310,10 @@
     else:
         sent = [low((rows, 2 * wide))]
         kv = jnp.concatenate([keys, values], axis=1).reshape(peers, 1, peer, 2 * width)
-        kv = jnp.broadcast_to(kv, kv_shape)
+        kv = jnp.broadcast_to(kv, (peers, planes, peer, 2 * width)).reshape(kv_shape)
+        if fine:
+            order = ORDER_IN if len(ORDER_IN) == peers * planes else range(peers * planes)
+            kv = kv[jnp.array(order, jnp.int32)]
         pieces = [jnp.concatenate([queries, out_grad], axis=1)]
         bias = pl.pallas_call(
             functools.partial(fill_bias, peer, False),
@@ -294,13 +323,13 @@
             compiler_params=params(4),
             name="mask",
         )(doc_lengths, slot_row)
-    kv = everywhere(kv)
+    kv = everywhere(kv, ORDER_IN)
     pieces = in_plane(pieces, pl.CostEstimate(flops=10**10, bytes_accessed=0, transcendentals=0))
     if not fine:
-        kv = kv.transpose(1, 0, 2, 3).reshape(1, planes, rows, 2 * width)
+        kv = by_plane(kv)
     count = rows * planes
     *pieces, kv = pl.pallas_call(
-        functools.partial(core_kernel, heads, len(pieces)),
+        functools.partial(core_kernel, heads, len(pieces), (spots_in, spots_out)),
         out_shape=sent + [low(kv.shape)],
         in_specs=[VMEM] * (2 + len(pieces)),
         out_specs=[VMEM] * len(sent) + [HBM],
@@ -318,15 +347,15 @@
         name="core",
     )(bias, kv, *pieces)
     if not fine:
-        kv = kv.reshape(planes, peers, peer, 2 * width).transpose(1, 0, 2, 3)
-    kv = everywhere(kv)
+        kv = kv.reshape(planes, peers, peer, 2 * width).transpose(1, 0, 2, 3).reshape(kv_shape)
+    kv = everywhere(kv, ORDER_OUT)
     if not fine:
-        kv = kv.transpose(1, 0, 2, 3).reshape(1, planes, rows, 2 * width)
-    pieces = in_plane(pieces)
+        kv = by_plane(kv)
+    pieces = in_plane(pieces, pl.CostEstimate(flops=10**10, bytes_accessed=0, transcendentals=0))
     count = 8 * 2 if swapped else 2
     return tuple(
         pl.pallas_call(
-            last_kernel,
+            functools.partial(last_kernel, spots_out),
             out_shape=[low((rows, wide))] * 2 + [low((rows, width))] * 2,
             in_specs=[VMEM] * (1 + len(pieces)),
             out_specs=[HBM] * 4,

time: 36.2 us -> 35.4 us (0.978)
  waiting for transfers between devices: 12.9 us -> 12.4 us
  starting transfers between devices: 18.6 us -> 18.2 us
    all_to_all x2, waiting for transfers between devices: 1.65 us -> 1.03 us  [everywhere(): lax.all_to_all(x, ('dp', 'ctx'), split_axis=0, concat_axis=0, tiled=True,...]
  transfers between devices with their start and end apart: 10 -> 10, of which waited for: 9 -> 5; matrix products, arithmetic and copies ran while one was open for 0% -> 0% of each run, Pallas kernels for 0% -> 0%
where the time goes in v5:
time: 35.4 us; the launch traced here: 35.1 us
  starting transfers between devices  18.2 us (51%)
  waiting for transfers between devices  12.4 us (35%)
  Pallas kernels  3.7 us (10%)
  between operations  0.71 us (2%)
    ppermute x8, waiting for transfers between devices, swap(): return lax.ppermute(x, 'dp', [(i, i ^ mask) for i in range(peers)])  11.4 us
    all_to_all x2, starting transfers between devices, everywhere(): lax.all_to_all(x, ('dp', 'ctx'), split_axis=0, concat_axis=0, tiled=True,...  10.5 us
    ppermute x8, starting transfers between devices, swap(): return lax.ppermute(x, 'dp', [(i, i ^ mask) for i in range(peers)])  7.7 us
    pallas_call x1, Pallas kernels, local(): pl.pallas_call(functools.partial(pack_kernel, spots_in), out_shape=sent +...  1.55 us
    pallas_call x1, Pallas kernels, local(): pl.pallas_call(functools.partial(core_kernel, heads, len(pieces), (spots_...  1.23 us
    all_to_all x2, waiting for transfers between devices, everywhere(): lax.all_to_all(x, ('dp', 'ctx'), split_axis=0, concat_axis=0, tiled=True,...  1.03 us
    pallas_call x1, Pallas kernels, local(): pl.pallas_call(functools.partial(last_kernel, spots_out), out_shape=[low(...  0.88 us
  transfers between devices with their start and end apart: 10, of which 5 were waited for; matrix products, arithmetic and copies ran while one was open for 0% of the time, Pallas kernels for 0%

profile of v5, /device:TPU:0, one launch (start us, length us, event | category | flops | bytes accessed | tf_op | source)
XLA Modules:
  0.0 35.1 jit_solution(481265659524229992)
XLA Ops:
  0.6 1.6 %pack.1 = (bf16[4,16,1024]{2,1,0:T(8,128)(2,1)S(1)}, bf16[4,16,1024]{2,1,0:T(8,128)(2,1)S(1)}, f32[136,128]{1,0:T(8,128)S(1)}, bf16[32,16,256]{2,1,0:T(8,128)(2,1)}) custom-call(bf16[8,16,128]{2,1,0:T(8,128)(2,1)} %bitcast.3, bf16[8,16,128]{2,1,0:T(8,128)(2,1)} %bitcast.4, bf16[128,512]{1,0:T(8,128)(2,1)} %queries.1, bf16[128,512]{1,0:T(8,128)(2,1)} %out_grad.1, ...), custom_call_target="tpu_custom_call" | custom-call | tf_op jit(solution)/shard_map/pack/pallas_call | solution.py:286
  2.2 0.5 %collective-permute-start = (bf16[4,16,1024]{2,1,0:T(8,128)(2,1)S(1)}, bf16[4,16,1024]{2,1,0:T(8,128)(2,1)S(1)}, u32[]{:S(2)}, u32[]{:S(2)}) collective-permute-start(bf16[4,16,1024]{2,1,0:T(8,128)(2,1)S(1)} %get-tuple-element.20), channel_id=1, source_target_pairs={{0,4},{4,0},{8,12},{12,8},{16,20},{20,16},{24,28},{28,24},{1,5},{5... | collective-permute-start | bytes 393224 | tf_op jit(solution)/shard_map/ppermute | solution.py:265
  2.7 7.0 %all-to-all-start = ((bf16[32,16,256]{2,1,0:T(8,128)(2,1)}), bf16[32,16,256]{2,1,0:T(8,128)(2,1)S(1)}, u32[]{:S(2)}, u32[]{:S(2)}) async-start(bf16[32,16,256]{2,1,0:T(8,128)(2,1)} %get-tuple-element.18), calls=%async_computation | async-start | bytes 524288 | tf_op jit(solution)/shard_map/all_to_all | solution.py:256
  9.7 0.0 collective-permute-done.swapped.refs_1_
  9.7 1.8 %collective-permute-start.1 = (bf16[2,16,1024]{2,1,0:T(8,128)(2,1)S(1)}, bf16[2,16,1024]{2,1,0:T(8,128)(2,1)S(1)}, u32[]{:S(2)}, u32[]{:S(2)}) collective-permute-start(bf16[2,16,1024]{2,1,0:T(8,128)(2,1)S(1)} %get-tuple-element.21), channel_id=1, source_target_pairs={{0,8},{4,12},{8,0},{12,4},{16,24},{20,28},{24,16},{28,20},{1,9},{5... | collective-permute-start | bytes 196616 | tf_op jit(solution)/shard_map/ppermute | solution.py:265
  11.5 1.5 %collective-permute-start.2 = (bf16[2,16,1024]{2,1,0:T(8,128)(2,1)S(1)}, bf16[2,16,1024]{2,1,0:T(8,128)(2,1)S(1)}, u32[]{:S(2)}, u32[]{:S(2)}) collective-permute-start(bf16[2,16,1024]{2,1,0:T(8,128)(2,1)S(1)} %get-tuple-element.22), channel_id=1, source_target_pairs={{0,16},{4,20},{8,24},{12,28},{16,0},{20,4},{24,8},{28,12},{1,17},{... | collective-permute-start | bytes 196616 | tf_op jit(solution)/shard_map/ppermute | solution.py:265
  13.0 0.3 collective-permute-start.3
  13.3 2.5 %collective-permute-done.1.refs_2_ = bf16[2,16,1024]{2,1,0:T(8,128)(2,1)S(1)} collective-permute-done((bf16[2,16,1024]{2,1,0:T(8,128)(2,1)S(1)}, bf16[2,16,1024]{2,1,0:T(8,128)(2,1)S(1)}, u32[]{:S(2)}, u32[]{:S(2)}) %collective-permute-start.1) | collective-permute-done | bytes 65568 | tf_op jit(solution)/shard_map/ppermute | solution.py:265
  15.8 3.2 %collective-permute-done.2.refs_3_ = bf16[2,16,1024]{2,1,0:T(8,128)(2,1)S(1)} collective-permute-done((bf16[2,16,1024]{2,1,0:T(8,128)(2,1)S(1)}, bf16[2,16,1024]{2,1,0:T(8,128)(2,1)S(1)}, u32[]{:S(2)}, u32[]{:S(2)}) %collective-permute-start.2) | collective-permute-done | bytes 65568 | tf_op jit(solution)/shard_map/ppermute | solution.py:265
  18.9 0.0 collective-permute-done.3.refs_4_
  18.9 1.0 %all-to-all-done.kv = bf16[32,16,256]{2,1,0:T(8,128)(2,1)S(1)} async-done(((bf16[32,16,256]{2,1,0:T(8,128)(2,1)}), bf16[32,16,256]{2,1,0:T(8,128)(2,1)S(1)}, u32[]{:S(2)}, u32[]{:S(2)}) %all-to-all-start) | async-done | bytes 262176 | tf_op jit(solution)/shard_map/all_to_all | solution.py:256
  20.0 1.2 %core.1 = (bf16[4,16,1024]{2,1,0:T(8,128)(2,1)S(1)}, bf16[4,16,1024]{2,1,0:T(8,128)(2,1)S(1)}, bf16[32,16,256]{2,1,0:T(8,128)(2,1)}) custom-call(f32[136,128]{1,0:T(8,128)S(1)} %get-tuple-element.17.bias, bf16[32,16,256]{2,1,0:T(8,128)(2,1)S(1)} %all-to-all-done.kv, bf16[4,16,1024]{2,1,0:T(8,128)(2,1)S(1)} %get-tuple-element.19.kept.refs_0_, ...), custom_call_target="tpu_custom_call" | custom-call | tf_op jit(solution)/shard_map/core/pallas_call | solution.py:331
  21.2 0.1 collective-permute-start.4
  21.3 3.6 %all-to-all-start.1 = ((bf16[32,16,256]{2,1,0:T(8,128)(2,1)}), bf16[32,16,256]{2,1,0:T(8,128)(2,1)S(1)}, u32[]{:S(2)}, u32[]{:S(2)}) async-start(bf16[32,16,256]{2,1,0:T(8,128)(2,1)} %get-tuple-element.24), calls=%async_computation.1 | async-start | bytes 524288 | tf_op jit(solution)/shard_map/all_to_all | solution.py:256
  24.9 0.0 collective-permute-done.4.swapped.refs_1_
  24.9 1.8 %collective-permute-start.5 = (bf16[2,16,1024]{2,1,0:T(8,128)(2,1)S(1)}, bf16[2,16,1024]{2,1,0:T(8,128)(2,1)S(1)}, u32[]{:S(2)}, u32[]{:S(2)}) collective-permute-start(bf16[2,16,1024]{2,1,0:T(8,128)(2,1)S(1)} %get-tuple-element.27), channel_id=1, source_target_pairs={{0,8},{4,12},{8,0},{12,4},{16,24},{20,28},{24,16},{28,20},{1,9},{5... | collective-permute-start | bytes 196616 | tf_op jit(solution)/shard_map/ppermute | solution.py:265
  26.7 1.5 %collective-permute-start.6 = (bf16[2,16,1024]{2,1,0:T(8,128)(2,1)S(1)}, bf16[2,16,1024]{2,1,0:T(8,128)(2,1)S(1)}, u32[]{:S(2)}, u32[]{:S(2)}) collective-permute-start(bf16[2,16,1024]{2,1,0:T(8,128)(2,1)S(1)} %get-tuple-element.28), channel_id=1, source_target_pairs={{0,16},{4,20},{8,24},{12,28},{16,0},{20,4},{24,8},{28,12},{1,17},{... | collective-permute-start | bytes 196616 | tf_op jit(solution)/shard_map/ppermute | solution.py:265
  28.2 0.3 collective-permute-start.7
  28.5 3.1 %collective-permute-done.5.refs_2_ = bf16[2,16,1024]{2,1,0:T(8,128)(2,1)S(1)} collective-permute-done((bf16[2,16,1024]{2,1,0:T(8,128)(2,1)S(1)}, bf16[2,16,1024]{2,1,0:T(8,128)(2,1)S(1)}, u32[]{:S(2)}, u32[]{:S(2)}) %collective-permute-start.5) | collective-permute-done | bytes 65568 | tf_op jit(solution)/shard_map/ppermute | solution.py:265
  31.6 2.6 %collective-permute-done.6.refs_3_ = bf16[2,16,1024]{2,1,0:T(8,128)(2,1)S(1)} collective-permute-done((bf16[2,16,1024]{2,1,0:T(8,128)(2,1)S(1)}, bf16[2,16,1024]{2,1,0:T(8,128)(2,1)S(1)}, u32[]{:S(2)}, u32[]{:S(2)}) %collective-permute-start.6) | collective-permute-done | bytes 65568 | tf_op jit(solution)/shard_map/ppermute | solution.py:265
  34.2 0.0 collective-permute-done.7.refs_4_
  34.2 0.0 all-to-all-done.1.kv
  34.2 0.9 %last.1 = (bf16[128,512]{1,0:T(8,128)(2,1)}, bf16[128,512]{1,0:T(8,128)(2,1)}, bf16[128,128]{1,0:T(8,128)(2,1)}, bf16[128,128]{1,0:T(8,128)(2,1)}) custom-call(bf16[32,16,256]{2,1,0:T(8,128)(2,1)S(1)} %all-to-all-done.1.kv, bf16[4,16,1024]{2,1,0:T(8,128)(2,1)S(1)} %get-tuple-element.25.kept.refs_0_, ...), custom_call_target="tpu_custom_call" | custom-call | tf_op jit(solution)/shard_map/last/pallas_call | solution.py:357
  (2 shorter events, 0.0 us)
Async XLA Ops:
  2.2 7.5 %collective-permute-start = (bf16[4,16,1024]{2,1,0:T(8,128)(2,1)S(1)}, bf16[4,16,1024]{2,1,0:T(8,128)(2,1)S(1)}, u32[]{:S(2)}, u32[]{:S(2)}) collective-permute-start(bf16[4,16,1024]{2,1,0:T(8,128)(2,1)S(1)} %get-tuple-element.20), channel_id=1, source_target_pairs={{0,4},{4,0},{8,12},{12,8},{16,20},{20,16},{24,28},{28,24},{1,5},{5... | collective-permute-start | bytes 393224 | tf_op jit(solution)/shard_map/ppermute | solution.py:265
  2.7 17.3 %all-to-all-start = ((bf16[32,16,256]{2,1,0:T(8,128)(2,1)}), bf16[32,16,256]{2,1,0:T(8,128)(2,1)S(1)}, u32[]{:S(2)}, u32[]{:S(2)}) async-start(bf16[32,16,256]{2,1,0:T(8,128)(2,1)} %get-tuple-element.18), calls=%async_computation | async-start | bytes 524288 | tf_op jit(solution)/shard_map/all_to_all | solution.py:256
  9.7 6.0 %collective-permute-start.1 = (bf16[2,16,1024]{2,1,0:T(8,128)(2,1)S(1)}, bf16[2,16,1024]{2,1,0:T(8,128)(2,1)S(1)}, u32[]{:S(2)}, u32[]{:S(2)}) collective-permute-start(bf16[2,16,1024]{2,1,0:T(8,128)(2,1)S(1)} %get-tuple-element.21), channel_id=1, source_target_pairs={{0,8},{4,12},{8,0},{12,4},{16,24},{20,28},{24,16},{28,20},{1,9},{5... | collective-permute-start | bytes 196616 | tf_op jit(solution)/shard_map/ppermute | solution.py:265
  11.5 7.4 %collective-permute-start.2 = (bf16[2,16,1024]{2,1,0:T(8,128)(2,1)S(1)}, bf16[2,16,1024]{2,1,0:T(8,128)(2,1)S(1)}, u32[]{:S(2)}, u32[]{:S(2)}) collective-permute-start(bf16[2,16,1024]{2,1,0:T(8,128)(2,1)S(1)} %get-tuple-element.22), channel_id=1, source_target_pairs={{0,16},{4,20},{8,24},{12,28},{16,0},{20,4},{24,8},{28,12},{1,17},{... | collective-permute-start | bytes 196616 | tf_op jit(solution)/shard_map/ppermute | solution.py:265
  13.0 5.9 %collective-permute-start.3 = (bf16[2,16,1024]{2,1,0:T(8,128)(2,1)S(1)}, bf16[2,16,1024]{2,1,0:T(8,128)(2,1)S(1)}, u32[]{:S(2)}, u32[]{:S(2)}) collective-permute-start(bf16[2,16,1024]{2,1,0:T(8,128)(2,1)S(1)} %get-tuple-element.23), channel_id=1, source_target_pairs={{0,24},{4,28},{8,16},{12,20},{16,8},{20,12},{24,0},{28,4},{1,25},{... | collective-permute-start | bytes 196616 | tf_op jit(solution)/shard_map/ppermute | solution.py:265
  21.2 3.7 %collective-permute-start.4 = (bf16[4,16,1024]{2,1,0:T(8,128)(2,1)S(1)}, bf16[4,16,1024]{2,1,0:T(8,128)(2,1)S(1)}, u32[]{:S(2)}, u32[]{:S(2)}) collective-permute-start(bf16[4,16,1024]{2,1,0:T(8,128)(2,1)S(1)} %get-tuple-element.26), channel_id=1, source_target_pairs={{0,4},{4,0},{8,12},{12,8},{16,20},{20,16},{24,28},{28,24},{1,5},{5... | collective-permute-start | bytes 393224 | tf_op jit(solution)/shard_map/ppermute | solution.py:265
  21.3 12.9 %all-to-all-start.1 = ((bf16[32,16,256]{2,1,0:T(8,128)(2,1)}), bf16[32,16,256]{2,1,0:T(8,128)(2,1)S(1)}, u32[]{:S(2)}, u32[]{:S(2)}) async-start(bf16[32,16,256]{2,1,0:T(8,128)(2,1)} %get-tuple-element.24), calls=%async_computation.1 | async-start | bytes 524288 | tf_op jit(solution)/shard_map/all_to_all | solution.py:256
  24.9 6.7 %collective-permute-start.5 = (bf16[2,16,1024]{2,1,0:T(8,128)(2,1)S(1)}, bf16[2,16,1024]{2,1,0:T(8,128)(2,1)S(1)}, u32[]{:S(2)}, u32[]{:S(2)}) collective-permute-start(bf16[2,16,1024]{2,1,0:T(8,128)(2,1)S(1)} %get-tuple-element.27), channel_id=1, source_target_pairs={{0,8},{4,12},{8,0},{12,4},{16,24},{20,28},{24,16},{28,20},{1,9},{5... | collective-permute-start | bytes 196616 | tf_op jit(solution)/shard_map/ppermute | solution.py:265
  26.7 7.4 %collective-permute-start.6 = (bf16[2,16,1024]{2,1,0:T(8,128)(2,1)S(1)}, bf16[2,16,1024]{2,1,0:T(8,128)(2,1)S(1)}, u32[]{:S(2)}, u32[]{:S(2)}) collective-permute-start(bf16[2,16,1024]{2,1,0:T(8,128)(2,1)S(1)} %get-tuple-element.28), channel_id=1, source_target_pairs={{0,16},{4,20},{8,24},{12,28},{16,0},{20,4},{24,8},{28,12},{1,17},{... | collective-permute-start | bytes 196616 | tf_op jit(solution)/shard_map/ppermute | solution.py:265
  28.2 6.0 %collective-permute-start.7 = (bf16[2,16,1024]{2,1,0:T(8,128)(2,1)S(1)}, bf16[2,16,1024]{2,1,0:T(8,128)(2,1)S(1)}, u32[]{:S(2)}, u32[]{:S(2)}) collective-permute-start(bf16[2,16,1024]{2,1,0:T(8,128)(2,1)S(1)} %get-tuple-element.29), channel_id=1, source_target_pairs={{0,24},{4,28},{8,16},{12,20},{16,8},{20,12},{24,0},{28,4},{1,25},{... | collective-permute-start | bytes 196616 | tf_op jit(solution)/shard_map/ppermute | solution.py:265

commit v6 on v5

--- a/solution.py
+++ b/solution.py
@@ -11,6 +11,8 @@
 HIDDEN = -1e30
 ORDER_IN = (0, 3, 14, 11, 6, 18, 25, 9, 8, 2, 16, 1, 12, 27, 28, 20, 10, 15, 19, 21, 23, 7, 22, 17, 4, 24, 26, 13, 31, 29, 30, 5)
 ORDER_OUT = (0, 3, 14, 11, 6, 18, 25, 9, 8, 2, 10, 1, 12, 27, 28, 20, 16, 19, 15, 21, 23, 7, 22, 17, 4, 24, 26, 13, 31, 29, 30, 5)
+CHIPS = (0, 3, 2, 1)
+MASKS = tuple(2 * chip + core for chip in CHIPS for core in range(2))
 VMEM = pl.BlockSpec(memory_space=pltpu.VMEM)
 SMEM = pl.BlockSpec(memory_space=pltpu.SMEM)
 HBM = pl.BlockSpec(memory_space=pltpu.HBM)
@@ -64,7 +66,13 @@
     down = lax.broadcasted_iota(jnp.int32, (rows, rows), 0)
     key_pos = jnp.sum(jnp.where(slot == down, along, 0), axis=1, keepdims=True)
     slot_down = slot.astype(jnp.float32).T.astype(jnp.int32)
-    wanted = lax.bitwise_xor(along // peer, own) * peer + along % peer if swapped else along
+    if swapped:
+        mask = jnp.zeros_like(along)
+        for index, value in enumerate(MASKS):
+            mask = jnp.where(along // peer == index, value, mask)
+        wanted = lax.bitwise_xor(mask, own) * peer + along % peer
+    else:
+        wanted = along
     query_pos = jnp.sum(jnp.where(slot_down == wanted, down, 0), axis=0, keepdims=True)
 
     def later(k, carry):
@@ -110,7 +118,7 @@
     for k, buf in enumerate((query_buf, grad_buf)):
         come[2 + k].wait()
         for index, piece in enumerate(parted((kept, crossed))):
-            start = pl.multiple_of(lax.bitwise_xor(own, index) * peer, peer)
+            start = pl.multiple_of(lax.bitwise_xor(own, MASKS[index]) * peer, peer)
             piece[:, k * wide : (k + 1) * wide] = buf[pl.ds(start, peer), :]
     leave.wait()
 
@@ -202,10 +210,10 @@
     *blocks, attended, query_grad, key_grad, value_grad, key_buf, value_buf, sems = refs
     pieces = paired(blocks)
     wide, size = attended.shape[1], pieces[0].shape[0]
-    own = lax.axis_index("dp") if len(pieces) > 1 else 0
+    own = lax.axis_index("dp") if len(pieces) > 1 else None
     copies = []
     for index, piece in enumerate(pieces):
-        start = pl.multiple_of(lax.bitwise_xor(own, index) * size, size)
+        start = pl.multiple_of(lax.bitwise_xor(own, MASKS[index]) * size, size) if own is not None else 0
         for k, target in enumerate((attended, query_grad)):
             copies.append(
                 pltpu.make_async_copy(
@@ -231,9 +239,7 @@
 
 
 def spots_of(order, peers, planes):
-    if len(order) != peers * planes:
-        order = range(peers * planes)
-    at = {index: spot for spot, index in enumerate(order)}
+    at = {index: spot for spot, index in enumerate(order or range(peers * planes))}
     return tuple(tuple(at[d * planes + j] for j in range(planes)) for d in range(peers))
 
 
@@ -246,13 +252,15 @@
     fine = peer % 16 == 0
     swapped = peers == 8 and fine
     kv_shape = (peers * planes, peer, 2 * width)
+    measured = swapped and planes == 4
+    order_in, order_out = (ORDER_IN, ORDER_OUT) if measured else (None, None)
     if fine:
-        spots_in, spots_out = (spots_of(order, peers, planes) for order in (ORDER_IN, ORDER_OUT))
+        spots_in, spots_out = (spots_of(order, peers, planes) for order in (order_in, order_out))
     else:
         spots_in = spots_out = (tuple(range(planes)),)
 
     def everywhere(x, order):
-        groups = [list(order)] if len(order) == peers * planes else None
+        groups = [list(order)] if order else None
         return lax.all_to_all(
             x, ("dp", "ctx"), split_axis=0, concat_axis=0, tiled=True, axis_index_groups=groups
         )
@@ -278,7 +286,7 @@
             cost_estimate=cost,
             name="pair",
         )(kept, crossed)
-        return [kept, crossed] + [swap(chip, 2 * s + 2) for s, chip in enumerate(chips)]
+        return [kept, crossed] + [swap(chip, 2 * mask) for chip, mask in zip(chips, CHIPS[1:])]
 
     slot_row = source_slot.reshape(1, rows)
     if swapped:
@@ -311,9 +319,6 @@
         sent = [low((rows, 2 * wide))]
         kv = jnp.concatenate([keys, values], axis=1).reshape(peers, 1, peer, 2 * width)
         kv = jnp.broadcast_to(kv, (peers, planes, peer, 2 * width)).reshape(kv_shape)
-        if fine:
-            order = ORDER_IN if len(ORDER_IN) == peers * planes else range(peers * planes)
-            kv = kv[jnp.array(order, jnp.int32)]
         pieces = [jnp.concatenate([queries, out_grad], axis=1)]
         bias = pl.pallas_call(
             functools.partial(fill_bias, peer, False),
@@ -323,7 +328,7 @@
             compiler_params=params(4),
             name="mask",
         )(doc_lengths, slot_row)
-    kv = everywhere(kv, ORDER_IN)
+    kv = everywhere(kv, order_in)
     pieces = in_plane(pieces, pl.CostEstimate(flops=10**10, bytes_accessed=0, transcendentals=0))
     if not fine:
         kv = by_plane(kv)
@@ -348,7 +353,7 @@
     )(bias, kv, *pieces)
     if not fine:
         kv = kv.reshape(planes, peers, peer, 2 * width).transpose(1, 0, 2, 3).reshape(kv_shape)
-    kv = everywhere(kv, ORDER_OUT)
+    kv = everywhere(kv, order_out)
     if not fine:
         kv = by_plane(kv)
     pieces = in_plane(pieces, pl.CostEstimate(flops=10**10, bytes_accessed=0, transcendentals=0))

time: 35.4 us -> 35.3 us (level)
  no operation moved by 1% of the time
where the time goes in v6:
time: 35.3 us; the launch traced here: 35 us
  starting transfers between devices  18.2 us (52%)
  waiting for transfers between devices  12.3 us (35%)
  Pallas kernels  3.7 us (10%)
  between operations  0.71 us (2%)
    ppermute x8, waiting for transfers between devices, swap(): return lax.ppermute(x, 'dp', [(i, i ^ mask) for i in range(peers)])  11.2 us
    all_to_all x2, starting transfers between devices, everywhere(): lax.all_to_all(x, ('dp', 'ctx'), split_axis=0, concat_axis=0, tiled=True,...  10.5 us
    ppermute x8, starting transfers between devices, swap(): return lax.ppermute(x, 'dp', [(i, i ^ mask) for i in range(peers)])  7.7 us
    pallas_call x1, Pallas kernels, local(): pl.pallas_call(functools.partial(pack_kernel, spots_in), out_shape=sent +...  1.55 us
    pallas_call x1, Pallas kernels, local(): pl.pallas_call(functools.partial(core_kernel, heads, len(pieces), (spots_...  1.23 us
    all_to_all x2, waiting for transfers between devices, everywhere(): lax.all_to_all(x, ('dp', 'ctx'), split_axis=0, concat_axis=0, tiled=True,...  1.14 us
    pallas_call x1, Pallas kernels, local(): pl.pallas_call(functools.partial(last_kernel, spots_out), out_shape=[low(...  0.88 us
  transfers between devices with their start and end apart: 10, of which 5 were waited for; matrix products, arithmetic and copies ran while one was open for 0% of the time, Pallas kernels for 0%

profile of v6, /device:TPU:0, one launch (start us, length us, event | category | flops | bytes accessed | tf_op | source)
XLA Modules:
  0.0 35.0 jit_solution(13336158569303411124)
XLA Ops:
  0.6 1.6 %pack.1 = (bf16[4,16,1024]{2,1,0:T(8,128)(2,1)S(1)}, bf16[4,16,1024]{2,1,0:T(8,128)(2,1)S(1)}, f32[136,128]{1,0:T(8,128)S(1)}, bf16[32,16,256]{2,1,0:T(8,128)(2,1)}) custom-call(bf16[8,16,128]{2,1,0:T(8,128)(2,1)} %bitcast.3, bf16[8,16,128]{2,1,0:T(8,128)(2,1)} %bitcast.4, bf16[128,512]{1,0:T(8,128)(2,1)} %queries.1, bf16[128,512]{1,0:T(8,128)(2,1)} %out_grad.1, ...), custom_call_target="tpu_custom_call" | custom-call | tf_op jit(solution)/shard_map/pack/pallas_call | solution.py:294
  2.2 0.5 %collective-permute-start = (bf16[4,16,1024]{2,1,0:T(8,128)(2,1)S(1)}, bf16[4,16,1024]{2,1,0:T(8,128)(2,1)S(1)}, u32[]{:S(2)}, u32[]{:S(2)}) collective-permute-start(bf16[4,16,1024]{2,1,0:T(8,128)(2,1)S(1)} %get-tuple-element.20), channel_id=1, source_target_pairs={{0,4},{4,0},{8,12},{12,8},{16,20},{20,16},{24,28},{28,24},{1,5},{5... | collective-permute-start | bytes 393224 | tf_op jit(solution)/shard_map/ppermute | solution.py:273
  2.7 7.0 %all-to-all-start = ((bf16[32,16,256]{2,1,0:T(8,128)(2,1)}), bf16[32,16,256]{2,1,0:T(8,128)(2,1)S(1)}, u32[]{:S(2)}, u32[]{:S(2)}) async-start(bf16[32,16,256]{2,1,0:T(8,128)(2,1)} %get-tuple-element.18), calls=%async_computation | async-start | bytes 524288 | tf_op jit(solution)/shard_map/all_to_all | solution.py:264
  9.7 0.0 collective-permute-done.swapped.refs_1_
  9.7 2.7 %collective-permute-start.1 = (bf16[2,16,1024]{2,1,0:T(8,128)(2,1)S(1)}, bf16[2,16,1024]{2,1,0:T(8,128)(2,1)S(1)}, u32[]{:S(2)}, u32[]{:S(2)}) collective-permute-start(bf16[2,16,1024]{2,1,0:T(8,128)(2,1)S(1)} %get-tuple-element.21), channel_id=1, source_target_pairs={{0,24},{4,28},{8,16},{12,20},{16,8},{20,12},{24,0},{28,4},{1,25},{... | collective-permute-start | bytes 196616 | tf_op jit(solution)/shard_map/ppermute | solution.py:273
  12.4 0.6 %collective-permute-start.2 = (bf16[2,16,1024]{2,1,0:T(8,128)(2,1)S(1)}, bf16[2,16,1024]{2,1,0:T(8,128)(2,1)S(1)}, u32[]{:S(2)}, u32[]{:S(2)}) collective-permute-start(bf16[2,16,1024]{2,1,0:T(8,128)(2,1)S(1)} %get-tuple-element.22), channel_id=1, source_target_pairs={{0,16},{4,20},{8,24},{12,28},{16,0},{20,4},{24,8},{28,12},{1,17},{... | collective-permute-start | bytes 196616 | tf_op jit(solution)/shard_map/ppermute | solution.py:273
  13.0 0.3 collective-permute-start.3
  13.3 4.2 %collective-permute-done.1.refs_2_ = bf16[2,16,1024]{2,1,0:T(8,128)(2,1)S(1)} collective-permute-done((bf16[2,16,1024]{2,1,0:T(8,128)(2,1)S(1)}, bf16[2,16,1024]{2,1,0:T(8,128)(2,1)S(1)}, u32[]{:S(2)}, u32[]{:S(2)}) %collective-permute-start.1) | collective-permute-done | bytes 65568 | tf_op jit(solution)/shard_map/ppermute | solution.py:273
  17.5 1.4 %collective-permute-done.2.refs_3_ = bf16[2,16,1024]{2,1,0:T(8,128)(2,1)S(1)} collective-permute-done((bf16[2,16,1024]{2,1,0:T(8,128)(2,1)S(1)}, bf16[2,16,1024]{2,1,0:T(8,128)(2,1)S(1)}, u32[]{:S(2)}, u32[]{:S(2)}) %collective-permute-start.2) | collective-permute-done | bytes 65568 | tf_op jit(solution)/shard_map/ppermute | solution.py:273
  18.8 0.0 collective-permute-done.3.refs_4_
  18.8 1.1 %all-to-all-done.kv = bf16[32,16,256]{2,1,0:T(8,128)(2,1)S(1)} async-done(((bf16[32,16,256]{2,1,0:T(8,128)(2,1)}), bf16[32,16,256]{2,1,0:T(8,128)(2,1)S(1)}, u32[]{:S(2)}, u32[]{:S(2)}) %all-to-all-start) | async-done | bytes 262176 | tf_op jit(solution)/shard_map/all_to_all | solution.py:264
  20.0 1.2 %core.1 = (bf16[4,16,1024]{2,1,0:T(8,128)(2,1)S(1)}, bf16[4,16,1024]{2,1,0:T(8,128)(2,1)S(1)}, bf16[32,16,256]{2,1,0:T(8,128)(2,1)}) custom-call(f32[136,128]{1,0:T(8,128)S(1)} %get-tuple-element.17.bias, bf16[32,16,256]{2,1,0:T(8,128)(2,1)S(1)} %all-to-all-done.kv, bf16[4,16,1024]{2,1,0:T(8,128)(2,1)S(1)} %get-tuple-element.19.kept.refs_0_, ...), custom_call_target="tpu_custom_call" | custom-call | tf_op jit(solution)/shard_map/core/pallas_call | solution.py:336
  21.2 0.1 collective-permute-start.4
  21.3 3.6 %all-to-all-start.1 = ((bf16[32,16,256]{2,1,0:T(8,128)(2,1)}), bf16[32,16,256]{2,1,0:T(8,128)(2,1)S(1)}, u32[]{:S(2)}, u32[]{:S(2)}) async-start(bf16[32,16,256]{2,1,0:T(8,128)(2,1)} %get-tuple-element.24), calls=%async_computation.1 | async-start | bytes 524288 | tf_op jit(solution)/shard_map/all_to_all | solution.py:264
  24.9 0.0 collective-permute-done.4.swapped.refs_1_
  24.9 2.7 %collective-permute-start.5 = (bf16[2,16,1024]{2,1,0:T(8,128)(2,1)S(1)}, bf16[2,16,1024]{2,1,0:T(8,128)(2,1)S(1)}, u32[]{:S(2)}, u32[]{:S(2)}) collective-permute-start(bf16[2,16,1024]{2,1,0:T(8,128)(2,1)S(1)} %get-tuple-element.27), channel_id=1, source_target_pairs={{0,24},{4,28},{8,16},{12,20},{16,8},{20,12},{24,0},{28,4},{1,25},{... | collective-permute-start | bytes 196616 | tf_op jit(solution)/shard_map/ppermute | solution.py:273
  27.6 0.6 %collective-permute-start.6 = (bf16[2,16,1024]{2,1,0:T(8,128)(2,1)S(1)}, bf16[2,16,1024]{2,1,0:T(8,128)(2,1)S(1)}, u32[]{:S(2)}, u32[]{:S(2)}) collective-permute-start(bf16[2,16,1024]{2,1,0:T(8,128)(2,1)S(1)} %get-tuple-element.28), channel_id=1, source_target_pairs={{0,16},{4,20},{8,24},{12,28},{16,0},{20,4},{24,8},{28,12},{1,17},{... | collective-permute-start | bytes 196616 | tf_op jit(solution)/shard_map/ppermute | solution.py:273
  28.2 0.3 collective-permute-start.7
  28.5 3.9 %collective-permute-done.5.refs_2_ = bf16[2,16,1024]{2,1,0:T(8,128)(2,1)S(1)} collective-permute-done((bf16[2,16,1024]{2,1,0:T(8,128)(2,1)S(1)}, bf16[2,16,1024]{2,1,0:T(8,128)(2,1)S(1)}, u32[]{:S(2)}, u32[]{:S(2)}) %collective-permute-start.5) | collective-permute-done | bytes 65568 | tf_op jit(solution)/shard_map/ppermute | solution.py:273
  32.3 1.7 %collective-permute-done.6.refs_3_ = bf16[2,16,1024]{2,1,0:T(8,128)(2,1)S(1)} collective-permute-done((bf16[2,16,1024]{2,1,0:T(8,128)(2,1)S(1)}, bf16[2,16,1024]{2,1,0:T(8,128)(2,1)S(1)}, u32[]{:S(2)}, u32[]{:S(2)}) %collective-permute-start.6) | collective-permute-done | bytes 65568 | tf_op jit(solution)/shard_map/ppermute | solution.py:273
  34.1 0.0 collective-permute-done.7.refs_4_
  34.1 0.0 all-to-all-done.1.kv
  34.1 0.9 %last.1 = (bf16[128,512]{1,0:T(8,128)(2,1)}, bf16[128,512]{1,0:T(8,128)(2,1)}, bf16[128,128]{1,0:T(8,128)(2,1)}, bf16[128,128]{1,0:T(8,128)(2,1)}) custom-call(bf16[32,16,256]{2,1,0:T(8,128)(2,1)S(1)} %all-to-all-done.1.kv, bf16[4,16,1024]{2,1,0:T(8,128)(2,1)S(1)} %get-tuple-element.25.kept.refs_0_, ...), custom_call_target="tpu_custom_call" | custom-call | tf_op jit(solution)/shard_map/last/pallas_call | solution.py:362
  (2 shorter events, 0.0 us)
Async XLA Ops:
  2.2 7.5 %collective-permute-start = (bf16[4,16,1024]{2,1,0:T(8,128)(2,1)S(1)}, bf16[4,16,1024]{2,1,0:T(8,128)(2,1)S(1)}, u32[]{:S(2)}, u32[]{:S(2)}) collective-permute-start(bf16[4,16,1024]{2,1,0:T(8,128)(2,1)S(1)} %get-tuple-element.20), channel_id=1, source_target_pairs={{0,4},{4,0},{8,12},{12,8},{16,20},{20,16},{24,28},{28,24},{1,5},{5... | collective-permute-start | bytes 393224 | tf_op jit(solution)/shard_map/ppermute | solution.py:273
  2.7 17.3 %all-to-all-start = ((bf16[32,16,256]{2,1,0:T(8,128)(2,1)}), bf16[32,16,256]{2,1,0:T(8,128)(2,1)S(1)}, u32[]{:S(2)}, u32[]{:S(2)}) async-start(bf16[32,16,256]{2,1,0:T(8,128)(2,1)} %get-tuple-element.18), calls=%async_computation | async-start | bytes 524288 | tf_op jit(solution)/shard_map/all_to_all | solution.py:264
  9.7 7.7 %collective-permute-start.1 = (bf16[2,16,1024]{2,1,0:T(8,128)(2,1)S(1)}, bf16[2,16,1024]{2,1,0:T(8,128)(2,1)S(1)}, u32[]{:S(2)}, u32[]{:S(2)}) collective-permute-start(bf16[2,16,1024]{2,1,0:T(8,128)(2,1)S(1)} %get-tuple-element.21), channel_id=1, source_target_pairs={{0,24},{4,28},{8,16},{12,20},{16,8},{20,12},{24,0},{28,4},{1,25},{... | collective-permute-start | bytes 196616 | tf_op jit(solution)/shard_map/ppermute | solution.py:273
  12.4 6.4 %collective-permute-start.2 = (bf16[2,16,1024]{2,1,0:T(8,128)(2,1)S(1)}, bf16[2,16,1024]{2,1,0:T(8,128)(2,1)S(1)}, u32[]{:S(2)}, u32[]{:S(2)}) collective-permute-start(bf16[2,16,1024]{2,1,0:T(8,128)(2,1)S(1)} %get-tuple-element.22), channel_id=1, source_target_pairs={{0,16},{4,20},{8,24},{12,28},{16,0},{20,4},{24,8},{28,12},{1,17},{... | collective-permute-start | bytes 196616 | tf_op jit(solution)/shard_map/ppermute | solution.py:273
  13.0 5.8 %collective-permute-start.3 = (bf16[2,16,1024]{2,1,0:T(8,128)(2,1)S(1)}, bf16[2,16,1024]{2,1,0:T(8,128)(2,1)S(1)}, u32[]{:S(2)}, u32[]{:S(2)}) collective-permute-start(bf16[2,16,1024]{2,1,0:T(8,128)(2,1)S(1)} %get-tuple-element.23), channel_id=1, source_target_pairs={{0,8},{4,12},{8,0},{12,4},{16,24},{20,28},{24,16},{28,20},{1,9},{5... | collective-permute-start | bytes 196616 | tf_op jit(solution)/shard_map/ppermute | solution.py:273
  21.2 3.7 %collective-permute-start.4 = (bf16[4,16,1024]{2,1,0:T(8,128)(2,1)S(1)}, bf16[4,16,1024]{2,1,0:T(8,128)(2,1)S(1)}, u32[]{:S(2)}, u32[]{:S(2)}) collective-permute-start(bf16[4,16,1024]{2,1,0:T(8,128)(2,1)S(1)} %get-tuple-element.26), channel_id=1, source_target_pairs={{0,4},{4,0},{8,12},{12,8},{16,20},{20,16},{24,28},{28,24},{1,5},{5... | collective-permute-start | bytes 393224 | tf_op jit(solution)/shard_map/ppermute | solution.py:273
  21.3 12.8 %all-to-all-start.1 = ((bf16[32,16,256]{2,1,0:T(8,128)(2,1)}), bf16[32,16,256]{2,1,0:T(8,128)(2,1)S(1)}, u32[]{:S(2)}, u32[]{:S(2)}) async-start(bf16[32,16,256]{2,1,0:T(8,128)(2,1)} %get-tuple-element.24), calls=%async_computation.1 | async-start | bytes 524288 | tf_op jit(solution)/shard_map/all_to_all | solution.py:264
  24.9 7.4 %collective-permute-start.5 = (bf16[2,16,1024]{2,1,0:T(8,128)(2,1)S(1)}, bf16[2,16,1024]{2,1,0:T(8,128)(2,1)S(1)}, u32[]{:S(2)}, u32[]{:S(2)}) collective-permute-start(bf16[2,16,1024]{2,1,0:T(8,128)(2,1)S(1)} %get-tuple-element.27), channel_id=1, source_target_pairs={{0,24},{4,28},{8,16},{12,20},{16,8},{20,12},{24,0},{28,4},{1,25},{... | collective-permute-start | bytes 196616 | tf_op jit(solution)/shard_map/ppermute | solution.py:273
  27.6 6.4 %collective-permute-start.6 = (bf16[2,16,1024]{2,1,0:T(8,128)(2,1)S(1)}, bf16[2,16,1024]{2,1,0:T(8,128)(2,1)S(1)}, u32[]{:S(2)}, u32[]{:S(2)}) collective-permute-start(bf16[2,16,1024]{2,1,0:T(8,128)(2,1)S(1)} %get-tuple-element.28), channel_id=1, source_target_pairs={{0,16},{4,20},{8,24},{12,28},{16,0},{20,4},{24,8},{28,12},{1,17},{... | collective-permute-start | bytes 196616 | tf_op jit(solution)/shard_map/ppermute | solution.py:273
  28.2 5.9 %collective-permute-start.7 = (bf16[2,16,1024]{2,1,0:T(8,128)(2,1)S(1)}, bf16[2,16,1024]{2,1,0:T(8,128)(2,1)S(1)}, u32[]{:S(2)}, u32[]{:S(2)}) collective-permute-start(bf16[2,16,1024]{2,1,0:T(8,128)(2,1)S(1)} %get-tuple-element.29), channel_id=1, source_target_pairs={{0,8},{4,12},{8,0},{12,4},{16,24},{20,28},{24,16},{28,20},{1,9},{5... | collective-permute-start | bytes 196616 | tf_op jit(solution)/shard_map/ppermute | solution.py:273

commit v7 on v6

--- a/solution.py
+++ b/solution.py
@@ -12,7 +12,10 @@
 ORDER_IN = (0, 3, 14, 11, 6, 18, 25, 9, 8, 2, 16, 1, 12, 27, 28, 20, 10, 15, 19, 21, 23, 7, 22, 17, 4, 24, 26, 13, 31, 29, 30, 5)
 ORDER_OUT = (0, 3, 14, 11, 6, 18, 25, 9, 8, 2, 10, 1, 12, 27, 28, 20, 16, 19, 15, 21, 23, 7, 22, 17, 4, 24, 26, 13, 31, 29, 30, 5)
 CHIPS = (0, 3, 2, 1)
-MASKS = tuple(2 * chip + core for chip in CHIPS for core in range(2))
+CHIPS_BACK = (0, 3, 1, 2)
+MASKS, MASKS_BACK = (
+    tuple(2 * chip + core for chip in chips for core in range(2)) for chips in (CHIPS, CHIPS_BACK)
+)
 VMEM = pl.BlockSpec(memory_space=pltpu.VMEM)
 SMEM = pl.BlockSpec(memory_space=pltpu.SMEM)
 HBM = pl.BlockSpec(memory_space=pltpu.HBM)
@@ -183,18 +186,22 @@
         delta = jnp.sum(probs * prob_grad, axis=0, keepdims=True)
         probs_all[:count, own] = probs.astype(jnp.bfloat16)
         score_all[:count, own] = (probs * (prob_grad - delta)).astype(jnp.bfloat16)
-    key_grad = (multiply(score_all[:count], query_flat[...]) * scale).astype(jnp.bfloat16)
-    value_grad = multiply(probs_all[:count], grad_flat[...]).astype(jnp.bfloat16)
-    for j in range(planes):
-        for d in range(peers):
-            if j * rows < count:
-                part = slice(j * rows + d * peer, j * rows + (d + 1) * peer)
-                grad_buf[spots_out[d][j], :, :width] = key_grad[part]
-                grad_buf[spots_out[d][j], :, width:] = value_grad[part]
-            else:
-                grad_buf[spots_out[d][j]] = jnp.zeros((peer, both), jnp.bfloat16)
-    leave = pltpu.make_async_copy(grad_buf, kv_grad, sem)
-    leave.start()
+    leave = []
+    for k, (left, right, factor) in enumerate(
+        ((probs_all, grad_flat, None), (score_all, query_flat, scale))
+    ):
+        half = slice((1 - k) * width, (2 - k) * width)
+        total = multiply(left[:count], right[...])
+        total = (total if factor is None else total * factor).astype(jnp.bfloat16)
+        for j in range(planes):
+            for d in range(peers):
+                at = j * rows + d * peer
+                part = total[at : at + peer] if at < count else jnp.zeros((peer, width), jnp.bfloat16)
+                grad_buf[spots_out[d][j], :, half] = part
+        leave.append(
+            pltpu.make_async_copy(grad_buf.at[:, :, half], kv_grad.at[:, :, half], sem.at[k])
+        )
+        leave[-1].start()
     attended = multiply(value_all[:count].T, probs_all[:count]).astype(jnp.bfloat16)
     query_grad = (multiply(key_all[:count].T, score_all[:count]) * scale).astype(jnp.bfloat16)
     for k, source in enumerate((attended, query_grad)):
@@ -202,8 +209,10 @@
             turned = source[:, h * rows : (h + 1) * rows].T
             at = (k * heads + h) * width
             for index, piece in enumerate(returned):
-                piece[:, at : at + width] = turned[index * size : (index + 1) * size]
-    leave.wait()
+                from_row = MASKS.index(MASKS_BACK[index]) * size if len(returned) > 1 else 0
+                piece[:, at : at + width] = turned[from_row : from_row + size]
+    for copy in leave:
+        copy.wait()
 
 
 def last_kernel(spots, kv, *refs):
@@ -213,7 +222,7 @@
     own = lax.axis_index("dp") if len(pieces) > 1 else None
     copies = []
     for index, piece in enumerate(pieces):
-        start = pl.multiple_of(lax.bitwise_xor(own, MASKS[index]) * size, size) if own is not None else 0
+        start = pl.multiple_of(lax.bitwise_xor(own, MASKS_BACK[index]) * size, size) if own is not None else 0
         for k, target in enumerate((attended, query_grad)):
             copies.append(
                 pltpu.make_async_copy(
@@ -272,7 +281,7 @@
     def swap(x, mask):
         return lax.ppermute(x, "dp", [(i, i ^ mask) for i in range(peers)])
 
-    def in_plane(pieces, cost=None):
+    def in_plane(pieces, order, cost):
         if not swapped:
             return [lax.all_to_all(pieces[0], "dp", split_axis=0, concat_axis=0, tiled=True)]
         kept, crossed = pieces
@@ -286,7 +295,7 @@
             cost_estimate=cost,
             name="pair",
         )(kept, crossed)
-        return [kept, crossed] + [swap(chip, 2 * mask) for chip, mask in zip(chips, CHIPS[1:])]
+        return [kept, crossed] + [swap(chip, 2 * mask) for chip, mask in zip(chips, order[1:])]
 
     slot_row = source_slot.reshape(1, rows)
     if swapped:
@@ -329,7 +338,7 @@
             name="mask",
         )(doc_lengths, slot_row)
     kv = everywhere(kv, order_in)
-    pieces = in_plane(pieces, pl.CostEstimate(flops=10**10, bytes_accessed=0, transcendentals=0))
+    pieces = in_plane(pieces, CHIPS, pl.CostEstimate(flops=10**10, bytes_accessed=0, transcendentals=0))
     if not fine:
         kv = by_plane(kv)
     count = rows * planes
@@ -346,7 +355,7 @@
             pltpu.VMEM((count, rows * heads), jnp.bfloat16),
             pltpu.VMEM((count, rows * heads), jnp.bfloat16),
             pltpu.VMEM(kv.shape, jnp.bfloat16),
-            pltpu.SemaphoreType.DMA,
+            pltpu.SemaphoreType.DMA((2,)),
         ],
         compiler_params=params(16 if planes <= 4 else 48),
         name="core",
@@ -356,7 +365,7 @@
     kv = everywhere(kv, order_out)
     if not fine:
         kv = by_plane(kv)
-    pieces = in_plane(pieces, pl.CostEstimate(flops=10**10, bytes_accessed=0, transcendentals=0))
+    pieces = in_plane(pieces, CHIPS_BACK, pl.CostEstimate(flops=10**10, bytes_accessed=0, transcendentals=0))
     count = 8 * 2 if swapped else 2
     return tuple(
         pl.pallas_call(

time: 35.3 us -> 35.2 us (level)
  transfers between devices with their start and end apart: 10 -> 10, of which waited for: 5 -> 6; matrix products, arithmetic and copies ran while one was open for 0% -> 0% of each run, Pallas kernels for 0% -> 0%
where the time goes in v7:
time: 35.2 us; the launch traced here: 34.9 us
  starting transfers between devices  18.2 us (52%)
  waiting for transfers between devices  12.3 us (35%)
  Pallas kernels  3.67 us (10%)
  between operations  0.71 us (2%)
    ppermute x8, waiting for transfers between devices, swap(): return lax.ppermute(x, 'dp', [(i, i ^ mask) for i in range(peers)])  11.2 us
    all_to_all x2, starting transfers between devices, everywhere(): lax.all_to_all(x, ('dp', 'ctx'), split_axis=0, concat_axis=0, tiled=True,...  10.5 us
    ppermute x8, starting transfers between devices, swap(): return lax.ppermute(x, 'dp', [(i, i ^ mask) for i in range(peers)])  7.7 us
    pallas_call x1, Pallas kernels, local(): pl.pallas_call(functools.partial(pack_kernel, spots_in), out_shape=sent +...  1.55 us
    pallas_call x1, Pallas kernels, local(): pl.pallas_call(functools.partial(core_kernel, heads, len(pieces), (spots_...  1.2 us
    all_to_all x2, waiting for transfers between devices, everywhere(): lax.all_to_all(x, ('dp', 'ctx'), split_axis=0, concat_axis=0, tiled=True,...  1.14 us
    pallas_call x1, Pallas kernels, local(): pl.pallas_call(functools.partial(last_kernel, spots_out), out_shape=[low(...  0.88 us
  transfers between devices with their start and end apart: 10, of which 6 were waited for; matrix products, arithmetic and copies ran while one was open for 0% of the time, Pallas kernels for 0%

profile of v7, /device:TPU:0, one launch (start us, length us, event | category | flops | bytes accessed | tf_op | source)
XLA Modules:
  0.0 34.9 jit_solution(17145431590572601658)
XLA Ops:
  0.6 1.6 %pack.1 = (bf16[4,16,1024]{2,1,0:T(8,128)(2,1)S(1)}, bf16[4,16,1024]{2,1,0:T(8,128)(2,1)S(1)}, f32[136,128]{1,0:T(8,128)S(1)}, bf16[32,16,256]{2,1,0:T(8,128)(2,1)}) custom-call(bf16[8,16,128]{2,1,0:T(8,128)(2,1)} %bitcast.3, bf16[8,16,128]{2,1,0:T(8,128)(2,1)} %bitcast.4, bf16[128,512]{1,0:T(8,128)(2,1)} %queries.1, bf16[128,512]{1,0:T(8,128)(2,1)} %out_grad.1, ...), custom_call_target="tpu_custom_call" | custom-call | tf_op jit(solution)/shard_map/pack/pallas_call | solution.py:303
  2.2 0.5 %collective-permute-start = (bf16[4,16,1024]{2,1,0:T(8,128)(2,1)S(1)}, bf16[4,16,1024]{2,1,0:T(8,128)(2,1)S(1)}, u32[]{:S(2)}, u32[]{:S(2)}) collective-permute-start(bf16[4,16,1024]{2,1,0:T(8,128)(2,1)S(1)} %get-tuple-element.20), channel_id=1, source_target_pairs={{0,4},{4,0},{8,12},{12,8},{16,20},{20,16},{24,28},{28,24},{1,5},{5... | collective-permute-start | bytes 393224 | tf_op jit(solution)/shard_map/ppermute | solution.py:282
  2.7 7.0 %all-to-all-start = ((bf16[32,16,256]{2,1,0:T(8,128)(2,1)}), bf16[32,16,256]{2,1,0:T(8,128)(2,1)S(1)}, u32[]{:S(2)}, u32[]{:S(2)}) async-start(bf16[32,16,256]{2,1,0:T(8,128)(2,1)} %get-tuple-element.18), calls=%async_computation | async-start | bytes 524288 | tf_op jit(solution)/shard_map/all_to_all | solution.py:273
  9.7 0.0 collective-permute-done.swapped.refs_1_
  9.7 2.7 %collective-permute-start.1 = (bf16[2,16,1024]{2,1,0:T(8,128)(2,1)S(1)}, bf16[2,16,1024]{2,1,0:T(8,128)(2,1)S(1)}, u32[]{:S(2)}, u32[]{:S(2)}) collective-permute-start(bf16[2,16,1024]{2,1,0:T(8,128)(2,1)S(1)} %get-tuple-element.21), channel_id=1, source_target_pairs={{0,24},{4,28},{8,16},{12,20},{16,8},{20,12},{24,0},{28,4},{1,25},{... | collective-permute-start | bytes 196616 | tf_op jit(solution)/shard_map/ppermute | solution.py:282
  12.4 0.6 %collective-permute-start.2 = (bf16[2,16,1024]{2,1,0:T(8,128)(2,1)S(1)}, bf16[2,16,1024]{2,1,0:T(8,128)(2,1)S(1)}, u32[]{:S(2)}, u32[]{:S(2)}) collective-permute-start(bf16[2,16,1024]{2,1,0:T(8,128)(2,1)S(1)} %get-tuple-element.22), channel_id=1, source_target_pairs={{0,16},{4,20},{8,24},{12,28},{16,0},{20,4},{24,8},{28,12},{1,17},{... | collective-permute-start | bytes 196616 | tf_op jit(solution)/shard_map/ppermute | solution.py:282
  13.0 0.3 collective-permute-start.3
  13.3 4.2 %collective-permute-done.1.refs_2_ = bf16[2,16,1024]{2,1,0:T(8,128)(2,1)S(1)} collective-permute-done((bf16[2,16,1024]{2,1,0:T(8,128)(2,1)S(1)}, bf16[2,16,1024]{2,1,0:T(8,128)(2,1)S(1)}, u32[]{:S(2)}, u32[]{:S(2)}) %collective-permute-start.1) | collective-permute-done | bytes 65568 | tf_op jit(solution)/shard_map/ppermute | solution.py:282
  17.5 1.4 %collective-permute-done.2.refs_3_ = bf16[2,16,1024]{2,1,0:T(8,128)(2,1)S(1)} collective-permute-done((bf16[2,16,1024]{2,1,0:T(8,128)(2,1)S(1)}, bf16[2,16,1024]{2,1,0:T(8,128)(2,1)S(1)}, u32[]{:S(2)}, u32[]{:S(2)}) %collective-permute-start.2) | collective-permute-done | bytes 65568 | tf_op jit(solution)/shard_map/ppermute | solution.py:282
  18.8 0.0 collective-permute-done.3.refs_4_
  18.8 1.1 %all-to-all-done.kv = bf16[32,16,256]{2,1,0:T(8,128)(2,1)S(1)} async-done(((bf16[32,16,256]{2,1,0:T(8,128)(2,1)}), bf16[32,16,256]{2,1,0:T(8,128)(2,1)S(1)}, u32[]{:S(2)}, u32[]{:S(2)}) %all-to-all-start) | async-done | bytes 262176 | tf_op jit(solution)/shard_map/all_to_all | solution.py:273
  20.0 1.2 %core.1 = (bf16[4,16,1024]{2,1,0:T(8,128)(2,1)S(1)}, bf16[4,16,1024]{2,1,0:T(8,128)(2,1)S(1)}, bf16[32,16,256]{2,1,0:T(8,128)(2,1)}) custom-call(f32[136,128]{1,0:T(8,128)S(1)} %get-tuple-element.17.bias, bf16[32,16,256]{2,1,0:T(8,128)(2,1)S(1)} %all-to-all-done.kv, bf16[4,16,1024]{2,1,0:T(8,128)(2,1)S(1)} %get-tuple-element.19.kept.refs_0_, ...), custom_call_target="tpu_custom_call" | custom-call | tf_op jit(solution)/shard_map/core/pallas_call | solution.py:345
  21.2 0.1 collective-permute-start.4
  21.3 3.6 %all-to-all-start.1 = ((bf16[32,16,256]{2,1,0:T(8,128)(2,1)}), bf16[32,16,256]{2,1,0:T(8,128)(2,1)S(1)}, u32[]{:S(2)}, u32[]{:S(2)}) async-start(bf16[32,16,256]{2,1,0:T(8,128)(2,1)} %get-tuple-element.24), calls=%async_computation.1 | async-start | bytes 524288 | tf_op jit(solution)/shard_map/all_to_all | solution.py:273
  24.8 0.0 collective-permute-done.4.swapped.refs_1_
  24.9 2.7 %collective-permute-start.5 = (bf16[2,16,1024]{2,1,0:T(8,128)(2,1)S(1)}, bf16[2,16,1024]{2,1,0:T(8,128)(2,1)S(1)}, u32[]{:S(2)}, u32[]{:S(2)}) collective-permute-start(bf16[2,16,1024]{2,1,0:T(8,128)(2,1)S(1)} %get-tuple-element.27), channel_id=1, source_target_pairs={{0,24},{4,28},{8,16},{12,20},{16,8},{20,12},{24,0},{28,4},{1,25},{... | collective-permute-start | bytes 196616 | tf_op jit(solution)/shard_map/ppermute | solution.py:282
  27.6 0.6 %collective-permute-start.6 = (bf16[2,16,1024]{2,1,0:T(8,128)(2,1)S(1)}, bf16[2,16,1024]{2,1,0:T(8,128)(2,1)S(1)}, u32[]{:S(2)}, u32[]{:S(2)}) collective-permute-start(bf16[2,16,1024]{2,1,0:T(8,128)(2,1)S(1)} %get-tuple-element.28), channel_id=1, source_target_pairs={{0,8},{4,12},{8,0},{12,4},{16,24},{20,28},{24,16},{28,20},{1,9},{5... | collective-permute-start | bytes 196616 | tf_op jit(solution)/shard_map/ppermute | solution.py:282
  28.2 0.3 collective-permute-start.7
  28.4 4.2 %collective-permute-done.5.refs_2_ = bf16[2,16,1024]{2,1,0:T(8,128)(2,1)S(1)} collective-permute-done((bf16[2,16,1024]{2,1,0:T(8,128)(2,1)S(1)}, bf16[2,16,1024]{2,1,0:T(8,128)(2,1)S(1)}, u32[]{:S(2)}, u32[]{:S(2)}) %collective-permute-start.5) | collective-permute-done | bytes 65568 | tf_op jit(solution)/shard_map/ppermute | solution.py:282
  32.6 0.8 %collective-permute-done.6.refs_3_ = bf16[2,16,1024]{2,1,0:T(8,128)(2,1)S(1)} collective-permute-done((bf16[2,16,1024]{2,1,0:T(8,128)(2,1)S(1)}, bf16[2,16,1024]{2,1,0:T(8,128)(2,1)S(1)}, u32[]{:S(2)}, u32[]{:S(2)}) %collective-permute-start.6) | collective-permute-done | bytes 65568 | tf_op jit(solution)/shard_map/ppermute | solution.py:282
  33.4 0.7 %collective-permute-done.7.refs_4_ = bf16[2,16,1024]{2,1,0:T(8,128)(2,1)S(1)} collective-permute-done((bf16[2,16,1024]{2,1,0:T(8,128)(2,1)S(1)}, bf16[2,16,1024]{2,1,0:T(8,128)(2,1)S(1)}, u32[]{:S(2)}, u32[]{:S(2)}) %collective-permute-start.7) | collective-permute-done | bytes 65568 | tf_op jit(solution)/shard_map/ppermute | solution.py:282
  34.0 0.0 all-to-all-done.1.kv
  34.0 0.9 %last.1 = (bf16[128,512]{1,0:T(8,128)(2,1)}, bf16[128,512]{1,0:T(8,128)(2,1)}, bf16[128,128]{1,0:T(8,128)(2,1)}, bf16[128,128]{1,0:T(8,128)(2,1)}) custom-call(bf16[32,16,256]{2,1,0:T(8,128)(2,1)S(1)} %all-to-all-done.1.kv, bf16[4,16,1024]{2,1,0:T(8,128)(2,1)S(1)} %get-tuple-element.25.kept.refs_0_, ...), custom_call_target="tpu_custom_call" | custom-call | tf_op jit(solution)/shard_map/last/pallas_call | solution.py:371
  (2 shorter events, 0.0 us)
Async XLA Ops:
  2.2 7.5 %collective-permute-start = (bf16[4,16,1024]{2,1,0:T(8,128)(2,1)S(1)}, bf16[4,16,1024]{2,1,0:T(8,128)(2,1)S(1)}, u32[]{:S(2)}, u32[]{:S(2)}) collective-permute-start(bf16[4,16,1024]{2,1,0:T(8,128)(2,1)S(1)} %get-tuple-element.20), channel_id=1, source_target_pairs={{0,4},{4,0},{8,12},{12,8},{16,20},{20,16},{24,28},{28,24},{1,5},{5... | collective-permute-start | bytes 393224 | tf_op jit(solution)/shard_map/ppermute | solution.py:282
  2.7 17.3 %all-to-all-start = ((bf16[32,16,256]{2,1,0:T(8,128)(2,1)}), bf16[32,16,256]{2,1,0:T(8,128)(2,1)S(1)}, u32[]{:S(2)}, u32[]{:S(2)}) async-start(bf16[32,16,256]{2,1,0:T(8,128)(2,1)} %get-tuple-element.18), calls=%async_computation | async-start | bytes 524288 | tf_op jit(solution)/shard_map/all_to_all | solution.py:273
  9.7 7.7 %collective-permute-start.1 = (bf16[2,16,1024]{2,1,0:T(8,128)(2,1)S(1)}, bf16[2,16,1024]{2,1,0:T(8,128)(2,1)S(1)}, u32[]{:S(2)}, u32[]{:S(2)}) collective-permute-start(bf16[2,16,1024]{2,1,0:T(8,128)(2,1)S(1)} %get-tuple-element.21), channel_id=1, source_target_pairs={{0,24},{4,28},{8,16},{12,20},{16,8},{20,12},{24,0},{28,4},{1,25},{... | collective-permute-start | bytes 196616 | tf_op jit(solution)/shard_map/ppermute | solution.py:282
  12.4 6.4 %collective-permute-start.2 = (bf16[2,16,1024]{2,1,0:T(8,128)(2,1)S(1)}, bf16[2,16,1024]{2,1,0:T(8,128)(2,1)S(1)}, u32[]{:S(2)}, u32[]{:S(2)}) collective-permute-start(bf16[2,16,1024]{2,1,0:T(8,128)(2,1)S(1)} %get-tuple-element.22), channel_id=1, source_target_pairs={{0,16},{4,20},{8,24},{12,28},{16,0},{20,4},{24,8},{28,12},{1,17},{... | collective-permute-start | bytes 196616 | tf_op jit(solution)/shard_map/ppermute | solution.py:282
  13.0 5.8 %collective-permute-start.3 = (bf16[2,16,1024]{2,1,0:T(8,128)(2,1)S(1)}, bf16[2,16,1024]{2,1,0:T(8,128)(2,1)S(1)}, u32[]{:S(2)}, u32[]{:S(2)}) collective-permute-start(bf16[2,16,1024]{2,1,0:T(8,128)(2,1)S(1)} %get-tuple-element.23), channel_id=1, source_target_pairs={{0,8},{4,12},{8,0},{12,4},{16,24},{20,28},{24,16},{28,20},{1,9},{5... | collective-permute-start | bytes 196616 | tf_op jit(solution)/shard_map/ppermute | solution.py:282
  21.2 3.7 %collective-permute-start.4 = (bf16[4,16,1024]{2,1,0:T(8,128)(2,1)S(1)}, bf16[4,16,1024]{2,1,0:T(8,128)(2,1)S(1)}, u32[]{:S(2)}, u32[]{:S(2)}) collective-permute-start(bf16[4,16,1024]{2,1,0:T(8,128)(2,1)S(1)} %get-tuple-element.26), channel_id=1, source_target_pairs={{0,4},{4,0},{8,12},{12,8},{16,20},{20,16},{24,28},{28,24},{1,5},{5... | collective-permute-start | bytes 393224 | tf_op jit(solution)/shard_map/ppermute | solution.py:282
  21.3 12.8 %all-to-all-start.1 = ((bf16[32,16,256]{2,1,0:T(8,128)(2,1)}), bf16[32,16,256]{2,1,0:T(8,128)(2,1)S(1)}, u32[]{:S(2)}, u32[]{:S(2)}) async-start(bf16[32,16,256]{2,1,0:T(8,128)(2,1)} %get-tuple-element.24), calls=%async_computation.1 | async-start | bytes 524288 | tf_op jit(solution)/shard_map/all_to_all | solution.py:273
  24.9 7.7 %collective-permute-start.5 = (bf16[2,16,1024]{2,1,0:T(8,128)(2,1)S(1)}, bf16[2,16,1024]{2,1,0:T(8,128)(2,1)S(1)}, u32[]{:S(2)}, u32[]{:S(2)}) collective-permute-start(bf16[2,16,1024]{2,1,0:T(8,128)(2,1)S(1)} %get-tuple-element.27), channel_id=1, source_target_pairs={{0,24},{4,28},{8,16},{12,20},{16,8},{20,12},{24,0},{28,4},{1,25},{... | collective-permute-start | bytes 196616 | tf_op jit(solution)/shard_map/ppermute | solution.py:282
  27.6 5.8 %collective-permute-start.6 = (bf16[2,16,1024]{2,1,0:T(8,128)(2,1)S(1)}, bf16[2,16,1024]{2,1,0:T(8,128)(2,1)S(1)}, u32[]{:S(2)}, u32[]{:S(2)}) collective-permute-start(bf16[2,16,1024]{2,1,0:T(8,128)(2,1)S(1)} %get-tuple-element.28), channel_id=1, source_target_pairs={{0,8},{4,12},{8,0},{12,4},{16,24},{20,28},{24,16},{28,20},{1,9},{5... | collective-permute-start | bytes 196616 | tf_op jit(solution)/shard_map/ppermute | solution.py:282
  28.2 5.9 %collective-permute-start.7 = (bf16[2,16,1024]{2,1,0:T(8,128)(2,1)S(1)}, bf16[2,16,1024]{2,1,0:T(8,128)(2,1)S(1)}, u32[]{:S(2)}, u32[]{:S(2)}) collective-permute-start(bf16[2,16,1024]{2,1,0:T(8,128)(2,1)S(1)} %get-tuple-element.29), channel_id=1, source_target_pairs={{0,16},{4,20},{8,24},{12,28},{16,0},{20,4},{24,8},{28,12},{1,17},{... | collective-permute-start | bytes 196616 | tf_op jit(solution)/shard_map/ppermute | solution.py:282

commit v8 on v7

--- a/solution.py
+++ b/solution.py
@@ -10,7 +10,7 @@
 
 HIDDEN = -1e30
 ORDER_IN = (0, 3, 14, 11, 6, 18, 25, 9, 8, 2, 16, 1, 12, 27, 28, 20, 10, 15, 19, 21, 23, 7, 22, 17, 4, 24, 26, 13, 31, 29, 30, 5)
-ORDER_OUT = (0, 3, 14, 11, 6, 18, 25, 9, 8, 2, 10, 1, 12, 27, 28, 20, 16, 19, 15, 21, 23, 7, 22, 17, 4, 24, 26, 13, 31, 29, 30, 5)
+ORDER_OUT = (0, 3, 14, 11, 6, 18, 25, 9, 8, 2, 10, 28, 12, 27, 1, 20, 16, 19, 15, 21, 23, 7, 22, 17, 4, 24, 26, 13, 31, 29, 30, 5)
 CHIPS = (0, 3, 2, 1)
 CHIPS_BACK = (0, 3, 1, 2)
 MASKS, MASKS_BACK = (

time: 35.2 us -> 35.2 us (level)
  no operation moved by 1% of the time
where the time goes in v8:
time: 35.2 us; the launch traced here: 34.9 us
  starting transfers between devices  18.2 us (52%)
  waiting for transfers between devices  12.3 us (35%)
  Pallas kernels  3.67 us (10%)
  between operations  0.71 us (2%)
    ppermute x8, waiting for transfers between devices, swap(): return lax.ppermute(x, 'dp', [(i, i ^ mask) for i in range(peers)])  11.2 us
    all_to_all x2, starting transfers between devices, everywhere(): lax.all_to_all(x, ('dp', 'ctx'), split_axis=0, concat_axis=0, tiled=True,...  10.5 us
    ppermute x8, starting transfers between devices, swap(): return lax.ppermute(x, 'dp', [(i, i ^ mask) for i in range(peers)])  7.7 us
    pallas_call x1, Pallas kernels, local(): pl.pallas_call(functools.partial(pack_kernel, spots_in), out_shape=sent +...  1.55 us
    pallas_call x1, Pallas kernels, local(): pl.pallas_call(functools.partial(core_kernel, heads, len(pieces), (spots_...  1.2 us
    all_to_all x2, waiting for transfers between devices, everywhere(): lax.all_to_all(x, ('dp', 'ctx'), split_axis=0, concat_axis=0, tiled=True,...  1.14 us
    pallas_call x1, Pallas kernels, local(): pl.pallas_call(functools.partial(last_kernel, spots_out), out_shape=[low(...  0.88 us
  transfers between devices with their start and end apart: 10, of which 6 were waited for; matrix products, arithmetic and copies ran while one was open for 0% of the time, Pallas kernels for 0%

profile of v8, /device:TPU:0, one launch (start us, length us, event | category | flops | bytes accessed | tf_op | source)
XLA Modules:
  0.0 34.9 jit_solution(10135177487603827778)
XLA Ops:
  0.6 1.6 %pack.1 = (bf16[4,16,1024]{2,1,0:T(8,128)(2,1)S(1)}, bf16[4,16,1024]{2,1,0:T(8,128)(2,1)S(1)}, f32[136,128]{1,0:T(8,128)S(1)}, bf16[32,16,256]{2,1,0:T(8,128)(2,1)}) custom-call(bf16[8,16,128]{2,1,0:T(8,128)(2,1)} %bitcast.3, bf16[8,16,128]{2,1,0:T(8,128)(2,1)} %bitcast.4, bf16[128,512]{1,0:T(8,128)(2,1)} %queries.1, bf16[128,512]{1,0:T(8,128)(2,1)} %out_grad.1, ...), custom_call_target="tpu_custom_call" | custom-call | tf_op jit(solution)/shard_map/pack/pallas_call | solution.py:303
  2.2 0.5 %collective-permute-start = (bf16[4,16,1024]{2,1,0:T(8,128)(2,1)S(1)}, bf16[4,16,1024]{2,1,0:T(8,128)(2,1)S(1)}, u32[]{:S(2)}, u32[]{:S(2)}) collective-permute-start(bf16[4,16,1024]{2,1,0:T(8,128)(2,1)S(1)} %get-tuple-element.20), channel_id=1, source_target_pairs={{0,4},{4,0},{8,12},{12,8},{16,20},{20,16},{24,28},{28,24},{1,5},{5... | collective-permute-start | bytes 393224 | tf_op jit(solution)/shard_map/ppermute | solution.py:282
  2.7 7.0 %all-to-all-start = ((bf16[32,16,256]{2,1,0:T(8,128)(2,1)}), bf16[32,16,256]{2,1,0:T(8,128)(2,1)S(1)}, u32[]{:S(2)}, u32[]{:S(2)}) async-start(bf16[32,16,256]{2,1,0:T(8,128)(2,1)} %get-tuple-element.18), calls=%async_computation | async-start | bytes 524288 | tf_op jit(solution)/shard_map/all_to_all | solution.py:273
  9.7 0.0 collective-permute-done.swapped.refs_1_
  9.7 2.7 %collective-permute-start.1 = (bf16[2,16,1024]{2,1,0:T(8,128)(2,1)S(1)}, bf16[2,16,1024]{2,1,0:T(8,128)(2,1)S(1)}, u32[]{:S(2)}, u32[]{:S(2)}) collective-permute-start(bf16[2,16,1024]{2,1,0:T(8,128)(2,1)S(1)} %get-tuple-element.21), channel_id=1, source_target_pairs={{0,24},{4,28},{8,16},{12,20},{16,8},{20,12},{24,0},{28,4},{1,25},{... | collective-permute-start | bytes 196616 | tf_op jit(solution)/shard_map/ppermute | solution.py:282
  12.4 0.6 %collective-permute-start.2 = (bf16[2,16,1024]{2,1,0:T(8,128)(2,1)S(1)}, bf16[2,16,1024]{2,1,0:T(8,128)(2,1)S(1)}, u32[]{:S(2)}, u32[]{:S(2)}) collective-permute-start(bf16[2,16,1024]{2,1,0:T(8,128)(2,1)S(1)} %get-tuple-element.22), channel_id=1, source_target_pairs={{0,16},{4,20},{8,24},{12,28},{16,0},{20,4},{24,8},{28,12},{1,17},{... | collective-permute-start | bytes 196616 | tf_op jit(solution)/shard_map/ppermute | solution.py:282
  13.0 0.3 collective-permute-start.3
  13.3 4.2 %collective-permute-done.1.refs_2_ = bf16[2,16,1024]{2,1,0:T(8,128)(2,1)S(1)} collective-permute-done((bf16[2,16,1024]{2,1,0:T(8,128)(2,1)S(1)}, bf16[2,16,1024]{2,1,0:T(8,128)(2,1)S(1)}, u32[]{:S(2)}, u32[]{:S(2)}) %collective-permute-start.1) | collective-permute-done | bytes 65568 | tf_op jit(solution)/shard_map/ppermute | solution.py:282
  17.5 1.4 %collective-permute-done.2.refs_3_ = bf16[2,16,1024]{2,1,0:T(8,128)(2,1)S(1)} collective-permute-done((bf16[2,16,1024]{2,1,0:T(8,128)(2,1)S(1)}, bf16[2,16,1024]{2,1,0:T(8,128)(2,1)S(1)}, u32[]{:S(2)}, u32[]{:S(2)}) %collective-permute-start.2) | collective-permute-done | bytes 65568 | tf_op jit(solution)/shard_map/ppermute | solution.py:282
  18.8 0.0 collective-permute-done.3.refs_4_
  18.8 1.1 %all-to-all-done.kv = bf16[32,16,256]{2,1,0:T(8,128)(2,1)S(1)} async-done(((bf16[32,16,256]{2,1,0:T(8,128)(2,1)}), bf16[32,16,256]{2,1,0:T(8,128)(2,1)S(1)}, u32[]{:S(2)}, u32[]{:S(2)}) %all-to-all-start) | async-done | bytes 262176 | tf_op jit(solution)/shard_map/all_to_all | solution.py:273
  20.0 1.2 %core.1 = (bf16[4,16,1024]{2,1,0:T(8,128)(2,1)S(1)}, bf16[4,16,1024]{2,1,0:T(8,128)(2,1)S(1)}, bf16[32,16,256]{2,1,0:T(8,128)(2,1)}) custom-call(f32[136,128]{1,0:T(8,128)S(1)} %get-tuple-element.17.bias, bf16[32,16,256]{2,1,0:T(8,128)(2,1)S(1)} %all-to-all-done.kv, bf16[4,16,1024]{2,1,0:T(8,128)(2,1)S(1)} %get-tuple-element.19.kept.refs_0_, ...), custom_call_target="tpu_custom_call" | custom-call | tf_op jit(solution)/shard_map/core/pallas_call | solution.py:345
  21.2 0.1 collective-permute-start.4
  21.3 3.6 %all-to-all-start.1 = ((bf16[32,16,256]{2,1,0:T(8,128)(2,1)}), bf16[32,16,256]{2,1,0:T(8,128)(2,1)S(1)}, u32[]{:S(2)}, u32[]{:S(2)}) async-start(bf16[32,16,256]{2,1,0:T(8,128)(2,1)} %get-tuple-element.24), calls=%async_computation.1 | async-start | bytes 524288 | tf_op jit(solution)/shard_map/all_to_all | solution.py:273
  24.8 0.0 collective-permute-done.4.swapped.refs_1_
  24.9 2.7 %collective-permute-start.5 = (bf16[2,16,1024]{2,1,0:T(8,128)(2,1)S(1)}, bf16[2,16,1024]{2,1,0:T(8,128)(2,1)S(1)}, u32[]{:S(2)}, u32[]{:S(2)}) collective-permute-start(bf16[2,16,1024]{2,1,0:T(8,128)(2,1)S(1)} %get-tuple-element.27), channel_id=1, source_target_pairs={{0,24},{4,28},{8,16},{12,20},{16,8},{20,12},{24,0},{28,4},{1,25},{... | collective-permute-start | bytes 196616 | tf_op jit(solution)/shard_map/ppermute | solution.py:282
  27.6 0.6 %collective-permute-start.6 = (bf16[2,16,1024]{2,1,0:T(8,128)(2,1)S(1)}, bf16[2,16,1024]{2,1,0:T(8,128)(2,1)S(1)}, u32[]{:S(2)}, u32[]{:S(2)}) collective-permute-start(bf16[2,16,1024]{2,1,0:T(8,128)(2,1)S(1)} %get-tuple-element.28), channel_id=1, source_target_pairs={{0,8},{4,12},{8,0},{12,4},{16,24},{20,28},{24,16},{28,20},{1,9},{5... | collective-permute-start | bytes 196616 | tf_op jit(solution)/shard_map/ppermute | solution.py:282
  28.2 0.3 collective-permute-start.7
  28.4 4.2 %collective-permute-done.5.refs_2_ = bf16[2,16,1024]{2,1,0:T(8,128)(2,1)S(1)} collective-permute-done((bf16[2,16,1024]{2,1,0:T(8,128)(2,1)S(1)}, bf16[2,16,1024]{2,1,0:T(8,128)(2,1)S(1)}, u32[]{:S(2)}, u32[]{:S(2)}) %collective-permute-start.5) | collective-permute-done | bytes 65568 | tf_op jit(solution)/shard_map/ppermute | solution.py:282
  32.6 0.8 %collective-permute-done.6.refs_3_ = bf16[2,16,1024]{2,1,0:T(8,128)(2,1)S(1)} collective-permute-done((bf16[2,16,1024]{2,1,0:T(8,128)(2,1)S(1)}, bf16[2,16,1024]{2,1,0:T(8,128)(2,1)S(1)}, u32[]{:S(2)}, u32[]{:S(2)}) %collective-permute-start.6) | collective-permute-done | bytes 65568 | tf_op jit(solution)/shard_map/ppermute | solution.py:282
  33.3 0.7 %collective-permute-done.7.refs_4_ = bf16[2,16,1024]{2,1,0:T(8,128)(2,1)S(1)} collective-permute-done((bf16[2,16,1024]{2,1,0:T(8,128)(2,1)S(1)}, bf16[2,16,1024]{2,1,0:T(8,128)(2,1)S(1)}, u32[]{:S(2)}, u32[]{:S(2)}) %collective-permute-start.7) | collective-permute-done | bytes 65568 | tf_op jit(solution)/shard_map/ppermute | solution.py:282
  34.0 0.0 all-to-all-done.1.kv
  34.0 0.9 %last.1 = (bf16[128,512]{1,0:T(8,128)(2,1)}, bf16[128,512]{1,0:T(8,128)(2,1)}, bf16[128,128]{1,0:T(8,128)(2,1)}, bf16[128,128]{1,0:T(8,128)(2,1)}) custom-call(bf16[32,16,256]{2,1,0:T(8,128)(2,1)S(1)} %all-to-all-done.1.kv, bf16[4,16,1024]{2,1,0:T(8,128)(2,1)S(1)} %get-tuple-element.25.kept.refs_0_, ...), custom_call_target="tpu_custom_call" | custom-call | tf_op jit(solution)/shard_map/last/pallas_call | solution.py:371
  (2 shorter events, 0.0 us)
Async XLA Ops:
  2.2 7.5 %collective-permute-start = (bf16[4,16,1024]{2,1,0:T(8,128)(2,1)S(1)}, bf16[4,16,1024]{2,1,0:T(8,128)(2,1)S(1)}, u32[]{:S(2)}, u32[]{:S(2)}) collective-permute-start(bf16[4,16,1024]{2,1,0:T(8,128)(2,1)S(1)} %get-tuple-element.20), channel_id=1, source_target_pairs={{0,4},{4,0},{8,12},{12,8},{16,20},{20,16},{24,28},{28,24},{1,5},{5... | collective-permute-start | bytes 393224 | tf_op jit(solution)/shard_map/ppermute | solution.py:282
  2.7 17.3 %all-to-all-start = ((bf16[32,16,256]{2,1,0:T(8,128)(2,1)}), bf16[32,16,256]{2,1,0:T(8,128)(2,1)S(1)}, u32[]{:S(2)}, u32[]{:S(2)}) async-start(bf16[32,16,256]{2,1,0:T(8,128)(2,1)} %get-tuple-element.18), calls=%async_computation | async-start | bytes 524288 | tf_op jit(solution)/shard_map/all_to_all | solution.py:273
  9.7 7.7 %collective-permute-start.1 = (bf16[2,16,1024]{2,1,0:T(8,128)(2,1)S(1)}, bf16[2,16,1024]{2,1,0:T(8,128)(2,1)S(1)}, u32[]{:S(2)}, u32[]{:S(2)}) collective-permute-start(bf16[2,16,1024]{2,1,0:T(8,128)(2,1)S(1)} %get-tuple-element.21), channel_id=1, source_target_pairs={{0,24},{4,28},{8,16},{12,20},{16,8},{20,12},{24,0},{28,4},{1,25},{... | collective-permute-start | bytes 196616 | tf_op jit(solution)/shard_map/ppermute | solution.py:282
  12.4 6.4 %collective-permute-start.2 = (bf16[2,16,1024]{2,1,0:T(8,128)(2,1)S(1)}, bf16[2,16,1024]{2,1,0:T(8,128)(2,1)S(1)}, u32[]{:S(2)}, u32[]{:S(2)}) collective-permute-start(bf16[2,16,1024]{2,1,0:T(8,128)(2,1)S(1)} %get-tuple-element.22), channel_id=1, source_target_pairs={{0,16},{4,20},{8,24},{12,28},{16,0},{20,4},{24,8},{28,12},{1,17},{... | collective-permute-start | bytes 196616 | tf_op jit(solution)/shard_map/ppermute | solution.py:282
  13.0 5.8 %collective-permute-start.3 = (bf16[2,16,1024]{2,1,0:T(8,128)(2,1)S(1)}, bf16[2,16,1024]{2,1,0:T(8,128)(2,1)S(1)}, u32[]{:S(2)}, u32[]{:S(2)}) collective-permute-start(bf16[2,16,1024]{2,1,0:T(8,128)(2,1)S(1)} %get-tuple-element.23), channel_id=1, source_target_pairs={{0,8},{4,12},{8,0},{12,4},{16,24},{20,28},{24,16},{28,20},{1,9},{5... | collective-permute-start | bytes 196616 | tf_op jit(solution)/shard_map/ppermute | solution.py:282
  21.2 3.7 %collective-permute-start.4 = (bf16[4,16,1024]{2,1,0:T(8,128)(2,1)S(1)}, bf16[4,16,1024]{2,1,0:T(8,128)(2,1)S(1)}, u32[]{:S(2)}, u32[]{:S(2)}) collective-permute-start(bf16[4,16,1024]{2,1,0:T(8,128)(2,1)S(1)} %get-tuple-element.26), channel_id=1, source_target_pairs={{0,4},{4,0},{8,12},{12,8},{16,20},{20,16},{24,28},{28,24},{1,5},{5... | collective-permute-start | bytes 393224 | tf_op jit(solution)/shard_map/ppermute | solution.py:282
  21.3 12.8 %all-to-all-start.1 = ((bf16[32,16,256]{2,1,0:T(8,128)(2,1)}), bf16[32,16,256]{2,1,0:T(8,128)(2,1)S(1)}, u32[]{:S(2)}, u32[]{:S(2)}) async-start(bf16[32,16,256]{2,1,0:T(8,128)(2,1)} %get-tuple-element.24), calls=%async_computation.1 | async-start | bytes 524288 | tf_op jit(solution)/shard_map/all_to_all | solution.py:273
  24.9 7.7 %collective-permute-start.5 = (bf16[2,16,1024]{2,1,0:T(8,128)(2,1)S(1)}, bf16[2,16,1024]{2,1,0:T(8,128)(2,1)S(1)}, u32[]{:S(2)}, u32[]{:S(2)}) collective-permute-start(bf16[2,16,1024]{2,1,0:T(8,128)(2,1)S(1)} %get-tuple-element.27), channel_id=1, source_target_pairs={{0,24},{4,28},{8,16},{12,20},{16,8},{20,12},{24,0},{28,4},{1,25},{... | collective-permute-start | bytes 196616 | tf_op jit(solution)/shard_map/ppermute | solution.py:282
  27.6 5.7 %collective-permute-start.6 = (bf16[2,16,1024]{2,1,0:T(8,128)(2,1)S(1)}, bf16[2,16,1024]{2,1,0:T(8,128)(2,1)S(1)}, u32[]{:S(2)}, u32[]{:S(2)}) collective-permute-start(bf16[2,16,1024]{2,1,0:T(8,128)(2,1)S(1)} %get-tuple-element.28), channel_id=1, source_target_pairs={{0,8},{4,12},{8,0},{12,4},{16,24},{20,28},{24,16},{28,20},{1,9},{5... | collective-permute-start | bytes 196616 | tf_op jit(solution)/shard_map/ppermute | solution.py:282
  28.2 5.9 %collective-permute-start.7 = (bf16[2,16,1024]{2,1,0:T(8,128)(2,1)S(1)}, bf16[2,16,1024]{2,1,0:T(8,128)(2,1)S(1)}, u32[]{:S(2)}, u32[]{:S(2)}) collective-permute-start(bf16[2,16,1024]{2,1,0:T(8,128)(2,1)S(1)} %get-tuple-element.29), channel_id=1, source_target_pairs={{0,16},{4,20},{8,24},{12,28},{16,0},{20,4},{24,8},{28,12},{1,17},{... | collective-permute-start | bytes 196616 | tf_op jit(solution)/shard_map/ppermute | solution.py:282
